TPU v7x, 128 devices: a whole 4x4x4 slice. The times are simulated.
128 devices in a mesh: expert: 8 (over x, core), ctx: 8 (over z_hi, y), dp: 2 (over z_lo).
Axes of the slice: x: 4, y: 4, z: 4 (z_hi: 2, z_lo: 2; z = z_hi * 2 + z_lo), core: 2. Of those that a mesh axis runs over, the one named last changes fastest.
Arguments:
- tokens: bfloat16 [16384, 1024], P(('expert', 'ctx', 'dp')), may hold values from -6 to 6
- norm_in: bfloat16 [1024], P('expert'), may hold values from 0.25 to 1.75
- w_query: bfloat16 [1024, 1024], P('expert'), may hold values from -0.1875 to 0.1875
- w_key: bfloat16 [1024, 512], P('expert'), may hold values from -0.1875 to 0.1875
- w_value: bfloat16 [1024, 512], P('expert'), may hold values from -0.1875 to 0.1875
- query_gain: bfloat16 [1024], P('expert'), may hold values from 0.25 to 1.75
- key_gain: bfloat16 [512], P('expert'), may hold values from 0.25 to 1.75
- w_out: bfloat16 [1024, 1024], P('expert'), may hold values from -4 to 4
- norm_mid: bfloat16 [1024], P('expert'), may hold values from 0.25 to 1.75
- w_router: bfloat16 [1024, 32], P('expert'), may hold values from -0.09375 to 0.09375
- expert_gate: bfloat16 [1024, 32, 512], P(('ctx', 'dp'), 'expert'), may hold values from -0.1875 to 0.1875
- expert_up: bfloat16 [1024, 32, 512], P(('ctx', 'dp'), 'expert'), may hold values from -0.1875 to 0.1875
- expert_down: bfloat16 [1024, 32, 512], P(('ctx', 'dp'), 'expert'), may hold values from -4 to 4
- routes: int32 [16384, 8], P(('expert', 'ctx', 'dp')), may hold values from 0 to 31, all different within a row; in each aligned block of 128 rows (0 to 127, 128 to 255, ...) at most 64 rows name the same one
- valid: int32 [16384], P(('expert', 'ctx', 'dp')), may hold values 0 or 1
- teacher: float32 [16384, 1024], P(('expert', 'ctx', 'dp')), may hold values from -18 to 18
Outputs:
- mixed: bfloat16 [16384, 1024], P(('expert', 'ctx', 'dp'))
- loss: float32 [], replicated
- grad_tokens: float32 [16384, 1024], P(('expert', 'ctx', 'dp'))
- grad_norm_in: float32 [1024], P('expert')
- grad_query: float32 [1024, 1024], P('expert')
- grad_key: float32 [1024, 512], P('expert')
- grad_value: float32 [1024, 512], P('expert')
- grad_query_gain: float32 [1024], P('expert')
- grad_key_gain: float32 [512], P('expert')
- grad_out: float32 [1024, 1024], P('expert')
- grad_norm_mid: float32 [1024], P('expert')
- grad_router: float32 [1024, 32], P('expert')
- grad_gate: float32 [1024, 32, 512], P(('ctx', 'dp'), 'expert')
- grad_up: float32 [1024, 32, 512], P(('ctx', 'dp'), 'expert')
- grad_down: float32 [1024, 32, 512], P(('ctx', 'dp'), 'expert')
Inputs may be any that keep to these rules, and one draw needn't show every extreme that they name: `routes`: in each aligned block of 128 rows (the rows of one device) no expert is named by more than 64 rows, a bound that some block reaches; each row names 8 different experts.
All inputs are finite; a program needn't handle non-finite values. No bound on the sum of `valid` on one device may be relied on, other than what follows from the above.
Results may differ from a plain program's by a relative error of at most 0.023.
Values may be sent and summed in bfloat16 or wider, within the bound.
A program may use at most 128 MiB of HBM per device.

v0:
```python
import jax
import jax.numpy as jnp
from jax import lax
from jax.sharding import PartitionSpec as P

HEADS = 16
HEAD = 64
KV_HEADS = 8
TOP = 8
BLOCK = 256
QW = 1024


EPS = 1e-06
THETA = 10000.0
NEG = -1e30
HIGH = lax.Precision.HIGHEST


def rms_norm(values):
    return values * lax.rsqrt(jnp.mean(values * values, axis=-1, keepdims=True) + EPS)


def rope_tables(positions):
    half_head = HEAD // 2
    frequency = THETA ** (-(jnp.arange(half_head).astype(jnp.float32) * (2.0 / HEAD)))
    angles = positions.astype(jnp.float32)[:, None] * frequency[None, :]
    return (jnp.cos(angles), jnp.sin(angles))


def rotate(values, cosine, sine, head_count):
    count_rows = values.shape[0]
    shaped = values.reshape(count_rows, head_count, HEAD)
    half_head = HEAD // 2
    first_half = shaped[..., :half_head]
    second_half = shaped[..., half_head:]
    cos_rows = cosine[:, None, :]
    sin_rows = sine[:, None, :]
    turned = jnp.concatenate(
        [
            first_half * cos_rows - second_half * sin_rows,
            second_half * cos_rows + first_half * sin_rows,
        ],
        axis=-1,
    )
    return turned.reshape(count_rows, head_count * HEAD)


def transpose_dot(left, right):
    return lax.dot_general(
        left, right, (((0,), (0,)), ((), ())), preferred_element_type=jnp.float32
    )


def dot_back(left, right):
    return lax.dot_general(
        left, right, (((1,), (1,)), ((), ())), preferred_element_type=jnp.float32
    )


def per_device(
    tokens,
    norm_in,
    w_query,
    w_key,
    w_value,
    query_gain,
    key_gain,
    w_out,
    norm_mid,
    w_router,
    expert_gate,
    expert_up,
    expert_down,
    routes,
    valid,
    teacher,
):
    norm_in, w_query, w_key, w_value, query_gain, key_gain, w_out, norm_mid, w_router = (
        lax.all_gather(norm_in, "expert", axis=0, tiled=True),
        lax.all_gather(w_query, "expert", axis=0, tiled=True),
        lax.all_gather(w_key, "expert", axis=0, tiled=True),
        lax.all_gather(w_value, "expert", axis=0, tiled=True),
        lax.all_gather(query_gain, "expert", axis=0, tiled=True),
        lax.all_gather(key_gain, "expert", axis=0, tiled=True),
        lax.all_gather(w_out, "expert", axis=0, tiled=True),
        lax.all_gather(norm_mid, "expert", axis=0, tiled=True),
        lax.all_gather(w_router, "expert", axis=0, tiled=True),
    )
    rows_here = tokens.shape[0]
    width = tokens.shape[1]
    seq_len = rows_here * lax.axis_size(("ctx", "dp"))
    kv_width = w_key.shape[1]
    group_size = HEADS // KV_HEADS
    score_scale = HEAD ** (-0.5)
    positions = lax.axis_index(("ctx", "dp")) * rows_here + jnp.arange(rows_here, dtype=jnp.int32)
    cosine, sine = rope_tables(positions)
    token_vals = tokens.astype(jnp.float32)

    def norm_first(values, gain):
        return rms_norm(values) * gain

    normed, norm_first_back = jax.vjp(norm_first, token_vals, norm_in.astype(jnp.float32))
    normed_low = normed.astype(jnp.bfloat16)
    query_pre = jnp.dot(normed_low, w_query, preferred_element_type=jnp.float32)
    key_pre = jnp.dot(normed_low, w_key, preferred_element_type=jnp.float32)
    value_low = jnp.dot(normed_low, w_value, preferred_element_type=jnp.float32).astype(
        jnp.bfloat16
    )

    def shape_heads(query_in, key_in, qgain, kgain):
        return (
            rotate(rms_norm(query_in) * qgain, cosine, sine, HEADS),
            rotate(rms_norm(key_in) * kgain, cosine, sine, KV_HEADS),
        )

    (query_rot, key_rot), shape_back = jax.vjp(
        shape_heads,
        query_pre,
        key_pre,
        query_gain.astype(jnp.float32),
        key_gain.astype(jnp.float32),
    )
    query_low = query_rot.astype(jnp.bfloat16)
    key_low = key_rot.astype(jnp.bfloat16)
    keys_all, values_all, keep_all = (
        lax.all_gather(key_low, ("ctx", "dp"), axis=0, tiled=True),
        lax.all_gather(value_low, ("ctx", "dp"), axis=0, tiled=True),
        lax.all_gather(valid, ("ctx", "dp"), axis=0, tiled=True),
    )
    block_keys = min(512, seq_len)
    block_total = seq_len // block_keys
    block_ids = jnp.arange(block_total, dtype=jnp.int32)
    query_grouped = query_low.reshape(rows_here, KV_HEADS, group_size, HEAD)
    query_block = positions // BLOCK

    def block_scores(block_index):
        begin = block_index * block_keys
        keys_part = lax.dynamic_slice_in_dim(keys_all, begin, block_keys, 0).reshape(
            block_keys, KV_HEADS, HEAD
        )
        values_part = lax.dynamic_slice_in_dim(values_all, begin, block_keys, 0).reshape(
            block_keys, KV_HEADS, HEAD
        )
        keep_part = lax.dynamic_slice_in_dim(keep_all, begin, block_keys, 0)
        key_pos = begin + jnp.arange(block_keys, dtype=jnp.int32)
        allowed = (key_pos[None, :] // BLOCK <= query_block[:, None]) & (
            (keep_part[None, :] > 0) | (key_pos[None, :] == positions[:, None])
        )
        scores = (
            jnp.einsum(
                "tkgd,skd->kgts", query_grouped, keys_part, preferred_element_type=jnp.float32
            )
            * score_scale
        )
        return (scores, allowed[None, None], keys_part, values_part)

    def pass_max(carry, block_index):
        running_max, running_sum = carry
        scores, allowed, keys_part, values_part = block_scores(block_index)
        masked = jnp.where(allowed, scores, NEG)
        new_max = jnp.maximum(running_max, jnp.max(masked, axis=-1))
        terms = jnp.where(allowed, jnp.exp(masked - new_max[..., None]), 0.0)
        running_sum = running_sum * jnp.exp(running_max - new_max) + jnp.sum(terms, axis=-1)
        return ((new_max, running_sum), None)

    stat_shape = (KV_HEADS, group_size, rows_here)
    (running_max, running_sum), _ = lax.scan(
        pass_max,
        (jnp.full(stat_shape, NEG, jnp.float32), jnp.zeros(stat_shape, jnp.float32)),
        block_ids,
    )
    log_total = running_max + jnp.log(running_sum)

    def pass_out(accum, block_index):
        scores, allowed, keys_part, values_part = block_scores(block_index)
        weights = jnp.where(allowed, jnp.exp(scores - log_total[..., None]), 0.0).astype(
            jnp.bfloat16
        )
        accum = accum + jnp.einsum(
            "kgts,skd->tkgd", weights, values_part, preferred_element_type=jnp.float32
        )
        return (accum, None)

    attended, _ = lax.scan(
        pass_out, jnp.zeros((rows_here, KV_HEADS, group_size, HEAD), jnp.float32), block_ids
    )
    attended = attended.reshape(rows_here, QW)
    attended_low = attended.astype(jnp.bfloat16)
    residual = token_vals + jnp.dot(attended_low, w_out, preferred_element_type=jnp.float32)

    def norm_second(values, gain):
        return rms_norm(values) * gain

    mid_vals, norm_second_back = jax.vjp(norm_second, residual, norm_mid.astype(jnp.float32))
    mid_low = mid_vals.astype(jnp.bfloat16)
    experts_total = w_router.shape[1]
    probs = jax.nn.softmax(jnp.dot(mid_low, w_router, preferred_element_type=jnp.float32), axis=-1)
    expert_ids = jnp.arange(experts_total, dtype=jnp.int32)
    chosen = (routes[:, :, None] == expert_ids[None, None, :]).astype(jnp.float32)
    gates = jnp.sum(chosen * probs[:, None, :], axis=-1)
    capacity = 2 * rows_here * TOP // experts_total
    flat_routes = routes.reshape(-1)
    picks = (flat_routes[:, None] == expert_ids[None, :]).astype(jnp.int32)
    slot_index = jnp.sum((jnp.cumsum(picks, axis=0) - 1) * picks, axis=1)
    dest_slot = flat_routes * capacity + slot_index
    entry_ids = jnp.arange(rows_here * TOP, dtype=jnp.int32)
    table = jnp.full((experts_total * capacity,), -1, jnp.int32).at[dest_slot].set(entry_ids)
    used = table >= 0
    safe = jnp.where(used, table, 0)
    expert_devs = lax.axis_size("expert")
    local_experts = experts_total // expert_devs
    zero_low = jnp.zeros((), jnp.bfloat16)
    send_rows = jnp.where(used[:, None], mid_low[safe // TOP], zero_low).reshape(
        expert_devs, local_experts, capacity, width
    )
    gate_all, up_all, down_all = (
        lax.all_gather(expert_gate, ("ctx", "dp"), axis=0, tiled=True),
        lax.all_gather(expert_up, ("ctx", "dp"), axis=0, tiled=True),
        lax.all_gather(expert_down, ("ctx", "dp"), axis=0, tiled=True),
    )
    inputs = lax.all_to_all(send_rows, "expert", split_axis=0, concat_axis=2, tiled=True).reshape(
        local_experts, expert_devs * capacity, width
    )
    gate_pre = jnp.einsum("erd,def->erf", inputs, gate_all, preferred_element_type=jnp.float32)
    up_pre = jnp.einsum("erd,def->erf", inputs, up_all, preferred_element_type=jnp.float32)
    sigma = jax.nn.sigmoid(gate_pre)
    silu_val = gate_pre * sigma
    silu_slope = sigma * (1.0 + gate_pre * (1.0 - sigma))
    act_low = (silu_val * up_pre).astype(jnp.bfloat16)
    out_rows = jnp.einsum(
        "erf,def->erd", act_low, down_all, preferred_element_type=jnp.float32
    ).astype(jnp.bfloat16)
    back_rows = lax.all_to_all(
        out_rows.reshape(1, local_experts, expert_devs * capacity, width),
        "expert",
        split_axis=2,
        concat_axis=0,
        tiled=True,
    ).reshape(experts_total * capacity, width)
    returned = back_rows[dest_slot].astype(jnp.float32).reshape(rows_here, TOP, width)
    out_vals = residual + jnp.sum(gates[:, :, None] * returned, axis=1)
    err = (out_vals - teacher) * valid.astype(jnp.float32)[:, None]
    square_sum, count = lax.psum(
        (jnp.sum(err * err), jnp.sum(valid.astype(jnp.float32))), ("expert", "ctx", "dp")
    )
    loss = square_sum / (count * width)
    d_gates = jnp.sum(returned * err[:, None, :], axis=-1)
    d_returned = (
        (gates[:, :, None] * err[:, None, :]).astype(jnp.bfloat16).reshape(rows_here * TOP, width)
    )
    grad_send = jnp.where(used[:, None], d_returned[safe], zero_low).reshape(
        expert_devs, local_experts, capacity, width
    )
    d_outputs = lax.all_to_all(
        grad_send, "expert", split_axis=0, concat_axis=2, tiled=True
    ).reshape(local_experts, expert_devs * capacity, width)
    d_act = jnp.einsum("erd,def->erf", d_outputs, down_all, preferred_element_type=jnp.float32)
    d_gate_low = (d_act * up_pre * silu_slope).astype(jnp.bfloat16)
    d_up_low = (d_act * silu_val).astype(jnp.bfloat16)
    d_inputs = (
        jnp.einsum("erf,def->erd", d_gate_low, gate_all, preferred_element_type=jnp.float32)
        + jnp.einsum("erf,def->erd", d_up_low, up_all, preferred_element_type=jnp.float32)
    ).astype(jnp.bfloat16)
    d_back = lax.all_to_all(
        d_inputs.reshape(1, local_experts, expert_devs * capacity, width),
        "expert",
        split_axis=2,
        concat_axis=0,
        tiled=True,
    ).reshape(experts_total * capacity, width)
    d_mid = jnp.sum(d_back[dest_slot].astype(jnp.float32).reshape(rows_here, TOP, width), axis=1)
    hidden_width = expert_gate.shape[2]
    gate_term = jnp.einsum("erd,erf->def", inputs, d_gate_low, preferred_element_type=jnp.float32)
    up_term = jnp.einsum("erd,erf->def", inputs, d_up_low, preferred_element_type=jnp.float32)
    down_term = jnp.einsum("erd,erf->def", d_outputs, act_low, preferred_element_type=jnp.float32)
    expert_stack = lax.psum_scatter(
        jnp.concatenate([gate_term, up_term, down_term], axis=2).astype(jnp.bfloat16),
        ("ctx", "dp"),
        scatter_dimension=0,
        tiled=True,
    ).astype(jnp.float32)
    grad_gate = expert_stack[:, :, :hidden_width]
    grad_up = expert_stack[:, :, hidden_width : 2 * hidden_width]
    grad_down = expert_stack[:, :, 2 * hidden_width :]
    d_probs = jnp.sum(chosen * d_gates[:, :, None], axis=1)
    d_logits = probs * (d_probs - jnp.sum(probs * d_probs, axis=-1, keepdims=True))
    router_vals = w_router.astype(jnp.float32)
    d_mid = d_mid + jnp.dot(d_logits, router_vals.T, precision=HIGH)
    grad_router = jnp.dot(mid_low.astype(jnp.float32).T, d_logits, precision=HIGH)
    d_residual, grad_norm_mid = norm_second_back(d_mid)
    d_residual = d_residual + err
    d_branch = d_residual.astype(jnp.bfloat16)
    grad_out = transpose_dot(attended_low, d_branch)
    d_attended = dot_back(d_branch, w_out).astype(jnp.bfloat16)
    delta = jnp.sum(
        (d_attended.astype(jnp.float32) * attended).reshape(rows_here, KV_HEADS, group_size, HEAD),
        axis=-1,
    )
    delta = jnp.transpose(delta, (1, 2, 0))
    d_att_grouped = d_attended.reshape(rows_here, KV_HEADS, group_size, HEAD)

    def pass_back(d_query, block_index):
        scores, allowed, keys_part, values_part = block_scores(block_index)
        weights = jnp.where(allowed, jnp.exp(scores - log_total[..., None]), 0.0)
        d_values = jnp.einsum(
            "kgts,tkgd->skd",
            weights.astype(jnp.bfloat16),
            d_att_grouped,
            preferred_element_type=jnp.float32,
        )
        d_weights = jnp.einsum(
            "tkgd,skd->kgts", d_att_grouped, values_part, preferred_element_type=jnp.float32
        )
        d_scores = (weights * (d_weights - delta[..., None])).astype(jnp.bfloat16)
        d_query = d_query + score_scale * jnp.einsum(
            "kgts,skd->tkgd", d_scores, keys_part, preferred_element_type=jnp.float32
        )
        d_keys = score_scale * jnp.einsum(
            "kgts,tkgd->skd", d_scores, query_grouped, preferred_element_type=jnp.float32
        )
        return (
            d_query,
            (d_keys.reshape(block_keys, kv_width), d_values.reshape(block_keys, kv_width)),
        )

    d_query, (d_keys_all, d_values_all) = lax.scan(
        pass_back, jnp.zeros((rows_here, KV_HEADS, group_size, HEAD), jnp.float32), block_ids
    )
    d_keys_mine, d_values_mine = (
        lax.psum_scatter(
            d_keys_all.reshape(seq_len, kv_width).astype(jnp.bfloat16),
            ("ctx", "dp"),
            scatter_dimension=0,
            tiled=True,
        ).astype(jnp.float32),
        lax.psum_scatter(
            d_values_all.reshape(seq_len, kv_width).astype(jnp.bfloat16),
            ("ctx", "dp"),
            scatter_dimension=0,
            tiled=True,
        ).astype(jnp.float32),
    )
    d_query_pre, d_key_pre, grad_query_gain, grad_key_gain = shape_back(
        (d_query.reshape(rows_here, QW), d_keys_mine)
    )
    d_query_low = d_query_pre.astype(jnp.bfloat16)
    d_key_low = d_key_pre.astype(jnp.bfloat16)
    d_value_low = d_values_mine.astype(jnp.bfloat16)
    d_normed = (
        dot_back(d_query_low, w_query) + dot_back(d_key_low, w_key) + dot_back(d_value_low, w_value)
    )
    grad_query = transpose_dot(normed_low, d_query_low)
    grad_key = transpose_dot(normed_low, d_key_low)
    grad_value = transpose_dot(normed_low, d_value_low)
    d_token_norm, grad_norm_in = norm_first_back(d_normed)
    grad_tokens = d_residual + d_token_norm
    grads = (
        grad_norm_in,
        grad_query,
        grad_key,
        grad_value,
        grad_query_gain,
        grad_key_gain,
        grad_out,
        grad_norm_mid,
        grad_router,
    )
    summed = (
        lax.psum(grads[0].astype(jnp.bfloat16), ("ctx", "dp")).astype(jnp.float32),
        lax.psum(grads[1].astype(jnp.bfloat16), ("ctx", "dp")).astype(jnp.float32),
        lax.psum(grads[2].astype(jnp.bfloat16), ("ctx", "dp")).astype(jnp.float32),
        lax.psum(grads[3].astype(jnp.bfloat16), ("ctx", "dp")).astype(jnp.float32),
        lax.psum(grads[4].astype(jnp.bfloat16), ("ctx", "dp")).astype(jnp.float32),
        lax.psum(grads[5].astype(jnp.bfloat16), ("ctx", "dp")).astype(jnp.float32),
        lax.psum(grads[6].astype(jnp.bfloat16), ("ctx", "dp")).astype(jnp.float32),
        lax.psum(grads[7].astype(jnp.bfloat16), ("ctx", "dp")).astype(jnp.float32),
        lax.psum(grads[8].astype(jnp.bfloat16), ("ctx", "dp")).astype(jnp.float32),
    )
    shares = (
        lax.psum_scatter(
            summed[0].astype(jnp.bfloat16), "expert", scatter_dimension=0, tiled=True
        ).astype(jnp.float32),
        lax.psum_scatter(
            summed[1].astype(jnp.bfloat16), "expert", scatter_dimension=0, tiled=True
        ).astype(jnp.float32),
        lax.psum_scatter(
            summed[2].astype(jnp.bfloat16), "expert", scatter_dimension=0, tiled=True
        ).astype(jnp.float32),
        lax.psum_scatter(
            summed[3].astype(jnp.bfloat16), "expert", scatter_dimension=0, tiled=True
        ).astype(jnp.float32),
        lax.psum_scatter(
            summed[4].astype(jnp.bfloat16), "expert", scatter_dimension=0, tiled=True
        ).astype(jnp.float32),
        lax.psum_scatter(
            summed[5].astype(jnp.bfloat16), "expert", scatter_dimension=0, tiled=True
        ).astype(jnp.float32),
        lax.psum_scatter(
            summed[6].astype(jnp.bfloat16), "expert", scatter_dimension=0, tiled=True
        ).astype(jnp.float32),
        lax.psum_scatter(
            summed[7].astype(jnp.bfloat16), "expert", scatter_dimension=0, tiled=True
        ).astype(jnp.float32),
        lax.psum_scatter(
            summed[8].astype(jnp.bfloat16), "expert", scatter_dimension=0, tiled=True
        ).astype(jnp.float32),
    )
    return (
        out_vals.astype(jnp.bfloat16),
        loss,
        grad_tokens,
        shares[0],
        shares[1],
        shares[2],
        shares[3],
        shares[4],
        shares[5],
        shares[6],
        shares[7],
        shares[8],
        grad_gate,
        grad_up,
        grad_down,
    )


def solution(mesh):
    placed = (
        P(("expert", "ctx", "dp"), None),
        P("expert"),
        P("expert", None),
        P("expert", None),
        P("expert", None),
        P("expert"),
        P("expert"),
        P("expert", None),
        P("expert"),
        P("expert", None),
        P(("ctx", "dp"), "expert", None),
        P(("ctx", "dp"), "expert", None),
        P(("ctx", "dp"), "expert", None),
        P(("expert", "ctx", "dp"), None),
        P(("expert", "ctx", "dp")),
        P(("expert", "ctx", "dp"), None),
    )
    return jax.shard_map(
        per_device,
        mesh=mesh,
        in_specs=placed,
        out_specs=(
            P(("expert", "ctx", "dp"), None),
            P(),
            P(("expert", "ctx", "dp"), None),
            P("expert"),
            P("expert", None),
            P("expert", None),
            P("expert", None),
            P("expert"),
            P("expert"),
            P("expert", None),
            P("expert"),
            P("expert", None),
            P(("ctx", "dp"), "expert", None),
            P(("ctx", "dp"), "expert", None),
            P(("ctx", "dp"), "expert", None),
        ),
        check_vma=False,
    )
```

profile of v0, /device:TPU:1, one launch (start us, length us, event | category | flops | bytes accessed | tf_op | source)
XLA Modules:
  0.0 1426.2 jit_solution(318637913844661692)
XLA Ops:
  9.5 12.0 all-gather
  24.4 11.9 all-reduce.4
  41.1 20.6 %all-gather.14.cloned.1.call-done = bf16[1024,512]{1,0:T(8,128)(2,1)} async-done(((bf16[128,512]{1,0:T(8,128)(2,1)}), bf16[1024,512]{1,0:T(8,128)(2,1)}) %all-gather.14.cloned.1.call-update) | async-done | bytes 1048592 | tf_op jit(solution)/shard_map/all_gather | solution.py:83
  67.6 9.0 reduce-window.6
  81.5 32.5 %all-gather.1 = s32[16,1,128]{2,1,0:T(1,128)S(1)} all-gather(s32[1,1,128]{2,1,0:T(1,128)S(1)} %bitcast.349), channel_id=1, replica_groups=mesh['expert'=8,'ctx'=8,'dp'=2] {'ctx','dp'}, dimensions={0}, use_global_device_ids=true | all-gather | bytes 8704 | tf_op jit(solution)/shard_map/all_gather | solution.py:129
  114.0 15.6 %all-gather.2 = bf16[8,1,128]{2,1,0:T(2,128)(2,1)S(1)} all-gather(bf16[1,1,128]{2,1,0:T(2,128)(2,1)S(1)} %bitcast.347), channel_id=1, replica_groups=mesh['expert'=8,'ctx'=8,'dp'=2] {'expert'}, dimensions={0}, use_global_device_ids=true | all-gather | bytes 2304 | tf_op jit(solution)/shard_map/all_gather | solution.py:84
  141.9 16.3 %all-gather.20.cloned.1.call-done = bf16[2048,512]{0,1:T(8,128)(2,1)} async-done(((bf16[128,512]{0,1:T(8,128)(2,1)}), bf16[2048,512]{0,1:T(8,128)(2,1)}) %all-gather.20.cloned.1.call-update) | async-done | bytes 2097168 | tf_op jit(solution)/shard_map/all_gather | solution.py:127
  158.2 35.1 %while.51 = (s32[]{:T(128)}, f32[8,2,128]{2,1,0:T(2,128)S(1)}, f32[8,2,128]{2,1,0:T(2,128)S(1)}, s32[4]{0:T(128)S(1)}, s32[2048]{0:T(1024)S(1)}, /*index=5*/bf16...) while((s32[]{:T(128)}, f32[8,2,128]{2,1,0:T(2,128)S(1)}, ...), condition=%wide.region_6.7_spmd.clone.clone.clone, body=%wide.region_3.6_spmd.clone.clone.clone.sunk | while | flops 142889472 | bytes 10540242 | solution.py:168
  193.3 45.2 %all-gather.16.cloned.1.call-done = bf16[2048,512]{1,0:T(8,128)(2,1)} async-done(((bf16[128,512]{1,0:T(8,128)(2,1)}), bf16[2048,512]{1,0:T(8,128)(2,1)}) %all-gather.16.cloned.1.call-update) | async-done | bytes 2097168 | tf_op jit(solution)/shard_map/all_gather | solution.py:128
  241.4 27.4 %while.52 = (s32[]{:T(128)}, f32[128,8,2,64]{0,3,2,1:T(8,128)}, s32[4]{0:T(128)S(1)}, bf16[2048,512]{0,1:T(8,128)(2,1)S(1)}, s32[2048]{0:T(1024)S(1)}, /*index=5...) while((s32[]{:T(128)}, f32[128,8,2,64]{0,3,2,1:T(8,128)}, ...), condition=%wide.region_8.9_spmd.clone.clone.clone, body=%wide.region_7.8_spmd.clone.clone.clone.sunk | while | flops 273164800 | bytes 4609241 | solution.py:185
  277.6 9.6 gather_fusion
  289.7 58.2 %all_to_all.60 = bf16[8,4,64,1024]{3,2,1,0:T(8,128)(2,1)S(1)} all-to-all(bf16[8,4,64,1024]{3,2,1,0:T(8,128)(2,1)S(1)} %broadcast_select_fusion.2), channel_id=1, replica_groups=mesh['expert'=8,'ctx'=8,'dp'=2] {'expert'}, dimensions={0} | all-to-all | bytes 8388608 | tf_op jit(solution)/shard_map/all_to_all | solution.py:222
  350.3 21.5 %all-gather.26.cloned.1.call-done = bf16[1024,4,512]{2,0,1:T(8,128)(2,1)} async-done(((bf16[64,4,512]{2,0,1:T(8,128)(2,1)}), bf16[1024,4,512]{2,0,1:T(8,128)(2,1)}) %all-gather.26.cloned.1.call-update) | async-done | bytes 4194320 | tf_op jit(solution)/shard_map/all_gather | solution.py:218
  379.6 91.5 %all-gather.28.cloned.1.call-done = bf16[1024,4,512]{2,0,1:T(8,128)(2,1)} async-done(((bf16[64,4,512]{2,0,1:T(8,128)(2,1)}), bf16[1024,4,512]{2,0,1:T(8,128)(2,1)}) %all-gather.28.cloned.1.call-update) | async-done | bytes 4194320 | tf_op jit(solution)/shard_map/all_gather | solution.py:219
  471.1 9.2 multiply_convert_fusion.2
  480.3 90.2 %all-gather.30.cloned.1.call-done = bf16[1024,4,512]{2,0,1:T(8,128)(2,1)} async-done(((bf16[64,4,512]{2,0,1:T(8,128)(2,1)}), bf16[1024,4,512]{2,0,1:T(8,128)(2,1)}) %all-gather.30.cloned.1.call-update) | async-done | bytes 4194320 | tf_op jit(solution)/shard_map/all_gather | solution.py:220
  588.3 54.6 %all_gather.56 = bf16[1024,32]{0,1:T(8,128)(2,1)S(1)} all-gather(bf16[128,32]{0,1:T(8,128)(2,1)S(1)} %copy-done.47), channel_id=1, replica_groups=mesh['expert'=8,'ctx'=8,'dp'=2] {'expert'}, dimensions={0}, use_global_device_ids=true | all-gather | bytes 73728 | tf_op jit(solution)/shard_map/all_gather | solution.py:88
  661.7 9.7 gather_fusion.2
  673.8 52.7 %all_to_all.61 = bf16[8,4,64,1024]{3,2,1,0:T(8,128)(2,1)S(1)} all-to-all(bf16[8,4,64,1024]{3,2,1,0:T(8,128)(2,1)S(1)} %broadcast_select_fusion.1), channel_id=1, replica_groups=mesh['expert'=8,'ctx'=8,'dp'=2] {'expert'}, dimensions={0} | all-to-all | bytes 8388608 | tf_op jit(solution)/shard_map/all_to_all | solution.py:255
  760.5 45.0 %all-to-all-done.3 = bf16[1,4,512,1024]{3,1,0,2:T(4,128)(2,1)} async-done(((bf16[1,4,512,1024]{3,1,0,2:T(4,128)(2,1)}), bf16[1,4,512,1024]{3,1,0,2:T(4,128)(2,1)}, u32[]{:S(2)}, u32[]{:S(2)}) %all-to-all-start.3) | async-done | bytes 4194336 | tf_op jit(solution)/shard_map/all_to_all | solution.py:265
  822.5 66.5 %while.53 = (s32[]{:T(128)}, f32[128,8,2,64]{0,3,2,1:T(8,128)}, bf16[4,512,512]{2,1,0:T(8,128)(2,1)}, bf16[4,512,512]{2,1,0:T(8,128)(2,1)}, s32[4]{0:T(128)S(1)}...) while((s32[]{:T(128)}, f32[128,8,2,64]{0,3,2,1:T(8,128)}, ...), condition=%wide.region_29.30_spmd.clone.clone.clone, body=%wide.region_28.29_spmd.clone.clone.clone.sunk | while | flops 682764800 | bytes 46896412 | solution.py:327
  895.3 63.0 %reduce-scatter.10.cloned.1.call-done = bf16[128,512]{1,0:T(8,128)(2,1)} async-done(((bf16[2048,512]{1,0:T(8,128)(2,1)}), bf16[128,512]{1,0:T(8,128)(2,1)}) %reduce-scatter.10.cloned.1.call-update) | async-done | bytes 131088 | tf_op jit(solution)/shard_map/reduce_scatter | solution.py:331
  962.0 77.0 %reduce-scatter.12.cloned.1.call-done = bf16[128,512]{1,0:T(8,128)(2,1)} async-done(((bf16[2048,512]{1,0:T(8,128)(2,1)}), bf16[128,512]{1,0:T(8,128)(2,1)}) %reduce-scatter.12.cloned.1.call-update) | async-done | bytes 131088 | tf_op jit(solution)/shard_map/reduce_scatter | solution.py:337
  1052.9 17.2 %pad_maximum_fusion = bf16[1024,4,1536]{0,2,1:T(8,128)(2,1)} fusion(bf16[1024,4,512]{0,2,1:T(8,128)(2,1)S(1)} %convert_bitcast_fusion, bf16[1024,4,512]{0,2,1:T(8,128)(2,1)S(1)} %convert_bitcast_fusion.1, bf16[1024,4,512]{0,2,1:T(8,128)(2,1)S(1)} %convert_bitcast_fusion.2), kind=kLoop, calls=%fused_computation.101 | loop fusion | flops 37748736 | bytes 25165824 | tf_op jit(solution)/shard_map/concatenate | solution.py:278
  1070.2 21.8 %copy.212 = bf16[1024,4,1536]{2,1,0:T(4,128)(2,1)} copy(bf16[1024,4,1536]{0,2,1:T(8,128)(2,1)} %pad_maximum_fusion) | data formatting | bytes 25165824 | tf_op jit(solution)/shard_map/concatenate | solution.py:278
  1092.0 22.2 %reduce-scatter.20.cloned.1.call-done = bf16[128,1024]{1,0:T(8,128)(2,1)} async-done(((bf16[1024,1024]{1,0:T(8,128)(2,1)}), bf16[128,1024]{1,0:T(8,128)(2,1)}) %reduce-scatter.20.cloned.1.call-update) | async-done | bytes 262160 | tf_op jit(solution)/shard_map/reduce_scatter | solution.py:399
  1114.2 33.0 %reduce-scatter.16.cloned.1.call-done = bf16[128,512]{1,0:T(8,128)(2,1)} async-done(((bf16[1024,512]{1,0:T(8,128)(2,1)}), bf16[128,512]{1,0:T(8,128)(2,1)}) %reduce-scatter.16.cloned.1.call-update) | async-done | bytes 131088 | tf_op jit(solution)/shard_map/reduce_scatter | solution.py:387
  1147.2 33.0 %reduce-scatter.18.cloned.1.call-done = bf16[128,512]{1,0:T(8,128)(2,1)} async-done(((bf16[1024,512]{1,0:T(8,128)(2,1)}), bf16[128,512]{1,0:T(8,128)(2,1)}) %reduce-scatter.18.cloned.1.call-update) | async-done | bytes 131088 | tf_op jit(solution)/shard_map/reduce_scatter | solution.py:390
  1183.5 69.5 %all-reduce.10 = (f32[]{:T(128)}, f32[]{:T(128)}) all-reduce(f32[]{:T(128)} %get-tuple-element.941, f32[]{:T(128)} %convert_reduce_fusion.1), channel_id=1, replica_groups=mesh['expert'=8,'ctx'=8,'dp'=2] {'expert','ctx','dp'}, use_global_device_ids=true, to_apply=%region_19.20 | all-reduce | flops 2 | bytes 16 | tf_op jit(solution)/shard_map/psum | solution.py:244
  1258.4 13.4 all-reduce.13
  1272.1 59.1 %all-reduce.11 = (bf16[128]{0:T(256)(128)(2,1)S(1)}, bf16[128]{0:T(256)(128)(2,1)S(1)}, bf16[64]{0:T(256)(128)(2,1)S(1)}, bf16[128]{0:T(256)(128)(2,1)S(1)}, bf16[128,32]{0,1:T(8,128)(2,1)S(1)}) all-reduce(bf16[128]{0:T(256)(128)(2,1)S(1)} %dynamic-slice.2, ...), channel_id=1, replica_groups=mesh['expert'=8,'ctx'=8,'dp'=2] {'ctx','dp'}, use_global_device_ids=true, to_apply=%region_36.37 | all-reduce | flops 4544 | bytes 18176 | tf_op jit(solution)/shard_map/psum | solution.py:370
  1334.9 73.9 %all-reduce.16.cloned.1.call-done = (bf16[128,1024]{1,0:T(8,128)(2,1)}, bf16[128,512]{1,0:T(8,128)(2,1)}, bf16[128,512]{1,0:T(8,128)(2,1)}, bf16[128,1024]{1,0:T(8,128)(2,1)}, bf16[1024,4,1536]{2,1,0:T(4,128)(2,1)}) async-done(((bf16[128,1024]{1,0:T(8,128)(2,1)}, bf16[128,512]{1,0:T(8,128)(2,1)}, bf16[128,512]{1,0:T(8,128)(2,1)}, bf16[128,1024]{1,0:T(8,128)(2,1)}, bf16[1024,4,1536]{2,1,0:T(4,128)(2,1)}), ...) | async-done | bytes 13369360 | tf_op jit(solution)/shard_map/psum | solution.py:371
  (465 shorter events, 308.4 us)
Async XLA Ops:
  7.2 30.4 %all-gather.18.cloned.1.call-start = ((), (), s32[]{:S(2)}) async-start(), calls=%async_computation.13 | async-start | bytes 1179648 | tf_op jit(solution)/shard_map/all_gather | solution.py:82
  8.0 53.8 %all-gather.14.cloned.1.call-start = ((), (), s32[]{:S(2)}) async-start(), calls=%async_computation.11 | async-start | bytes 1179648 | tf_op jit(solution)/shard_map/all_gather | solution.py:83
  8.7 129.7 %all-gather.22.cloned.1.call-start = ((), (), s32[]{:S(2)}) async-start(), calls=%async_computation.15 | async-start | bytes 2359296 | tf_op jit(solution)/shard_map/all_gather | solution.py:81
  9.5 148.7 %all-gather.20.cloned.1.call-start = ((), (), s32[]{:S(2)}) async-start(), calls=%async_computation.14 | async-start | bytes 2228224 | tf_op jit(solution)/shard_map/all_gather | solution.py:127
  21.5 117.0 %copy-start.31 = (f32[8,1,128]{2,1,0:T(1,128)}, f32[8,1,128]{2,1,0:T(1,128)S(1)}, u32[]{:S(2)}) copy-start(f32[8,1,128]{2,1,0:T(1,128)S(1)} %convert_element_type.282) | copy-start | bytes 12292
  37.4 101.0 %copy-start.45 = (f32[128]{0:T(128)}, f32[128]{0:T(128)S(1)}, u32[]{:S(2)}) copy-start(f32[128]{0:T(128)S(1)} %fusion.78) | copy-start | bytes 1540
  37.6 104.2 %copy-start.27 = (f32[128,32]{0,1:T(8,128)}, f32[128,32]{0,1:T(8,128)S(1)}, u32[]{:S(2)}) copy-start(f32[128,32]{0,1:T(8,128)S(1)} %get-tuple-element.977) | copy-start | bytes 49156
  37.6 104.2 %copy-start.29 = (f32[128,32]{0,1:T(8,128)}, f32[128,32]{0,1:T(8,128)S(1)}, u32[]{:S(2)}) copy-start(f32[128,32]{0,1:T(8,128)S(1)} %get-tuple-element.978) | copy-start | bytes 49156
  39.5 90.2 %copy-start.60 = (bf16[128]{0:T(256)(128)(2,1)S(1)}, bf16[128]{0:T(256)(128)(2,1)}, u32[]{:S(2)}) copy-start(bf16[128]{0:T(256)(128)(2,1)} %param.30) | copy-start | bytes 772
  41.1 197.4 %all-gather.16.cloned.1.call-start = ((), (), s32[]{:S(2)}) async-start(), calls=%async_computation.12 | async-start | bytes 2228224 | tf_op jit(solution)/shard_map/all_gather | solution.py:128
  64.0 211.1 %all-gather.24.cloned.1.call-start = ((), (), s32[]{:S(2)}) async-start(), calls=%async_computation.16 | async-start | bytes 2359296 | tf_op jit(solution)/shard_map/all_gather | solution.py:86
  64.6 307.2 %all-gather.26.cloned.1.call-start = ((), (), s32[]{:S(2)}) async-start(), calls=%async_computation.17 | async-start | bytes 4456448 | tf_op jit(solution)/shard_map/all_gather | solution.py:218
  65.4 405.7 %all-gather.28.cloned.1.call-start = ((), (), s32[]{:S(2)}) async-start(), calls=%async_computation.18 | async-start | bytes 4456448 | tf_op jit(solution)/shard_map/all_gather | solution.py:219
  66.2 504.3 %all-gather.30.cloned.1.call-start = ((), (), s32[]{:S(2)}) async-start(), calls=%async_computation.19 | async-start | bytes 4456448 | tf_op jit(solution)/shard_map/all_gather | solution.py:220
  480.3 94.8 %copy-start.68 = (bf16[4,512,512]{2,1,0:T(8,128)(2,1)}, bf16[4,512,512]{2,1,0:T(8,128)(2,1)S(1)}, u32[]{:S(2)}) copy-start(bf16[4,512,512]{2,1,0:T(8,128)(2,1)S(1)} %get-tuple-element.987) | copy-start | bytes 6291460
  580.3 63.1 %all-to-all-start.1 = ((bf16[1,4,512,1024]{3,1,0,2:T(4,128)(2,1)}), bf16[1,4,512,1024]{3,1,0,2:T(4,128)(2,1)}, u32[]{:S(2)}, u32[]{:S(2)}) async-start(bf16[1,4,512,1024]{3,1,0,2:T(4,128)(2,1)} %copy.191), calls=%async_computation.1 | async-start | bytes 8388608 | tf_op jit(solution)/shard_map/all_to_all | solution.py:234
  643.1 177.2 %copy-start.33 = (f32[128,32]{0,1:T(8,128)}, f32[128,32]{0,1:T(8,128)S(1)}, u32[]{:S(2)}) copy-start(f32[128,32]{0,1:T(8,128)S(1)} %fusion.70) | copy-start | bytes 49156
  751.0 54.6 %all-to-all-start.3 = ((bf16[1,4,512,1024]{3,1,0,2:T(4,128)(2,1)}), bf16[1,4,512,1024]{3,1,0,2:T(4,128)(2,1)}, u32[]{:S(2)}, u32[]{:S(2)}) async-start(bf16[1,4,512,1024]{3,1,0,2:T(4,128)(2,1)} %copy.195), calls=%async_computation.3 | async-start | bytes 8388608 | tf_op jit(solution)/shard_map/all_to_all | solution.py:265
  756.6 201.7 %reduce-scatter.10.cloned.1.call-start = ((), (), s32[]{:S(2)}) async-start(), calls=%async_computation.20 | async-start | bytes 2228224 | tf_op jit(solution)/shard_map/reduce_scatter | solution.py:331
  889.1 149.9 %reduce-scatter.12.cloned.1.call-start = ((), (), s32[]{:S(2)}) async-start(), calls=%async_computation.21 | async-start | bytes 2228224 | tf_op jit(solution)/shard_map/reduce_scatter | solution.py:337
  889.8 202.1 %reduce-scatter.14.cloned.1.call-start = ((), (), s32[]{:S(2)}) async-start(), calls=%async_computation.22 | async-start | bytes 2359296 | tf_op jit(solution)/shard_map/reduce_scatter | solution.py:384
  893.1 221.1 %reduce-scatter.20.cloned.1.call-start = ((), (), s32[]{:S(2)}) async-start(), calls=%async_computation.25 | async-start | bytes 2359296 | tf_op jit(solution)/shard_map/reduce_scatter | solution.py:399
  895.2 146.2 %copy-start.34 = (f32[128,32]{0,1:T(8,128)S(1)}, f32[128,32]{0,1:T(8,128)}, u32[]{:S(2)}) copy-start(f32[128,32]{0,1:T(8,128)} %copy-done.33) | copy-start | bytes 49156
  895.3 146.2 %copy-start.36 = (f32[128,32]{0,1:T(8,128)S(1)}, f32[128,32]{0,1:T(8,128)}, u32[]{:S(2)}) copy-start(f32[128,32]{0,1:T(8,128)} %copy-done.35) | copy-start | bytes 49156
  895.3 146.2 %copy-start.51 = (f32[128]{0:T(128)S(1)}, f32[128]{0:T(128)}, u32[]{:S(2)}) copy-start(f32[128]{0:T(128)} %copy-done.50) | copy-start | bytes 1540
  895.3 251.9 %reduce-scatter.16.cloned.1.call-start = ((), (), s32[]{:S(2)}) async-start(), calls=%async_computation.23 | async-start | bytes 1179648 | tf_op jit(solution)/shard_map/reduce_scatter | solution.py:387
  961.9 218.2 %reduce-scatter.18.cloned.1.call-start = ((), (), s32[]{:S(2)}) async-start(), calls=%async_computation.24 | async-start | bytes 1179648 | tf_op jit(solution)/shard_map/reduce_scatter | solution.py:390
  1041.4 212.9 %reduce-scatter.22.cloned.1.call-start = ((), (), s32[]{:S(2)}) async-start(), calls=%async_computation.26 | async-start | bytes 294912
  1042.6 366.2 %all-reduce.16.cloned.1.call-start = ((), (), s32[]{:S(2)}) async-start(), calls=%async_computation.27 | async-start | bytes 26738688 | tf_op jit(solution)/shard_map/psum | solution.py:371
  1180.2 77.6 %copy-start.26 = (bf16[128,512]{1,0:T(8,128)(2,1)S(1)}, bf16[128,512]{1,0:T(8,128)(2,1)}, u32[]{:S(2)}) copy-start(bf16[128,512]{1,0:T(8,128)(2,1)} %reduce-scatter.12.cloned.1.call-done) | copy-start | bytes 393220
  1180.2 78.2 %copy-start.54 = (bf16[512]{0:T(512)(128)(2,1)S(1)}, bf16[512]{0:T(512)(128)(2,1)}, u32[]{:S(2)}) copy-start(bf16[512]{0:T(512)(128)(2,1)} %get-tuple-element.863) | copy-start | bytes 3076
  1180.2 153.7 %copy-start.56 = (f32[128]{0:T(128)S(1)}, f32[128]{0:T(128)}, u32[]{:S(2)}) copy-start(f32[128]{0:T(128)} %copy-done.55) | copy-start | bytes 1540
  (59 other events, 1098.3 us)
Sparse Core Ops, SparseCore 0:
  9.8 26.9 all-gather.17
  38.5 23.1 all-gather.13
  63.4 25.0 all-gather.21
  90.5 67.6 all-gather.19
  160.2 78.1 all-gather.15
  240.0 35.0 all-gather.23
  277.3 94.3 all-gather.25
  374.0 97.0 all-gather.27
  473.3 97.1 all-gather.29
  889.2 69.1 reduce-scatter.9
  960.8 78.1 reduce-scatter.11
  1041.2 37.9 reduce-scatter.13
  1081.7 32.4 reduce-scatter.19
  1116.4 30.7 reduce-scatter.15
  1149.4 30.7 reduce-scatter.17
  1182.9 29.6 reduce-scatter.21
  1218.0 190.8 all-reduce.15
where the time goes:
time: 1440 us; the launch traced here: 1430 us
  waiting for transfers between devices  642 us (45%)
  blocking collectives  388 us (27%)
  local copies, waits for them, and re-layouts  152 us (11%)
  matrix products  128 us (9%)
  other arithmetic  72.2 us (5%)
  between operations  21 us (1%)
  starting transfers between devices  14.6 us (1%)
    all_gather x1, waiting for transfers between devices, per_device(): lax.all_gather(expert_up, ('ctx', 'dp'), axis=0, tiled=True)  91.5 us
    all_gather x1, waiting for transfers between devices, per_device(): lax.all_gather(expert_down, ('ctx', 'dp'), axis=0, tiled=True)  90.2 us
    reduce_scatter x1, waiting for transfers between devices, per_device(): lax.psum_scatter(d_values_all.reshape(seq_len, kv_width).astype(jnp.bfloa...  77 us
    psum x1, waiting for transfers between devices, per_device(): lax.psum(grads[1].astype(jnp.bfloat16), ('ctx', 'dp')).astype(jnp.float32)  73.9 us
    psum x1, blocking collectives, per_device(): lax.psum((jnp.sum(err * err), jnp.sum(valid.astype(jnp.float32))), ('expe...  69.5 us
    reduce_scatter x1, waiting for transfers between devices, per_device(): lax.psum_scatter(d_keys_all.reshape(seq_len, kv_width).astype(jnp.bfloat1...  63 us
    psum x1, blocking collectives, per_device(): lax.psum(grads[0].astype(jnp.bfloat16), ('ctx', 'dp')).astype(jnp.float32)  59.1 us
    all_to_all x1, blocking collectives, per_device(): lax.all_to_all(send_rows, 'expert', split_axis=0, concat_axis=2, tiled=True)  58.2 us
  transfers between devices with their start and end apart: 19, of which 14 were waited for; matrix products, arithmetic and copies ran while one was open for 14% of the time, Pallas kernels for 0%

commit v1 on v0

v1 whole, which is shorter than its diff:
```python
import jax
import jax.numpy as jnp
from jax import lax
from jax.experimental import pallas as pl
from jax.experimental.pallas import tpu as pltpu
from jax.sharding import PartitionSpec as P

MESH = pl.DeviceIdType.MESH
F32 = jnp.float32
BF16 = jnp.bfloat16

HEAD = 64
TOP = 8
EPS = 1e-06
THETA = 10000.0
NEG = -1e30
HIGH = lax.Precision.HIGHEST


def mm(a, b):
    return lax.dot_general(a, b, (((1,), (0,)), ((), ())), preferred_element_type=F32)


def mm_nt(a, b):
    return lax.dot_general(a, b, (((1,), (1,)), ((), ())), preferred_element_type=F32)


def mm_tn(a, b):
    return lax.dot_general(a, b, (((0,), (0,)), ((), ())), preferred_element_type=F32)


def places():
    e, c, d = lax.axis_index("expert"), lax.axis_index("ctx"), lax.axis_index("dp")
    return e // 2, e % 2, c, d


def remote(src, dst, send, recv, device):
    return pltpu.make_async_remote_copy(
        src_ref=src, dst_ref=dst, send_sem=send, recv_sem=recv, device_id=device, device_id_type=MESH
    )


def line_device(x, core):
    return (lax.rem(x + 4, 4) * 2 + core, lax.axis_index("ctx"), lax.axis_index("dp"))


def greet_line():
    barrier = pltpu.get_barrier_semaphore()
    e, c, d = lax.axis_index("expert"), lax.axis_index("ctx"), lax.axis_index("dp")
    for o in range(1, 8):
        pl.semaphore_signal(barrier, inc=1, device_id=(lax.rem(e + o, 8), c, d), device_id_type=MESH)
    pl.semaphore_wait(barrier, 7)


def line_gather_start(own, buf, send, recv):
    x, core, _, _ = places()
    me = x * 2 + core
    copies = [remote(own, buf(me), send.at[o], recv.at[o], line_device(x + o, core)) for o in (2, 1, 3)]
    copies.append(remote(own, buf(me), send.at[0], recv.at[0], line_device(x, 1 - core)))
    for copy in copies:
        copy.start()
    return copies


def line_gather_finish(copies, buf, send, recv):
    x, core, _, _ = places()
    forwards = []
    for at, o in ((1, 1), (2, 3), (0, 2)):
        copies[at].wait_recv()
        block = buf(lax.rem(x - o + 4, 4) * 2 + core)
        copy = remote(block, block, send.at[4 + o], recv.at[4 + o], line_device(x, 1 - core))
        copy.start()
        forwards.append(copy)
    copies[3].wait_recv()
    for copy in forwards:
        copy.wait_recv()
    for copy in copies + forwards:
        copy.wait_send()


def line_scatter_send_pair(pair, sib, send, recv):
    x, core, _, _ = places()
    copy = remote(pair, sib, send.at[0], recv.at[0], line_device(x, 1 - core))
    copy.start()
    return copy


def line_scatter_send_x(mine, pair_copy, sib, inbox, send, recv):
    x, core, _, _ = places()
    pair_copy.wait_recv()
    copies = []
    for o in (2, 1, 3):
        to = lax.rem(x + o, 4)
        mine[to] = (mine[to].astype(F32) + sib[to].astype(F32)).astype(mine.dtype)
        copy = remote(mine.at[to], inbox.at[o - 1], send.at[o], recv.at[o], line_device(x + o, core))
        copy.start()
        copies.append(copy)
    return copies


def line_scatter_sum(mine, sib, inbox, copies):
    x, _, _, _ = places()
    total = mine[x].astype(F32) + sib[x].astype(F32)
    for at, o in ((1, 1), (2, 3), (0, 2)):
        copies[at].wait_recv()
        total = total + inbox[o - 1].astype(F32)
    return total


def moe_kernel(
    wg_hbm, xall, meta, residual, teacher, valid_row,
    mixed, err_out, stats, dw_hbm, dmid, dgates,
    wg, pcat, gslot, xc, oc, dc, gpre, upre, gact, dg, du,
    mine1, pair1, sib1, inbox1, dlow, dall, mine2, pair2, sib2, inbox2, dgsend, stage,
    load_sem, s1, r1, s2, r2, s3, r3, s4, r4, store_sem,
):
    x, core, _, _ = places()
    me = x * 2 + core
    loads = [pltpu.make_async_copy(wg_hbm.at[m], wg.at[m], load_sem.at[m]) for m in range(12)]
    for m in (0, 4, 8, 1, 5, 9, 2, 6, 10, 3, 7, 11):
        loads[m].start()
    greet_line()

    slot_ids = lax.broadcasted_iota(jnp.int32, (64, 128), 0).astype(F32)

    def compact(s, _):
        for e in range(4):
            hit = slot_ids == meta[s, 4 + e : 5 + e, :]
            pcat[s, e * 64 : (e + 1) * 64, :] = hit.astype(F32).astype(BF16)
            gate = jnp.sum(jnp.where(hit, meta[s, e : e + 1, :], 0.0), axis=1, keepdims=True)
            gslot[e, s] = jnp.broadcast_to(gate, (64, 128))
        rows = mm(pcat[s], xall[s]).astype(BF16)
        for e in range(4):
            xc[e, s] = rows[e * 64 : (e + 1) * 64]
        return 0

    lax.fori_loop(0, 8, compact, 0)
    for copy in loads:
        copy.wait()

    def forward(e, _):
        rows = xc[e].reshape(512, 1024)
        g = mm(rows, wg[e])
        u = mm(rows, wg[4 + e])
        gpre[e] = g
        upre[e] = u
        act = g * jax.nn.sigmoid(g) * u
        gate = gslot[e].reshape(512, 128)[:, :1]
        gact[e] = (act * gate).astype(BF16)
        back = mm_nt(act.astype(BF16), wg[8 + e]) * gate
        oc[e] = back.astype(BF16).reshape(8, 64, 1024)
        return 0

    lax.fori_loop(0, 4, forward, 0)

    def combine(mine, pair):
        def one(xs, _):
            for k in range(2):
                s = xs * 2 + (1 - core if k == 0 else core)
                rows = jnp.concatenate([oc[e, s] for e in range(4)], axis=0)
                part = mm_tn(pcat[s], rows).astype(BF16)
                if k == 0:
                    pair[xs] = part
                else:
                    mine[xs] = part
            return 0

        lax.fori_loop(0, 4, one, 0)

    combine(mine1, pair1)
    pair_copy = line_scatter_send_pair(pair1, sib1, s1, r1)
    x_copies = line_scatter_send_x(mine1, pair_copy, sib1, inbox1, s1, r1)
    out = residual[...] + line_scatter_sum(mine1, sib1, inbox1, x_copies)
    mixed[...] = out.astype(BF16)
    eye = lax.broadcasted_iota(jnp.int32, (128, 128), 0) == lax.broadcasted_iota(jnp.int32, (128, 128), 1)
    valid_col = jnp.sum(jnp.where(eye, valid_row[0:1, :], 0.0), axis=1, keepdims=True)
    err = (out - teacher[...]) * valid_col
    err_out[...] = err
    dlow[...] = err.astype(BF16)
    dall[me] = dlow[...]
    gather = line_gather_start(dlow, lambda i: dall.at[i], s2, r2)
    square = jnp.sum(jnp.sum(err * err, axis=1, keepdims=True), axis=0, keepdims=True)
    count = jnp.sum(valid_row[0:1, :], axis=1, keepdims=True)
    stats[0:1, :] = jnp.broadcast_to(square, (1, 128))
    stats[1:2, :] = jnp.broadcast_to(count, (1, 128))
    stats[2:8, :] = jnp.zeros((6, 128), F32)
    line_gather_finish(gather, lambda i: dall.at[i], s2, r2)

    def spread(s, _):
        rows = mm(pcat[s], dall[s]).astype(BF16)
        for e in range(4):
            dc[e, s] = rows[e * 64 : (e + 1) * 64]
        return 0

    lax.fori_loop(0, 8, spread, 0)

    def backward(e, _):
        g = gpre[e]
        u = upre[e]
        sigma = jax.nn.sigmoid(g)
        silu = g * sigma
        gate = gslot[e].reshape(512, 128)[:, :1]
        raw = mm(dc[e].reshape(512, 1024), wg[8 + e])
        act = (silu * u).astype(BF16).astype(F32)
        dgate = jnp.sum(raw * act, axis=1, keepdims=True)
        gslot[e] = jnp.broadcast_to(dgate, (512, 128)).reshape(8, 64, 128)
        da = raw * gate
        dg_e = (da * u * (sigma * (1.0 + g * (1.0 - sigma)))).astype(BF16)
        du_e = (da * silu).astype(BF16)
        dg[e] = dg_e
        du[e] = du_e
        dx = mm_nt(dg_e, wg[e]) + mm_nt(du_e, wg[4 + e])
        oc[e] = dx.astype(BF16).reshape(8, 64, 1024)
        return 0

    lax.fori_loop(0, 4, backward, 0)
    combine(mine2, pair2)
    pair_copy2 = line_scatter_send_pair(pair2, sib2, s3, r3)

    def gate_rows(s, _):
        rows = []
        for e in range(4):
            hit = pcat[s, e * 64 : (e + 1) * 64, :].astype(F32)
            rows.append(jnp.sum(hit * gslot[e, s], axis=0, keepdims=True))
        dgsend[s] = jnp.concatenate(rows + [jnp.zeros((4, 128), F32)], axis=0)
        return 0

    lax.fori_loop(0, 8, gate_rows, 0)
    gate_copies = []
    c, d = lax.axis_index("ctx"), lax.axis_index("dp")
    for o in range(1, 8):
        to = lax.rem(me + o, 8)
        copy = remote(dgsend.at[to], dgates.at[me], s4.at[o], r4.at[o], (to, c, d))
        copy.start()
        gate_copies.append(copy)
    dgates[me] = dgsend[me]
    x_copies2 = line_scatter_send_x(mine2, pair_copy2, sib2, inbox2, s3, r3)

    def weight_grads(e, _):
        rows = xc[e].reshape(512, 1024)
        drows = dc[e].reshape(512, 1024)
        for m, (a, b) in enumerate(((rows, dg[e]), (rows, du[e]), (drows, gact[e]))):
            copy = pltpu.make_async_copy(stage.at[m], dw_hbm.at[m * 4 + e], store_sem.at[m])

            @pl.when(e > 0)
            def _():
                copy.wait()

            stage[m] = mm_tn(a, b).astype(BF16)
            copy.start()
        return 0

    lax.fori_loop(0, 4, weight_grads, 0)
    dmid[...] = line_scatter_sum(mine2, sib2, inbox2, x_copies2)
    for copy in gate_copies:
        copy.wait()
    for m in range(3):
        pltpu.make_async_copy(stage.at[m], dw_hbm.at[m * 4], store_sem.at[m]).wait()
    for copy in [pair_copy, pair_copy2] + x_copies + x_copies2:
        copy.wait_send()


def moe(wg, xall, meta, residual, teacher, valid_row):
    vm = pl.BlockSpec(memory_space=pltpu.VMEM)
    hbm = pl.BlockSpec(memory_space=pl.ANY)
    sems = pltpu.SemaphoreType.DMA
    return pl.pallas_call(
        moe_kernel,
        out_shape=(
            jax.ShapeDtypeStruct((128, 1024), BF16),
            jax.ShapeDtypeStruct((128, 1024), F32),
            jax.ShapeDtypeStruct((8, 128), F32),
            jax.ShapeDtypeStruct((12, 1024, 512), BF16),
            jax.ShapeDtypeStruct((128, 1024), F32),
            jax.ShapeDtypeStruct((8, 8, 128), F32),
        ),
        in_specs=[hbm, vm, vm, vm, vm, vm],
        out_specs=(vm, vm, vm, hbm, vm, vm),
        scratch_shapes=[
            pltpu.VMEM((12, 1024, 512), BF16),
            pltpu.VMEM((8, 256, 128), BF16),
            pltpu.VMEM((4, 8, 64, 128), F32),
            pltpu.VMEM((4, 8, 64, 1024), BF16),
            pltpu.VMEM((4, 8, 64, 1024), BF16),
            pltpu.VMEM((4, 8, 64, 1024), BF16),
            pltpu.VMEM((4, 512, 512), F32),
            pltpu.VMEM((4, 512, 512), F32),
            pltpu.VMEM((4, 512, 512), BF16),
            pltpu.VMEM((4, 512, 512), BF16),
            pltpu.VMEM((4, 512, 512), BF16),
            pltpu.VMEM((4, 128, 1024), BF16),
            pltpu.VMEM((4, 128, 1024), BF16),
            pltpu.VMEM((4, 128, 1024), BF16),
            pltpu.VMEM((3, 128, 1024), BF16),
            pltpu.VMEM((128, 1024), BF16),
            pltpu.VMEM((8, 128, 1024), BF16),
            pltpu.VMEM((4, 128, 1024), BF16),
            pltpu.VMEM((4, 128, 1024), BF16),
            pltpu.VMEM((4, 128, 1024), BF16),
            pltpu.VMEM((3, 128, 1024), BF16),
            pltpu.VMEM((8, 8, 128), F32),
            pltpu.VMEM((3, 1024, 512), BF16),
            sems((12,)),
            sems((4,)),
            sems((4,)),
            sems((8,)),
            sems((8,)),
            sems((4,)),
            sems((4,)),
            sems((8,)),
            sems((8,)),
            sems((3,)),
        ],
        compiler_params=pltpu.CompilerParams(
            collective_id=1, has_side_effects=True, vmem_limit_bytes=63 << 20
        ),
        cost_estimate=pl.CostEstimate(flops=22 * 10**9, bytes_accessed=30 << 20, transcendentals=4 << 20),
        name="moe",
    )(wg, xall, meta, residual, teacher, valid_row)


def plane_device(y, z):
    return (lax.axis_index("expert"), lax.div(z, 2) * 4 + y, lax.rem(z, 2))


def yz():
    c, d = lax.axis_index("ctx"), lax.axis_index("dp")
    return lax.rem(c, 4), lax.div(c, 4) * 2 + d


def greet_all():
    barrier = pltpu.get_barrier_semaphore()
    e, c, d = lax.axis_index("expert"), lax.axis_index("ctx"), lax.axis_index("dp")
    p = c * 2 + d
    for o in range(1, 8):
        pl.semaphore_signal(barrier, inc=1, device_id=(lax.rem(e + o, 8), c, d), device_id_type=MESH)
    for o in range(1, 16):
        q = lax.rem(p + o, 16)
        pl.semaphore_signal(barrier, inc=1, device_id=(e, lax.div(q, 2), lax.rem(q, 2)), device_id_type=MESH)
    pl.semaphore_wait(barrier, 22)


def low_lanes():
    return lax.broadcasted_iota(jnp.int32, (128, 128), 1) < 64


def swap_halves(tile):
    lane = lax.rem(lax.broadcasted_iota(jnp.int32, (128, 128), 1), 64)
    return jnp.where(lane < 32, pltpu.roll(tile, 96, 1), pltpu.roll(tile, 32, 1))


def gain_row(small, row):
    return jnp.concatenate([small[i, row : row + 1, :] for i in range(8)], axis=1)


def key_gain_row(small):
    lane = lax.broadcasted_iota(jnp.int32, (1, 128), 1)
    return jnp.concatenate(
        [jnp.where(lane < 64, small[2 * t, 3:4, :], small[2 * t + 1, 3:4, :]) for t in range(4)], axis=1
    )


def router_rows(small):
    return jnp.concatenate([small[i, 16:48, :] for i in range(8)], axis=1)


def inverse_rms(values):
    return lax.rsqrt(jnp.mean(values * values, axis=1, keepdims=True) + EPS)


def key_bias(vbuf, c):
    row = jnp.concatenate([vbuf[2 * c, 0:1, :], vbuf[2 * c + 1, 0:1, :]], axis=1)
    return (row - 1.0) * 1e30


def diagonal(d):
    row = lax.rem(lax.broadcasted_iota(jnp.int32, (256, 256), 0), 128) + 128 * d
    return row == lax.broadcasted_iota(jnp.int32, (256, 256), 1)


def stack_heads(tile, upper):
    lo = low_lanes()
    turned = pltpu.roll(tile, 64, 1)
    first, second = (turned, tile) if upper else (tile, turned)
    keep = jnp.logical_not(lo) if upper else lo
    return jnp.concatenate([jnp.where(keep, first, 0.0), jnp.where(keep, second, 0.0)], axis=0)


def front_kernel(
    tokens, wq, wk, wv, wo, small, ew, valid, cosine, sine, routes,
    wg, wall_out, small_all, vbuf, kvbuf, qbuf, oheads, lse, att, residual, normed_t, qpre, kpre, xall, meta, probs_out, picks_out,
    wall, sendkv, sendq, osend, low, metasend,
    own_sem, ew_sem, wall_sem, ssm, rsm, sqkv, rqkv, swo, rwo, sv, rv, sa1, ra1, sb1, rb1, sa2, ra2, sb2, rb2,
    skv, rkv, sq, rq, so, ro, sx, rx, sm, rm,
):
    x, core, c, d = places()
    me = x * 2 + core
    p = c * 2 + d
    y, z = yz()
    zh, zl = lax.div(z, 2), lax.rem(z, 2)
    e = lax.axis_index("expert")
    own = [
        pltpu.make_async_copy(wq, wall.at[me, :, pl.ds(0, 1024)], own_sem.at[0]),
        pltpu.make_async_copy(wk, wall.at[me, :, pl.ds(1024, 512)], own_sem.at[1]),
        pltpu.make_async_copy(wv, wall.at[me, :, pl.ds(1536, 512)], own_sem.at[2]),
        pltpu.make_async_copy(wo, wall.at[me, :, pl.ds(2048, 1024)], own_sem.at[3]),
    ]
    for copy in own:
        copy.start()
    own_ew = pltpu.make_async_copy(ew, wg.at[:, zh, y, zl], ew_sem)
    own_ew.start()
    small_all[me] = small[...]
    vbuf[p] = valid[...]
    greet_all()

    small_gather = line_gather_start(small, lambda i: small_all.at[i], ssm, rsm)
    ew_a, ew_b = ew.at[pl.ds(0, 6)], ew.at[pl.ds(6, 6)]
    a1 = [
        remote(ew_a, wg.at[pl.ds(0, 6), zh, y, zl], sa1.at[o], ra1.at[o], plane_device(lax.rem(y + o, 4), z))
        for o in (2, 1, 3)
    ]
    b1 = [
        remote(ew_b, wg.at[pl.ds(6, 6), zh, y, zl], sb1.at[o], rb1.at[o], plane_device(y, lax.rem(z + o, 4)))
        for o in (2, 1, 3)
    ]
    for copy in a1 + b1:
        copy.start()
    for copy in own[:3]:
        copy.wait()
    qkv_gather = line_gather_start(
        wall.at[me, :, pl.ds(0, 2048)], lambda i: wall.at[i, :, pl.ds(0, 2048)], sqkv, rqkv
    )
    own[3].wait()
    out_gather = line_gather_start(
        wall.at[me, :, pl.ds(2048, 1024)], lambda i: wall.at[i, :, pl.ds(2048, 1024)], swo, rwo
    )
    valid_copies = []
    for o in range(1, 16):
        q = lax.rem(p + o, 16)
        copy = remote(valid, vbuf.at[p], sv.at[o], rv.at[o], (e, lax.div(q, 2), lax.rem(q, 2)))
        copy.start()
        valid_copies.append(copy)

    line_gather_finish(small_gather, lambda i: small_all.at[i], ssm, rsm)
    gains = small_all[...].astype(F32)
    values = tokens[...].astype(F32)
    normed = (values * inverse_rms(values) * gain_row(gains, 0)).astype(BF16)
    for t in range(8):
        normed_t[t] = normed[:, 128 * t : 128 * t + 128]

    own_ew.wait()
    for copy in a1 + b1:
        copy.wait_recv()
    a2, b2 = [], []
    for o in (2, 1, 3):
        view = wg.at[pl.ds(0, 6), zh, :, zl]
        a2.append(remote(view, view, sa2.at[o], ra2.at[o], plane_device(y, lax.rem(z + o, 4))))
        view = wg.at[pl.ds(6, 6), :, y, :]
        b2.append(remote(view, view, sb2.at[o], rb2.at[o], plane_device(lax.rem(y + o, 4), z)))
    for copy in a2 + b2:
        copy.start()

    line_gather_finish(qkv_gather, lambda i: wall.at[i, :, pl.ds(0, 2048)], sqkv, rqkv)
    q_pre = mm(normed, wall[:, :, 0:1024].reshape(1024, 1024))
    k_pre = mm(normed, wall[:, :, 1024:1536].reshape(1024, 512))
    v_low = mm(normed, wall[:, :, 1536:2048].reshape(1024, 512)).astype(BF16).astype(F32)
    qpre[...] = q_pre
    kpre[...] = k_pre
    cos, sin = cosine[...], sine[...]
    lo = low_lanes()
    kn = k_pre * inverse_rms(k_pre) * key_gain_row(gains)
    for t in range(4):
        tile = kn[:, 128 * t : 128 * t + 128]
        k_rot = tile * cos + swap_halves(tile) * sin
        v_tile = v_low[:, 128 * t : 128 * t + 128]
        sendkv[2 * t] = jnp.where(lo, k_rot, pltpu.roll(v_tile, 64, 1)).astype(BF16)
        sendkv[2 * t + 1] = jnp.where(lo, pltpu.roll(k_rot, 64, 1), v_tile).astype(BF16)
    kvbuf[p] = sendkv[c]
    kv_copies = []
    for o in range(1, 16):
        q = lax.rem(p + o, 16)
        to = lax.div(q, 2)
        copy = remote(sendkv.at[to], kvbuf.at[p], skv.at[o], rkv.at[o], (e, to, lax.rem(q, 2)))
        copy.start()
        kv_copies.append(copy)
    qn = q_pre * inverse_rms(q_pre) * gain_row(gains, 1)
    for t in range(8):
        tile = qn[:, 128 * t : 128 * t + 128]
        sendq[t] = (tile * cos + swap_halves(tile) * sin).astype(BF16)
    qbuf[c] = sendq[c]
    q_copies = []
    for o in range(1, 8):
        to = lax.rem(c + o, 8)
        copy = remote(sendq.at[to], qbuf.at[c], sq.at[o], rq.at[o], (e, to, d))
        copy.start()
        q_copies.append(copy)
    for copy in valid_copies + kv_copies + q_copies:
        copy.wait_recv()

    def chunk(i, _):
        b = lax.rem(c + 1 + i, 8)
        queries = (stack_heads(qbuf[b].astype(F32), False) * (HEAD**-0.5)).astype(BF16)

        def update(carry, block, scores):
            top, total, acc = carry
            new_top = jnp.maximum(top, jnp.max(scores, axis=1, keepdims=True))
            weights = jnp.exp(scores - new_top)
            shrink = jnp.exp(top - new_top)
            total = total * shrink + jnp.sum(weights, axis=1, keepdims=True)
            acc = acc * shrink + mm(weights.astype(BF16), block)
            return (new_top, total, acc)

        def keys(k, carry):
            block = kvbuf[pl.ds(2 * k, 2)].reshape(256, 128)
            return update(carry, block, mm_nt(queries, block) + key_bias(vbuf, k))

        zero = jnp.zeros((256, 1), F32)
        carry = lax.fori_loop(0, b, keys, (zero + NEG, zero, jnp.zeros((256, 128), F32)))
        block = kvbuf[pl.ds(2 * b, 2)].reshape(256, 128)
        scores = mm_nt(queries, block)
        scores = jnp.where(diagonal(d), scores, scores + key_bias(vbuf, b))
        top, total, acc = update(carry, block, scores)
        acc = acc / total
        lse[b] = jnp.broadcast_to(top + jnp.log(total), (256, 128))
        merged = jnp.where(lo, pltpu.roll(acc[:128], 64, 1), acc[128:])
        oheads[b] = merged
        osend[b] = merged.astype(BF16)

        @pl.when(b != c)
        def _():
            remote(osend.at[b], att.at[c], so.at[b], ro.at[c], (e, b, d)).start()

        @pl.when(b == c)
        def _():
            att[c] = osend[c]

        return 0

    lax.fori_loop(0, 8, chunk, 0)
    line_gather_finish(out_gather, lambda i: wall.at[i, :, pl.ds(2048, 1024)], swo, rwo)
    store = pltpu.make_async_copy(wall, wall_out, wall_sem)
    store.start()

    def wait_rest(i, _):
        b = lax.rem(c + 1 + i, 8)
        copy = remote(osend.at[b], att.at[b], so.at[b], ro.at[b], (e, b, d))
        copy.wait_send()
        copy.wait_recv()
        return 0

    lax.fori_loop(0, 7, wait_rest, 0)
    attended = jnp.concatenate([att[t] for t in range(8)], axis=1)
    res = tokens[...].astype(F32) + mm(attended, wall[:, :, 2048:3072].reshape(1024, 1024))
    residual[...] = res
    mid = (res * inverse_rms(res) * gain_row(gains, 2)).astype(BF16)
    low[...] = mid
    xall[me] = mid
    mid_gather = line_gather_start(low, lambda i: xall.at[i], sx, rx)
    logits = mm_nt(router_rows(small_all[...]), mid)
    terms = jnp.exp(logits - jnp.max(logits, axis=0, keepdims=True))
    probs = terms / jnp.sum(terms, axis=0, keepdims=True)
    ids = lax.broadcasted_iota(jnp.int32, (32, 128), 0)
    picks = jnp.zeros((32, 128), F32)
    for k in range(TOP):
        picks = picks + (ids == routes[k : k + 1, :]).astype(F32)
    before = lax.broadcasted_iota(jnp.int32, (128, 128), 0) < lax.broadcasted_iota(jnp.int32, (128, 128), 1)
    slots = mm(picks.astype(BF16), before.astype(F32).astype(BF16))
    slots = jnp.where(picks > 0.0, slots, -1.0)
    probs_out[...] = probs
    picks_out[...] = picks
    gates = probs * picks
    for i in range(8):
        metasend[i, 0:4, :] = gates[4 * i : 4 * i + 4, :]
        metasend[i, 4:8, :] = slots[4 * i : 4 * i + 4, :]
    meta[me] = metasend[me]
    meta_copies = []
    for o in range(1, 8):
        to = lax.rem(me + o, 8)
        copy = remote(metasend.at[to], meta.at[me], sm.at[o], rm.at[o], (to, c, d))
        copy.start()
        meta_copies.append(copy)
    line_gather_finish(mid_gather, lambda i: xall.at[i], sx, rx)
    for copy in meta_copies:
        copy.wait()
    for copy in a2 + b2:
        copy.wait()
    for copy in a1 + b1 + valid_copies + kv_copies + q_copies:
        copy.wait_send()
    store.wait()


def front(tokens, wq, wk, wv, wo, small, ew, valid, cosine, sine, routes):
    vm = pl.BlockSpec(memory_space=pltpu.VMEM)
    hbm = pl.BlockSpec(memory_space=pl.ANY)
    sems = pltpu.SemaphoreType.DMA
    shape = jax.ShapeDtypeStruct
    return pl.pallas_call(
        front_kernel,
        out_shape=(
            shape((12, 2, 4, 2, 64, 512), BF16),
            shape((8, 128, 3072), BF16),
            shape((8, 48, 128), BF16),
            shape((16, 8, 128), F32),
            shape((16, 128, 128), BF16),
            shape((8, 128, 128), BF16),
            shape((8, 128, 128), F32),
            shape((8, 256, 128), F32),
            shape((8, 128, 128), BF16),
            shape((128, 1024), F32),
            shape((8, 128, 128), BF16),
            shape((128, 1024), F32),
            shape((128, 512), F32),
            shape((8, 128, 1024), BF16),
            shape((8, 8, 128), F32),
            shape((32, 128), F32),
            shape((32, 128), F32),
        ),
        in_specs=[vm, hbm, hbm, hbm, hbm, vm, hbm, vm, vm, vm, vm],
        out_specs=(hbm, hbm) + (vm,) * 15,
        scratch_shapes=[
            pltpu.VMEM((8, 128, 3072), BF16),
            pltpu.VMEM((8, 128, 128), BF16),
            pltpu.VMEM((8, 128, 128), BF16),
            pltpu.VMEM((8, 128, 128), BF16),
            pltpu.VMEM((128, 1024), BF16),
            pltpu.VMEM((8, 8, 128), F32),
            sems((4,)), sems(()), sems(()),
            sems((8,)), sems((8,)), sems((8,)), sems((8,)), sems((8,)), sems((8,)),
            sems((16,)), sems((16,)),
            sems((4,)), sems((4,)), sems((4,)), sems((4,)), sems((4,)), sems((4,)), sems((4,)), sems((4,)),
            sems((16,)), sems((16,)),
            sems((8,)), sems((8,)), sems((8,)), sems((8,)), sems((8,)), sems((8,)), sems((8,)), sems((8,)),
        ],
        compiler_params=pltpu.CompilerParams(
            collective_id=0, has_side_effects=True, vmem_limit_bytes=48 << 20
        ),
        cost_estimate=pl.CostEstimate(flops=3 * 10**9, bytes_accessed=30 << 20, transcendentals=3 << 20),
        name="front",
    )(tokens, wq, wk, wv, wo, small, ew, valid, cosine, sine, routes)


def line_scatter_begin(parts_of, pair, mine, sib, send, recv):
    x, core, _, _ = places()

    def one(k, _):
        pair[k] = parts_of(k * 2 + 1 - core)
        return 0

    def other(k, _):
        mine[k] = parts_of(k * 2 + core)
        return 0

    lax.fori_loop(0, 4, one, 0)
    copy = line_scatter_send_pair(pair, sib, send, recv)
    lax.fori_loop(0, 4, other, 0)
    return copy


def plane_peer(o):
    e, c, d = lax.axis_index("expert"), lax.axis_index("ctx"), lax.axis_index("dp")
    q = lax.rem(c * 2 + d + o, 16)
    return q, (e, lax.div(q, 2), lax.rem(q, 2))


def plane_sum_send(pieces, n, inbox, send, recv):
    copies = []
    for o in range(1, 16):
        q, device = plane_peer(o)
        copy = remote(pieces.at[pl.ds(q * n, n)], inbox.at[o], send.at[o], recv.at[o], device)
        copy.start()
        copies.append(copy)
    return copies


def plane_sum_share(copies, pieces, n, inbox, result, send, recv):
    p = lax.axis_index("ctx") * 2 + lax.axis_index("dp")
    total = pieces[pl.ds(p * n, n)].astype(F32)
    for at, copy in enumerate(copies):
        copy.wait_recv()
        total = total + inbox[at + 1].astype(F32)
    result[pl.ds(p * n, n)] = total.astype(BF16)
    shares = []
    view = result.at[pl.ds(p * n, n)]
    for o in range(1, 16):
        _, device = plane_peer(o)
        copy = remote(view, view, send.at[o], recv.at[o], device)
        copy.start()
        shares.append(copy)
    return shares


def rms_back(values, inverse, grad):
    hat = values * inverse
    return inverse * (grad - hat * jnp.mean(grad * hat, axis=1, keepdims=True))


def back_kernel(
    dw, wall_hbm, small_in, vbuf, kvbuf, qbuf, oheads, lse, att, residual, normed_t, qpre, kpre, xall,
    probs_in, picks_in, err, stats, dmid_in, dgates, tokens, cosine, sine,
    gw, gtok, gq, gk, gv, gout, gsmall,
    wall, own_a, own_b, in_a, in_b, sum_a, sum_b, in2_a, in2_b,
    dsend, dattbuf, qpad, dop, delta, dqacc, dkvsend, dqsend, dqbuf, dkvbuf, dqkv, dnorm, dlog,
    pair_o, mine_o, sib_o, inbox_o, pair_n, mine_n, sib_n, inbox_n, smsend, sminbox, smsum, small,
    pieces_o, pin_o, res_o, pieces_n, pin_n, res_n,
    wall_sem, own_sem, sa1, ra1, sb1, rb1, sa2, ra2, sb2, rb2, sd, rd, sdq, rdq, sdkv, rdkv,
    so, ro, sn, rn, ssm, rsm, sp1, rp1, sp2, rp2, sp3, rp3, sp4, rp4, sp5, rp5,
):
    x, core, c, d = places()
    me = x * 2 + core
    p = c * 2 + d
    y, z = yz()
    zh, zl = lax.div(z, 2), lax.rem(z, 2)
    e = lax.axis_index("expert")
    wall_load = pltpu.make_async_copy(wall_hbm, wall, wall_sem)
    wall_load.start()
    own = [
        pltpu.make_async_copy(dw.at[pl.ds(0, 6), zh, :, zl], own_a, own_sem.at[0]),
        pltpu.make_async_copy(dw.at[pl.ds(6, 6), :, y, :], own_b, own_sem.at[1]),
    ]
    for copy in own:
        copy.start()
    greet_all()
    a1, b1 = [], []
    for o in (2, 1, 3):
        to = lax.rem(z + o, 4)
        a1.append(remote(
            dw.at[pl.ds(0, 6), lax.div(to, 2), :, lax.rem(to, 2)], in_a.at[o - 1], sa1.at[o], ra1.at[o], plane_device(y, to)
        ))
        to = lax.rem(y + o, 4)
        b1.append(remote(dw.at[pl.ds(6, 6), :, to, :], in_b.at[o - 1], sb1.at[o], rb1.at[o], plane_device(to, z)))
    for copy in a1 + b1:
        copy.start()

    gains = small_in[...].astype(F32)
    lo = low_lanes()
    probs = probs_in[...]
    dprobs = jnp.concatenate([dgates[i, 0:4, :] for i in range(8)], axis=0) * picks_in[...]
    dlogits = probs * (dprobs - jnp.sum(probs * dprobs, axis=0, keepdims=True))
    high = dlogits.astype(BF16)
    rest = (dlogits - high.astype(F32)).astype(BF16)
    dlog[0:32, :] = high
    dlog[32:64, :] = rest

    def router_back(i, _):
        at = pl.ds(pl.multiple_of(128 * i, 128), 128)
        part = mm(dlog[...], xall[me, :, at])
        smsend[i, 16:48, :] = part[:32] + part[32:]
        router = small_in[i, 16:48, :]
        dnorm[i] = mm_tn(dlog[...], jnp.concatenate([router, router], axis=0))
        return 0

    lax.fori_loop(0, 8, router_back, 0)
    dmid = dmid_in[...] + jnp.concatenate([dnorm[i] for i in range(8)], axis=1)
    res = residual[...]
    res_inv = inverse_rms(res)
    dgain_mid = jnp.sum(dmid * (res * res_inv), axis=0, keepdims=True)
    dres = err[...] + rms_back(res, res_inv, dmid * gain_row(gains, 2))
    dbranch = dres.astype(BF16)
    gtok[...] = dres
    wall_load.wait()
    dqkv[:, 0:1024] = dbranch

    def attended_back(t, _):
        dsend[t] = mm_nt(dqkv[:, 0:1024], wall[t, :, 2048:3072]).astype(BF16)
        return 0

    lax.fori_loop(0, 8, attended_back, 0)
    dattbuf[c] = dsend[c]
    d_copies = []
    for o in range(1, 8):
        to = lax.rem(c + o, 8)
        copy = remote(dsend.at[to], dattbuf.at[c], sd.at[o], rd.at[o], (e, to, d))
        copy.start()
        d_copies.append(copy)
    pair_copy_o = line_scatter_begin(lambda i: mm_tn(att[i], dqkv[:, 0:1024]).astype(BF16), pair_o, mine_o, sib_o, so, ro)

    def prepare(b, _):
        qpad[b] = (stack_heads(qbuf[b].astype(F32), False) * (HEAD**-0.5)).astype(BF16)
        return 0

    lax.fori_loop(0, 8, prepare, 0)
    x_copies_o = line_scatter_send_x(mine_o, pair_copy_o, sib_o, inbox_o, so, ro)
    for copy in d_copies:
        copy.wait_recv()

    def prepare_back(b, _):
        tile = dattbuf[b].astype(F32)
        dop[b] = stack_heads(tile, True).astype(BF16)
        both = tile * oheads[b]
        first = jnp.sum(jnp.where(lo, both, 0.0), axis=1, keepdims=True)
        second = jnp.sum(jnp.where(lo, 0.0, both), axis=1, keepdims=True)
        delta[b] = jnp.broadcast_to(jnp.concatenate([first, second], axis=0), (256, 128))
        dqacc[b] = jnp.zeros((256, 128), F32)
        return 0

    lax.fori_loop(0, 8, prepare_back, 0)

    def key_block(k, _):
        block = kvbuf[pl.ds(2 * k, 2)].reshape(256, 128)
        bias = key_bias(vbuf, k)

        def one(b, acc, scores):
            weights = jnp.exp(scores - lse[b][:, 0:1])
            dweights = mm_nt(dop[b], block)
            dscores = (weights * (dweights - delta[b][:, 0:1])).astype(BF16)
            dqacc[b] = dqacc[b] + mm(dscores, block)
            return acc + mm_tn(weights.astype(BF16), dop[b]) + mm_tn(dscores, qpad[b])

        scores = mm_nt(qpad[k], block)
        acc = one(k, jnp.zeros((256, 128), F32), jnp.where(diagonal(d), scores, scores + bias))
        acc = lax.fori_loop(k + 1, 8, lambda b, acc: one(b, acc, mm_nt(qpad[b], block) + bias), acc)
        dkvsend[pl.ds(2 * k, 2)] = acc.astype(BF16).reshape(2, 128, 128)
        done = dqacc[k] * (HEAD**-0.5)
        dqsend[k] = jnp.where(lo, done[:128], pltpu.roll(done[128:], 64, 1)).astype(BF16)

        @pl.when(k != c)
        def _():
            remote(dqsend.at[k], dqbuf.at[c], sdq.at[k], rdq.at[c], (e, k, d)).start()
            remote(dkvsend.at[2 * k], dkvbuf.at[p], sdkv.at[2 * k], rdkv.at[p], (e, k, 0)).start()
            remote(dkvsend.at[2 * k + 1], dkvbuf.at[p], sdkv.at[2 * k + 1], rdkv.at[p], (e, k, 1)).start()

        @pl.when(k == c)
        def _():
            dqbuf[c] = dqsend[c]
            dkvbuf[p] = dkvsend[p]
            other = c * 2 + 1 - d
            remote(dkvsend.at[other], dkvbuf.at[p], sdkv.at[other], rdkv.at[p], (e, c, 1 - d)).start()

        return 0

    lax.fori_loop(0, 8, key_block, 0)

    sum_o = line_scatter_sum(mine_o, sib_o, inbox_o, x_copies_o).astype(BF16)
    for t in range(8):
        for h in range(2):
            pieces_o[2 * t + h] = sum_o[64 * h : 64 * h + 64, 128 * t : 128 * t + 128]
    p_copies_o = plane_sum_send(pieces_o, 1, pin_o, sp1, rp1)

    def wait_dq(i, _):
        b = lax.rem(c + 1 + i, 8)
        copy = remote(dqsend.at[b], dqbuf.at[b], sdq.at[b], rdq.at[b], (e, b, d))
        copy.wait_send()
        copy.wait_recv()
        return 0

    def wait_dkv(i, _):
        q = lax.rem(p + 1 + i, 16)
        copy = remote(dkvsend.at[q], dkvbuf.at[q], sdkv.at[q], rdkv.at[q], (e, lax.div(q, 2), lax.rem(q, 2)))
        copy.wait_send()
        copy.wait_recv()
        return 0

    lax.fori_loop(0, 7, wait_dq, 0)
    lax.fori_loop(0, 15, wait_dkv, 0)
    cos, sin = cosine[...], -sine[...]
    dq = jnp.concatenate([dqbuf[t] for t in range(8)], axis=1).astype(F32)
    dq = jnp.concatenate(
        [dq[:, 128 * t : 128 * t + 128] * cos + swap_halves(dq[:, 128 * t : 128 * t + 128]) * sin for t in range(8)], axis=1
    )
    q_pre = qpre[...]
    q_inv = inverse_rms(q_pre)
    dgain_q = jnp.sum(dq * (q_pre * q_inv), axis=0, keepdims=True)
    dqkv[:, 0:1024] = rms_back(q_pre, q_inv, dq * gain_row(gains, 1)).astype(BF16)
    dk_tiles, dv_tiles = [], []
    for t in range(4):
        even = dkvbuf[4 * t].astype(F32) + dkvbuf[4 * t + 1].astype(F32)
        odd = dkvbuf[4 * t + 2].astype(F32) + dkvbuf[4 * t + 3].astype(F32)
        tile = jnp.where(lo, even, pltpu.roll(odd, 64, 1))
        dk_tiles.append(tile * cos + swap_halves(tile) * sin)
        dv_tiles.append(jnp.where(lo, pltpu.roll(even, 64, 1), odd))
    dk = jnp.concatenate(dk_tiles, axis=1)
    k_pre = kpre[...]
    k_inv = inverse_rms(k_pre)
    dgain_k = jnp.sum(dk * (k_pre * k_inv), axis=0, keepdims=True)
    dqkv[:, 1024:1536] = rms_back(k_pre, k_inv, dk * key_gain_row(gains)).astype(BF16)
    dqkv[:, 1536:2048] = jnp.concatenate(dv_tiles, axis=1).astype(BF16)
    pair_copy_n = line_scatter_begin(lambda i: mm_tn(normed_t[i], dqkv[...]).astype(BF16), pair_n, mine_n, sib_n, sn, rn)

    shares_o = plane_sum_share(p_copies_o, pieces_o, 1, pin_o, res_o, sp2, rp2)

    def normed_back(t, _):
        dnorm[t] = mm_nt(dqkv[...], wall[t, :, 0:2048])
        return 0

    lax.fori_loop(0, 8, normed_back, 0)
    dnormed = jnp.concatenate([dnorm[t] for t in range(8)], axis=1)
    x_copies_n = line_scatter_send_x(mine_n, pair_copy_n, sib_n, inbox_n, sn, rn)
    values = tokens[...].astype(F32)
    inv = inverse_rms(values)
    dgain_in = jnp.sum(dnormed * (values * inv), axis=0, keepdims=True)
    gtok[...] = gtok[...] + rms_back(values, inv, dnormed * gain_row(gains, 0))
    for i in range(8):
        at = slice(128 * i, 128 * i + 128)
        smsend[i, 0:1, :] = dgain_in[:, at]
        smsend[i, 1:2, :] = dgain_q[:, at]
        smsend[i, 2:3, :] = dgain_mid[:, at]
        half = dgain_k[:, 128 * (i // 2) : 128 * (i // 2) + 128]
        smsend[i, 3:4, :] = half if i % 2 == 0 else pltpu.roll(jnp.broadcast_to(half, (8, 128)), 64, 1)[0:1]
        smsend[i, 4:6, :] = stats[0:2, :]
        smsend[i, 6:16, :] = jnp.zeros((10, 128), F32)
    sm_copies = []
    for o in range(1, 8):
        to = lax.rem(me + o, 8)
        copy = remote(smsend.at[to], sminbox.at[o], ssm.at[o], rsm.at[o], (to, c, d))
        copy.start()
        sm_copies.append(copy)

    for copy in own:
        copy.wait()
    for copy in a1 + b1:
        copy.wait_recv()

    def first_sums(m, _):
        sum_a[m] = (
            own_a[m].astype(F32) + in_a[0, m].astype(F32) + in_a[1, m].astype(F32) + in_a[2, m].astype(F32)
        ).astype(BF16)
        sum_b[m] = (
            own_b[m].astype(F32) + in_b[0, m].astype(F32) + in_b[1, m].astype(F32) + in_b[2, m].astype(F32)
        ).astype(BF16)
        return 0

    lax.fori_loop(0, 6, first_sums, 0)
    a2, b2 = [], []
    for o in (2, 1, 3):
        to = lax.rem(y + o, 4)
        a2.append(remote(sum_a.at[:, to], in2_a.at[o - 1], sa2.at[o], ra2.at[o], plane_device(to, z)))
        to = lax.rem(z + o, 4)
        b2.append(remote(
            sum_b.at[:, lax.div(to, 2), lax.rem(to, 2)], in2_b.at[o - 1], sb2.at[o], rb2.at[o], plane_device(y, to)
        ))
    for copy in a2 + b2:
        copy.start()

    total = smsend[me]
    for at, copy in enumerate(sm_copies):
        copy.wait_recv()
        total = total + sminbox[at + 1]
    smsum[...] = total
    small_copies = []
    for o in range(1, 16):
        _, device = plane_peer(o)
        copy = remote(smsum, small.at[o], sp5.at[o], rp5.at[o], device)
        copy.start()
        small_copies.append(copy)
    sum_n = line_scatter_sum(mine_n, sib_n, inbox_n, x_copies_n).astype(BF16)
    for t in range(16):
        for h in range(2):
            pieces_n[2 * t + h] = sum_n[64 * h : 64 * h + 64, 128 * t : 128 * t + 128]
    p_copies_n = plane_sum_send(pieces_n, 2, pin_n, sp3, rp3)
    for copy in shares_o:
        copy.wait_recv()
    for t in range(8):
        gout[:, 128 * t : 128 * t + 128] = jnp.concatenate([res_o[2 * t], res_o[2 * t + 1]], axis=0).astype(F32)
    shares_n = plane_sum_share(p_copies_n, pieces_n, 2, pin_n, res_n, sp4, rp4)
    for at, copy in enumerate(small_copies):
        copy.wait_recv()
        total = total + small[at + 1]
    gsmall[...] = total
    for copy in a2 + b2:
        copy.wait_recv()

    def second_sums(m, _):
        gw[m] = sum_a[m, y].astype(F32) + in2_a[0, m].astype(F32) + in2_a[1, m].astype(F32) + in2_a[2, m].astype(F32)
        gw[6 + m] = (
            sum_b[m, zh, zl].astype(F32) + in2_b[0, m].astype(F32) + in2_b[1, m].astype(F32) + in2_b[2, m].astype(F32)
        )
        return 0

    lax.fori_loop(0, 6, second_sums, 0)
    for copy in shares_n:
        copy.wait_recv()
    for t in range(16):
        tile = jnp.concatenate([res_n[2 * t], res_n[2 * t + 1]], axis=0).astype(F32)
        if t < 8:
            gq[:, 128 * t : 128 * t + 128] = tile
        elif t < 12:
            gk[:, 128 * (t - 8) : 128 * (t - 8) + 128] = tile
        else:
            gv[:, 128 * (t - 12) : 128 * (t - 12) + 128] = tile
    for copy in (
        a1 + b1 + a2 + b2 + d_copies + [pair_copy_o, pair_copy_n] + x_copies_o + x_copies_n + sm_copies
        + small_copies + p_copies_o + p_copies_n + shares_o + shares_n
    ):
        copy.wait_send()


def back(*args):
    vm = pl.BlockSpec(memory_space=pltpu.VMEM)
    hbm = pl.BlockSpec(memory_space=pl.ANY)
    sems = pltpu.SemaphoreType.DMA
    shape = jax.ShapeDtypeStruct
    return pl.pallas_call(
        back_kernel,
        out_shape=(
            shape((12, 64, 512), F32),
            shape((128, 1024), F32),
            shape((128, 1024), F32),
            shape((128, 512), F32),
            shape((128, 512), F32),
            shape((128, 1024), F32),
            shape((48, 128), F32),
        ),
        in_specs=[hbm, hbm] + [vm] * 21,
        out_specs=(vm,) * 7,
        scratch_shapes=[
            pltpu.VMEM((8, 128, 3072), BF16),
            pltpu.VMEM((6, 4, 64, 512), BF16),
            pltpu.VMEM((6, 2, 2, 64, 512), BF16),
            pltpu.VMEM((3, 6, 4, 64, 512), BF16),
            pltpu.VMEM((3, 6, 2, 2, 64, 512), BF16),
            pltpu.VMEM((6, 4, 64, 512), BF16),
            pltpu.VMEM((6, 2, 2, 64, 512), BF16),
            pltpu.VMEM((3, 6, 64, 512), BF16),
            pltpu.VMEM((3, 6, 64, 512), BF16),
            pltpu.VMEM((8, 128, 128), BF16),
            pltpu.VMEM((8, 128, 128), BF16),
            pltpu.VMEM((8, 256, 128), BF16),
            pltpu.VMEM((8, 256, 128), BF16),
            pltpu.VMEM((8, 256, 128), F32),
            pltpu.VMEM((8, 256, 128), F32),
            pltpu.VMEM((16, 128, 128), BF16),
            pltpu.VMEM((8, 128, 128), BF16),
            pltpu.VMEM((8, 128, 128), BF16),
            pltpu.VMEM((16, 128, 128), BF16),
            pltpu.VMEM((128, 2048), BF16),
            pltpu.VMEM((8, 128, 128), F32),
            pltpu.VMEM((64, 128), BF16),
            pltpu.VMEM((4, 128, 1024), BF16),
            pltpu.VMEM((4, 128, 1024), BF16),
            pltpu.VMEM((4, 128, 1024), BF16),
            pltpu.VMEM((3, 128, 1024), BF16),
            pltpu.VMEM((4, 128, 2048), BF16),
            pltpu.VMEM((4, 128, 2048), BF16),
            pltpu.VMEM((4, 128, 2048), BF16),
            pltpu.VMEM((3, 128, 2048), BF16),
            pltpu.VMEM((8, 48, 128), F32),
            pltpu.VMEM((8, 48, 128), F32),
            pltpu.VMEM((48, 128), F32),
            pltpu.VMEM((16, 48, 128), F32),
            pltpu.VMEM((16, 64, 128), BF16),
            pltpu.VMEM((16, 1, 64, 128), BF16),
            pltpu.VMEM((16, 64, 128), BF16),
            pltpu.VMEM((32, 64, 128), BF16),
            pltpu.VMEM((16, 2, 64, 128), BF16),
            pltpu.VMEM((32, 64, 128), BF16),
            sems(()), sems((2,)),
            sems((4,)), sems((4,)), sems((4,)), sems((4,)), sems((4,)), sems((4,)), sems((4,)), sems((4,)),
            sems((8,)), sems((8,)), sems((8,)), sems((8,)), sems((16,)), sems((16,)),
            sems((4,)), sems((4,)), sems((4,)), sems((4,)), sems((8,)), sems((8,)),
        ] + [sems((16,))] * 10,
        compiler_params=pltpu.CompilerParams(
            collective_id=2, has_side_effects=True, vmem_limit_bytes=60 << 20
        ),
        cost_estimate=pl.CostEstimate(flops=6 * 10**9, bytes_accessed=60 << 20, transcendentals=3 << 20),
        name="back",
    )(*args)


def per_device(
    tokens,
    norm_in,
    w_query,
    w_key,
    w_value,
    query_gain,
    key_gain,
    w_out,
    norm_mid,
    w_router,
    expert_gate,
    expert_up,
    expert_down,
    routes,
    valid,
    teacher,
):
    positions = (lax.axis_index("ctx") * 2 + lax.axis_index("dp")) * 128 + jnp.arange(128, dtype=jnp.int32)
    frequency = THETA ** (-(jnp.arange(HEAD // 2).astype(F32) * (2.0 / HEAD)))
    angles = positions.astype(F32)[:, None] * frequency[None, :]
    cos, sin = jnp.cos(angles), jnp.sin(angles)
    cosine = jnp.concatenate([cos, cos, cos, cos], axis=1)
    sine = jnp.concatenate([-sin, sin, -sin, sin], axis=1)
    rows = jnp.stack([norm_in, query_gain, norm_mid, jnp.concatenate([key_gain, key_gain])])
    small = jnp.concatenate([rows, jnp.zeros((12, 128), BF16), w_router.T], axis=0)
    ew = jnp.concatenate([jnp.transpose(w, (1, 0, 2)) for w in (expert_gate, expert_up, expert_down)], axis=0)
    valid_rows = jnp.broadcast_to(valid.astype(F32)[None, :], (8, 128))
    (
        wg, wall, small_all, vbuf, kvbuf, qbuf, oheads, lse, att, residual, normed_t, qpre, kpre, xall, meta, probs, picks
    ) = front(tokens, w_query, w_key, w_value, w_out, small, ew, valid_rows, cosine, sine, routes.T)
    mixed, err, stats, dw, dmid, dgates = moe(
        wg.reshape(12, 1024, 512), xall, meta, residual, teacher, valid_rows
    )
    gw, gtok, gq, gk, gv, gout, gsmall = back(
        dw.reshape(12, 2, 4, 2, 64, 512), wall, small_all, vbuf, kvbuf, qbuf, oheads, lse, att, residual, normed_t,
        qpre, kpre, xall, probs, picks, err, stats, dmid, dgates, tokens, cosine, sine,
    )
    loss = gsmall[4, 0] / (gsmall[5, 0] * 1024.0)
    grad_gate, grad_up, grad_down = [jnp.transpose(gw[4 * m : 4 * m + 4], (1, 0, 2)) for m in range(3)]
    return (
        mixed, loss, gtok, gsmall[0], gq, gk, gv, gsmall[1], gsmall[3, :64], gout, gsmall[2], gsmall[16:48].T,
        grad_gate, grad_up, grad_down,
    )


def solution(mesh):
    placed = (
        P(("expert", "ctx", "dp"), None),
        P("expert"),
        P("expert", None),
        P("expert", None),
        P("expert", None),
        P("expert"),
        P("expert"),
        P("expert", None),
        P("expert"),
        P("expert", None),
        P(("ctx", "dp"), "expert", None),
        P(("ctx", "dp"), "expert", None),
        P(("ctx", "dp"), "expert", None),
        P(("expert", "ctx", "dp"), None),
        P(("expert", "ctx", "dp")),
        P(("expert", "ctx", "dp"), None),
    )
    return jax.shard_map(
        per_device,
        mesh=mesh,
        in_specs=placed,
        out_specs=(
            P(("expert", "ctx", "dp"), None),
            P(),
            P(("expert", "ctx", "dp"), None),
            P("expert"),
            P("expert", None),
            P("expert", None),
            P("expert", None),
            P("expert"),
            P("expert"),
            P("expert", None),
            P("expert"),
            P("expert", None),
            P(("ctx", "dp"), "expert", None),
            P(("ctx", "dp"), "expert", None),
            P(("ctx", "dp"), "expert", None),
        ),
        check_vma=False,
    )
```

time: 1440 us -> 434 us (0.30)
  waiting for transfers between devices: 642 us -> 0 us
  Pallas kernels: 0 us -> 394 us
  blocking collectives: 388 us -> 0 us
  matrix products: 128 us -> 0 us
  local copies, waits for them, and re-layouts: 152 us -> 32.8 us
  other arithmetic: 72.2 us -> 2.04 us
  between operations: 21 us -> 3.3 us
  starting transfers between devices: 14.6 us -> 0 us
    pallas_call x0 -> x3, Pallas kernels: none -> 394 us  [the longest x1 171 us: back(): pl.pallas_call(back_kernel, out_shape=(shape((12, 64, 512), F32), shape((...]
    all_gather x9 -> x0, waiting for transfers between devices: 292 us -> none  [the longest x1 91.5 us: per_device(): lax.all_gather(expert_up, ('ctx', 'dp'), axis=0, tiled=True)]
    reduce_scatter x6 -> x0, waiting for transfers between devices: 228 us -> none  [the longest x1 77 us: per_device(): lax.psum_scatter(d_values_all.reshape(seq_len, kv_width).astype(jnp.bfloa...]
    psum x2 -> x0, blocking collectives: 129 us -> none  [the longest x1 69.5 us: per_device(): lax.psum((jnp.sum(err * err), jnp.sum(valid.astype(jnp.float32))), ('expe...]
    dot_general x52 -> x0, matrix products: 128 us -> none  [the longest x8 14.3 us: block_scores(): jnp.einsum('tkgd,skd->kgts', query_grouped, keys_part, preferred_element_...]
    all_gather x5 -> x0, blocking collectives: 123 us -> none  [the longest x1 54.6 us: per_device(): lax.all_gather(w_router, 'expert', axis=0, tiled=True)]
    all_to_all x2 -> x0, blocking collectives: 111 us -> none  [the longest x1 58.2 us: per_device(): lax.all_to_all(send_rows, 'expert', split_axis=0, concat_axis=2, tiled=True)]
    psum x1 -> x0, waiting for transfers between devices: 73.9 us -> none  [per_device(): lax.psum(grads[1].astype(jnp.bfloat16), ('ctx', 'dp')).astype(jnp.float32)]
  transfers between devices with their start and end apart: 19 -> 0, of which waited for: 14 -> 0; matrix products, arithmetic and copies ran while one was open for 14% -> 0% of each run, Pallas kernels for 0% -> 0%
where the time goes in v1:
time: 434 us; the launch traced here: 432 us
  Pallas kernels  394 us (91%)
  local copies, waits for them, and re-layouts  32.8 us (8%)
    pallas_call x1, Pallas kernels, back(): pl.pallas_call(back_kernel, out_shape=(shape((12, 64, 512), F32), shape((...  171 us
    pallas_call x1, Pallas kernels, front(): pl.pallas_call(front_kernel, out_shape=(shape((12, 2, 4, 2, 64, 512), BF1...  146 us
    pallas_call x1, Pallas kernels, moe(): pl.pallas_call(moe_kernel, out_shape=(jax.ShapeDtypeStruct((128, 1024), B...  76.7 us
    unnamed x66, local copies, waits for them, and re-layouts  23.4 us

profile of v1, /device:TPU:1, one launch (start us, length us, event | category | flops | bytes accessed | tf_op | source)
XLA Modules:
  0.0 431.8 jit_solution(13837025641324144753)
XLA Ops:
  0.7 0.8 maximum_bitcast_fusion
  2.2 1.5 concatenate.16.small
  4.2 1.0 copy.47
  5.2 1.1 copy_bitcast_fusion
  6.5 0.9 copy-done.4
  7.4 0.9 copy-done.16
  8.4 0.9 copy-done.17
  9.3 0.9 copy-done.18
  10.2 0.9 copy-done.19
  11.8 145.7 %front.1 = (bf16[12,2,4,2,64,512]{5,4,3,2,1,0:T(8,128)(2,1)}, bf16[8,128,3072]{2,1,0:T(8,128)(2,1)}, bf16[8,48,128]{2,1,0:T(8,128)(2,1)S(1)}, f32[16,8,128]{2,1,...) custom-call(bf16[128,1024]{1,0:T(8,128)(2,1)S(1)} %copy-done.4, ...), custom_call_target="tpu_custom_call" | custom-call | flops 3000000000 | bytes 31457280 | tf_op jit(solution)/shard_map/front/pallas_call | solution.py:597
  157.5 0.8 copy-done
  158.3 0.8 copy-done.1
  159.1 0.8 copy-done.2
  159.9 0.8 copy-done.3
  160.7 0.7 copy-done.5
  161.4 0.7 copy-done.6
  166.6 76.7 %moe.1 = (bf16[128,1024]{1,0:T(8,128)(2,1)}, f32[128,1024]{1,0:T(8,128)}, f32[8,128]{1,0:T(8,128)}, bf16[12,1024,512]{2,1,0:T(8,128)(2,1)}, f32[128,1024]{1,0:T(8,128)}, /*index=5*/f32[8,8,128]{2,1,0:T(8,128)}) custom-call(bf16[12,1024,512]{2,1,0:T(8,128)(2,1)} %bitcast.40, bf16[8,128,1024]{2,1,0:T(8,128)(2,1)} %get-tuple-element.46.xall, ...), custom_call_target="tpu_custom_call" | custom-call | flops 22000001024 | bytes 31457280 | tf_op jit(solution)/shard_map/moe/pallas_call | solution.py:267
  243.3 171.3 %back.1 = (f32[12,64,512]{2,1,0:T(8,128)}, f32[128,1024]{1,0:T(8,128)}, f32[128,1024]{1,0:T(8,128)}, f32[128,512]{1,0:T(8,128)}, f32[128,512]{1,0:T(8,128)}, /*index=5*/f32[128,1024]{1,0:T(8,128)}, f32[48,128]{1,0:T(8,128)}) custom-call(bf16[12,2,4,2,64,512]{5,4,3,2,1,0:T(8,128)(2,1)} %bitcast.34, bf16[8,128,3072]{2,1,0:T(8,128)(2,1)} %get-tuple-element.51.wall_hbm, ...), custom_call_target="tpu_custom_call" | custom-call | flops 6000000000 | bytes 62914560 | tf_op jit(solution)/shard_map/back/pallas_call | solution.py:992
  414.7 1.3 slice_bitcast_fusion.5
  416.0 1.3 fusion.1
  418.6 1.3 slice_bitcast_fusion.4
  419.9 1.3 slice_bitcast_fusion.3
  421.2 1.6 slice_bitcast_fusion
  422.8 1.1 copy.43
  423.9 1.1 copy.42
  425.1 1.1 copy.41
  426.2 0.7 copy.54
  426.9 0.8 copy.55
  427.7 0.8 copy.56
  428.5 0.7 copy.57
  429.2 0.7 copy.58
  429.9 0.8 copy.59
  (53 shorter events, 6.5 us)
Async XLA Ops:
  2.1 155.4 %copy-start.15 = (f32[8,128]{1,0:T(8,128)}, f32[8,128]{1,0:T(8,128)S(1)}, u32[]{:S(2)}) copy-start(f32[8,128]{1,0:T(8,128)S(1)} %broadcast_in_dim.5.valid.valid_row) | copy-start | bytes 12292
  4.2 153.3 %copy-start.9 = (f32[128,128]{1,0:T(8,128)}, f32[128,128]{1,0:T(8,128)S(1)}, u32[]{:S(2)}) copy-start(f32[128,128]{1,0:T(8,128)S(1)} %get-tuple-element.118.cosine) | copy-start | bytes 196612
  4.2 153.3 %copy-start.10 = (f32[128,128]{1,0:T(8,128)}, f32[128,128]{1,0:T(8,128)S(1)}, u32[]{:S(2)}) copy-start(f32[128,128]{1,0:T(8,128)S(1)} %get-tuple-element.119.sine) | copy-start | bytes 196612
  6.5 1.0 copy-start.4
  7.4 0.9 copy-start.16
  8.4 0.9 copy-start.17
  9.3 0.9 copy-start.18
  10.2 0.9 copy-start.19
  11.1 0.7 copy-start.20
  157.5 0.8 copy-start
  158.3 0.8 copy-start.1
  159.1 0.8 copy-start.2
  159.9 0.8 copy-start.3
  160.7 0.7 copy-start.5
  161.4 0.7 copy-start.6
  162.1 0.7 copy-start.7
  162.8 0.7 copy-start.8
  163.5 0.6 copy-start.11
  164.1 0.6 copy-start.12
  164.8 0.6 copy-start.13
  165.4 0.6 copy-start.14
  166.0 0.6 copy-start.21
  414.6 11.6 %copy-start.25 = (bf16[128,1024]{1,0:T(8,128)(2,1)S(1)}, bf16[128,1024]{1,0:T(8,128)(2,1)}, u32[]{:S(2)}) copy-start(bf16[128,1024]{1,0:T(8,128)(2,1)} %get-tuple-element.135) | copy-start | bytes 786436
  414.6 12.3 %copy-start.24 = (f32[128,1024]{1,0:T(8,128)S(1)}, f32[128,1024]{1,0:T(8,128)}, u32[]{:S(2)}) copy-start(f32[128,1024]{1,0:T(8,128)} %get-tuple-element.137) | copy-start | bytes 1572868
  414.6 13.0 %copy-start.23 = (f32[128,1024]{1,0:T(8,128)S(1)}, f32[128,1024]{1,0:T(8,128)}, u32[]{:S(2)}) copy-start(f32[128,1024]{1,0:T(8,128)} %get-tuple-element.139) | copy-start | bytes 1572868
  414.7 13.8 %copy-start.27 = (f32[128,512]{1,0:T(8,128)S(1)}, f32[128,512]{1,0:T(8,128)}, u32[]{:S(2)}) copy-start(f32[128,512]{1,0:T(8,128)} %get-tuple-element.140) | copy-start | bytes 786436
  414.7 14.5 %copy-start.26 = (f32[128,512]{1,0:T(8,128)S(1)}, f32[128,512]{1,0:T(8,128)}, u32[]{:S(2)}) copy-start(f32[128,512]{1,0:T(8,128)} %get-tuple-element.141) | copy-start | bytes 786436
  414.7 15.2 %copy-start.22 = (f32[128,1024]{1,0:T(8,128)S(1)}, f32[128,1024]{1,0:T(8,128)}, u32[]{:S(2)}) copy-start(f32[128,1024]{1,0:T(8,128)} %get-tuple-element.144) | copy-start | bytes 1572868

commit v2 on v1

--- a/solution.py
+++ b/solution.py
@@ -119,6 +119,7 @@
     loads = [pltpu.make_async_copy(wg_hbm.at[m], wg.at[m], load_sem.at[m]) for m in range(12)]
     for m in (0, 4, 8, 1, 5, 9, 2, 6, 10, 3, 7, 11):
         loads[m].start()
+
     greet_line()
 
     slot_ids = lax.broadcasted_iota(jnp.int32, (64, 128), 0).astype(F32)
@@ -135,6 +136,7 @@
         return 0
 
     lax.fori_loop(0, 8, compact, 0)
+
     for copy in loads:
         copy.wait()
 
@@ -168,9 +170,11 @@
         lax.fori_loop(0, 4, one, 0)
 
     combine(mine1, pair1)
+
     pair_copy = line_scatter_send_pair(pair1, sib1, s1, r1)
     x_copies = line_scatter_send_x(mine1, pair_copy, sib1, inbox1, s1, r1)
     out = residual[...] + line_scatter_sum(mine1, sib1, inbox1, x_copies)
+
     mixed[...] = out.astype(BF16)
     eye = lax.broadcasted_iota(jnp.int32, (128, 128), 0) == lax.broadcasted_iota(jnp.int32, (128, 128), 1)
     valid_col = jnp.sum(jnp.where(eye, valid_row[0:1, :], 0.0), axis=1, keepdims=True)
@@ -184,6 +188,7 @@
     stats[0:1, :] = jnp.broadcast_to(square, (1, 128))
     stats[1:2, :] = jnp.broadcast_to(count, (1, 128))
     stats[2:8, :] = jnp.zeros((6, 128), F32)
+
     line_gather_finish(gather, lambda i: dall.at[i], s2, r2)
 
     def spread(s, _):
@@ -214,6 +219,7 @@
         return 0
 
     lax.fori_loop(0, 4, backward, 0)
+
     combine(mine2, pair2)
     pair_copy2 = line_scatter_send_pair(pair2, sib2, s3, r3)
 
@@ -251,6 +257,7 @@
         return 0
 
     lax.fori_loop(0, 4, weight_grads, 0)
+
     dmid[...] = line_scatter_sum(mine2, sib2, inbox2, x_copies2)
     for copy in gate_copies:
         copy.wait()
@@ -386,11 +393,75 @@
     return jnp.concatenate([jnp.where(keep, first, 0.0), jnp.where(keep, second, 0.0)], axis=0)
 
 
+class PlaneGather:
+    def __init__(self, ew, wg, send, recv):
+        self.ew, self.wg, self.send, self.recv = ew, wg, send, recv
+        self.y, self.z = yz()
+        self.copies = {}
+
+    def go(self, n, src, dst, device):
+        copy = remote(src, dst, self.send.at[n], self.recv.at[n], device)
+        copy.start()
+        self.copies[n] = copy
+
+    def place(self, m, y, z):
+        return self.wg.at[m, lax.div(z, 2), y, lax.rem(z, 2)]
+
+    def shards(self):
+        y, z = self.y, self.z
+        a, b = pl.ds(0, 6), pl.ds(6, 6)
+        for i, o in enumerate((1, 3)):
+            self.go(i, self.ew.at[a], self.place(a, y, z), plane_device(lax.rem(y + o, 4), z))
+            self.go(2 + i, self.ew.at[b], self.place(b, y, z), plane_device(y, lax.rem(z + o, 4)))
+
+    def shards_on(self):
+        y, z = self.y, self.z
+        a, b = pl.ds(0, 6), pl.ds(6, 6)
+        for i, o in enumerate((1, 3)):
+            rows = pl.ds(32 * i, 32)
+            self.copies[i].wait_recv()
+            view = self.place(a, lax.rem(y - o + 4, 4), z).at[:, rows]
+            self.go(4 + i, view, view, plane_device(lax.rem(y + o, 4), z))
+            self.copies[2 + i].wait_recv()
+            view = self.place(b, y, lax.rem(z - o + 4, 4)).at[:, rows]
+            self.go(6 + i, view, view, plane_device(y, lax.rem(z + o, 4)))
+
+    def shards_wait(self):
+        for n in range(4, 8):
+            self.copies[n].wait_recv()
+
+    def lines(self, j):
+        y, z = self.y, self.z
+        for i, o in enumerate((1, 3)):
+            view = self.wg.at[j, lax.div(z, 2), :, lax.rem(z, 2)]
+            self.go(8 + 8 * j + i, view, view, plane_device(y, lax.rem(z + o, 4)))
+            view = self.wg.at[6 + j, :, y]
+            self.go(10 + 8 * j + i, view, view, plane_device(lax.rem(y + o, 4), z))
+
+    def lines_on(self, j):
+        y, z = self.y, self.z
+        for i, o in enumerate((1, 3)):
+            self.copies[8 + 8 * j + i].wait_recv()
+            from_z = lax.rem(z - o + 4, 4)
+            view = self.wg.at[j, lax.div(from_z, 2), pl.ds(2 * i, 2), lax.rem(from_z, 2)]
+            self.go(12 + 8 * j + i, view, view, plane_device(y, lax.rem(z + o, 4)))
+            self.copies[10 + 8 * j + i].wait_recv()
+            view = self.wg.at[6 + j, i, lax.rem(y - o + 4, 4)]
+            self.go(14 + 8 * j + i, view, view, plane_device(lax.rem(y + o, 4), z))
+
+    def finish(self):
+        for j in range(6):
+            for n in range(12 + 8 * j, 16 + 8 * j):
+                self.copies[n].wait_recv()
+        for copy in self.copies.values():
+            copy.wait_send()
+
+
 def front_kernel(
     tokens, wq, wk, wv, wo, small, ew, valid, cosine, sine, routes,
-    wg, wall_out, small_all, vbuf, kvbuf, qbuf, oheads, lse, att, residual, normed_t, qpre, kpre, xall, meta, probs_out, picks_out,
+    wg, wall_out, small_all, vbuf, kvbuf, qbuf, oheads, lse, att, residual, normed_t, qpre, kpre, xall, meta, probs_out, picks_out, nx, attx,
     wall, sendkv, sendq, osend, low, metasend,
-    own_sem, ew_sem, wall_sem, ssm, rsm, sqkv, rqkv, swo, rwo, sv, rv, sa1, ra1, sb1, rb1, sa2, ra2, sb2, rb2,
+    own_sem, ew_sem, wall_sem, ssm, rsm, sqkv, rqkv, swo, rwo, sv, rv, sew, rew, snx, rnx, sax, rax,
     skv, rkv, sq, rq, so, ro, sx, rx, sm, rm,
 ):
     x, core, c, d = places()
@@ -414,17 +485,8 @@
     greet_all()
 
     small_gather = line_gather_start(small, lambda i: small_all.at[i], ssm, rsm)
-    ew_a, ew_b = ew.at[pl.ds(0, 6)], ew.at[pl.ds(6, 6)]
-    a1 = [
-        remote(ew_a, wg.at[pl.ds(0, 6), zh, y, zl], sa1.at[o], ra1.at[o], plane_device(lax.rem(y + o, 4), z))
-        for o in (2, 1, 3)
-    ]
-    b1 = [
-        remote(ew_b, wg.at[pl.ds(6, 6), zh, y, zl], sb1.at[o], rb1.at[o], plane_device(y, lax.rem(z + o, 4)))
-        for o in (2, 1, 3)
-    ]
-    for copy in a1 + b1:
-        copy.start()
+    bulk = PlaneGather(ew, wg, sew, rew)
+    bulk.shards()
     for copy in own[:3]:
         copy.wait()
     qkv_gather = line_gather_start(
@@ -448,19 +510,21 @@
     for t in range(8):
         normed_t[t] = normed[:, 128 * t : 128 * t + 128]
 
+    nx[me] = normed_t[me]
+    nx_copies = []
+    for o in range(1, 8):
+        to = lax.rem(me + o, 8)
+        copy = remote(normed_t.at[to], nx.at[me], snx.at[o], rnx.at[o], (to, c, d))
+        copy.start()
+        nx_copies.append(copy)
+    bulk.shards_on()
     own_ew.wait()
-    for copy in a1 + b1:
-        copy.wait_recv()
-    a2, b2 = [], []
-    for o in (2, 1, 3):
-        view = wg.at[pl.ds(0, 6), zh, :, zl]
-        a2.append(remote(view, view, sa2.at[o], ra2.at[o], plane_device(y, lax.rem(z + o, 4))))
-        view = wg.at[pl.ds(6, 6), :, y, :]
-        b2.append(remote(view, view, sb2.at[o], rb2.at[o], plane_device(lax.rem(y + o, 4), z)))
-    for copy in a2 + b2:
-        copy.start()
-
+    bulk.shards_wait()
+    for j in range(2):
+        bulk.lines(j)
     line_gather_finish(qkv_gather, lambda i: wall.at[i, :, pl.ds(0, 2048)], sqkv, rqkv)
+    for j in range(2):
+        bulk.lines_on(j)
     q_pre = mm(normed, wall[:, :, 0:1024].reshape(1024, 1024))
     k_pre = mm(normed, wall[:, :, 1024:1536].reshape(1024, 512))
     v_low = mm(normed, wall[:, :, 1536:2048].reshape(1024, 512)).astype(BF16).astype(F32)
@@ -497,6 +561,8 @@
     for copy in valid_copies + kv_copies + q_copies:
         copy.wait_recv()
 
+    bulk.lines(2)
+
     def chunk(i, _):
         b = lax.rem(c + 1 + i, 8)
         queries = (stack_heads(qbuf[b].astype(F32), False) * (HEAD**-0.5)).astype(BF16)
@@ -536,7 +602,9 @@
 
         return 0
 
-    lax.fori_loop(0, 8, chunk, 0)
+    lax.fori_loop(0, 4, chunk, 0)
+    bulk.lines_on(2)
+    lax.fori_loop(4, 8, chunk, 0)
     line_gather_finish(out_gather, lambda i: wall.at[i, :, pl.ds(2048, 1024)], swo, rwo)
     store = pltpu.make_async_copy(wall, wall_out, wall_sem)
     store.start()
@@ -549,6 +617,14 @@
         return 0
 
     lax.fori_loop(0, 7, wait_rest, 0)
+    for j in range(3, 6):
+        bulk.lines(j)
+    attx[me] = att[me]
+    for o in range(1, 8):
+        to = lax.rem(me + o, 8)
+        copy = remote(att.at[to], attx.at[me], sax.at[o], rax.at[o], (to, c, d))
+        copy.start()
+        nx_copies.append(copy)
     attended = jnp.concatenate([att[t] for t in range(8)], axis=1)
     res = tokens[...].astype(F32) + mm(attended, wall[:, :, 2048:3072].reshape(1024, 1024))
     residual[...] = res
@@ -579,12 +655,16 @@
         copy = remote(metasend.at[to], meta.at[me], sm.at[o], rm.at[o], (to, c, d))
         copy.start()
         meta_copies.append(copy)
+    bulk.lines_on(3)
     line_gather_finish(mid_gather, lambda i: xall.at[i], sx, rx)
     for copy in meta_copies:
         copy.wait()
-    for copy in a2 + b2:
+    bulk.lines_on(4)
+    bulk.lines_on(5)
+    bulk.finish()
+    for copy in nx_copies:
         copy.wait()
-    for copy in a1 + b1 + valid_copies + kv_copies + q_copies:
+    for copy in valid_copies + kv_copies + q_copies:
         copy.wait_send()
     store.wait()
 
@@ -614,9 +694,11 @@
             shape((8, 8, 128), F32),
             shape((32, 128), F32),
             shape((32, 128), F32),
+            shape((8, 128, 128), BF16),
+            shape((8, 128, 128), BF16),
         ),
         in_specs=[vm, hbm, hbm, hbm, hbm, vm, hbm, vm, vm, vm, vm],
-        out_specs=(hbm, hbm) + (vm,) * 15,
+        out_specs=(hbm, hbm) + (vm,) * 17,
         scratch_shapes=[
             pltpu.VMEM((8, 128, 3072), BF16),
             pltpu.VMEM((8, 128, 128), BF16),
@@ -627,7 +709,7 @@
             sems((4,)), sems(()), sems(()),
             sems((8,)), sems((8,)), sems((8,)), sems((8,)), sems((8,)), sems((8,)),
             sems((16,)), sems((16,)),
-            sems((4,)), sems((4,)), sems((4,)), sems((4,)), sems((4,)), sems((4,)), sems((4,)), sems((4,)),
+            sems((56,)), sems((56,)), sems((8,)), sems((8,)), sems((8,)), sems((8,)),
             sems((16,)), sems((16,)),
             sems((8,)), sems((8,)), sems((8,)), sems((8,)), sems((8,)), sems((8,)), sems((8,)), sems((8,)),
         ],
@@ -637,23 +719,6 @@
         cost_estimate=pl.CostEstimate(flops=3 * 10**9, bytes_accessed=30 << 20, transcendentals=3 << 20),
         name="front",
     )(tokens, wq, wk, wv, wo, small, ew, valid, cosine, sine, routes)
-
-
-def line_scatter_begin(parts_of, pair, mine, sib, send, recv):
-    x, core, _, _ = places()
-
-    def one(k, _):
-        pair[k] = parts_of(k * 2 + 1 - core)
-        return 0
-
-    def other(k, _):
-        mine[k] = parts_of(k * 2 + core)
-        return 0
-
-    lax.fori_loop(0, 4, one, 0)
-    copy = line_scatter_send_pair(pair, sib, send, recv)
-    lax.fori_loop(0, 4, other, 0)
-    return copy
 
 
 def plane_peer(o):
@@ -694,15 +759,136 @@
     return inverse * (grad - hat * jnp.mean(grad * hat, axis=1, keepdims=True))
 
 
+class PlaneScatter:
+    def __init__(self, dw, own, near, far_in, near_in, far2_in, near2_in, load, send, recv):
+        self.dw, self.own, self.near, self.far_in, self.near_in = dw, own, near, far_in, near_in
+        self.far2_in, self.near2_in, self.load, self.send, self.recv = far2_in, near2_in, load, send, recv
+        self.y, self.z = yz()
+        self.copies = {}
+        self.loads = []
+
+    def go(self, n, src, dst, device):
+        copy = remote(src, dst, self.send.at[n], self.recv.at[n], device)
+        copy.start()
+        self.copies[n] = copy
+
+    def block(self, half, m, at):
+        if half == 0:
+            return self.dw.at[m, lax.div(at, 2), :, lax.rem(at, 2)]
+        return self.dw.at[6 + m, :, at]
+
+    def all_blocks(self, half, at):
+        if half == 0:
+            return self.dw.at[pl.ds(0, 6), lax.div(at, 2), :, lax.rem(at, 2)]
+        return self.dw.at[pl.ds(6, 6), :, at]
+
+    def due(self, half, m, at):
+        if half == 0:
+            return self.own[0].at[m, at]
+        return self.own[1].at[m, lax.div(at, 2), lax.rem(at, 2)]
+
+    def device(self, half, at):
+        return plane_device(self.y, at) if half == 0 else plane_device(at, self.z)
+
+    def place(self, half):
+        return self.z if half == 0 else self.y
+
+    def loads_start(self):
+        for half in range(2):
+            me = self.place(half)
+            spots = [(self.own[half], me)] + [(self.near[half].at[i], lax.rem(me + o, 4)) for i, o in enumerate((1, 3))]
+            for n, (ref, at) in enumerate(spots):
+                copy = pltpu.make_async_copy(self.all_blocks(half, at), ref, self.load.at[3 * half + n])
+                copy.start()
+                self.loads.append(copy)
+
+    def far(self, j):
+        for half in range(2):
+            me = self.place(half)
+            far = lax.rem(me + 2, 4)
+            for i, o in enumerate((1, 3)):
+                view = self.block(half, j, far)
+                view = view.at[pl.ds(2 * i, 2)] if half == 0 else view.at[i]
+                dst = self.far_in.at[half, i, j]
+                self.go(8 * j + 2 * half + i, view, dst, self.device(half, lax.rem(me + o, 4)))
+
+    def near_out(self, j):
+        for half in range(2):
+            me = self.place(half)
+            for i, o in enumerate((1, 3)):
+                self.copies[8 * j + 2 * half + i].wait_recv()
+                part = self.near[0].at[i, j, pl.ds(2 * i, 2)] if half == 0 else self.near[1].at[i, j, i]
+                part[...] = (part[...].astype(F32) + self.far_in[half, i, j].astype(F32)).astype(BF16)
+                self.go(
+                    8 * j + 4 + 2 * half + i, self.near[half].at[i, j], self.near_in[half].at[i, j],
+                    self.device(half, lax.rem(me + o, 4)),
+                )
+
+    def near_sum(self, j):
+        for half in range(2):
+            for i in range(2):
+                self.copies[8 * j + 4 + 2 * half + i].wait_recv()
+            own, near_in = self.own[half], self.near_in[half]
+            own[j] = (own[j].astype(F32) + near_in[0, j].astype(F32) + near_in[1, j].astype(F32)).astype(BF16)
+
+    def place2(self, half):
+        return self.y if half == 0 else self.z
+
+    def device2(self, half, at):
+        return plane_device(at, self.z) if half == 0 else plane_device(self.y, at)
+
+    def far2(self):
+        for half in range(2):
+            me = self.place2(half)
+            for i, o in enumerate((1, 3)):
+                view = self.due(half, pl.ds(0, 6), lax.rem(me + 2, 4)).at[:, pl.ds(32 * i, 32)]
+                self.go(48 + 2 * half + i, view, self.far2_in.at[half, i], self.device2(half, lax.rem(me + o, 4)))
+
+    def near2(self):
+        for half in range(2):
+            me = self.place2(half)
+            for i, o in enumerate((1, 3)):
+                self.copies[48 + 2 * half + i].wait_recv()
+                to = lax.rem(me + o, 4)
+
+                def add(m, _):
+                    part = self.due(half, m, to).at[pl.ds(32 * i, 32)]
+                    part[...] = (part[...].astype(F32) + self.far2_in[half, i, m].astype(F32)).astype(BF16)
+                    return 0
+
+                lax.fori_loop(0, 6, add, 0)
+                self.go(52 + 2 * half + i, self.due(half, pl.ds(0, 6), to), self.near2_in.at[half, i], self.device2(half, to))
+
+    def finish(self, result):
+        for half in range(2):
+            me = self.place2(half)
+            for i in range(2):
+                self.copies[52 + 2 * half + i].wait_recv()
+
+            def add(m, _):
+                result[6 * half + m] = (
+                    self.due(half, m, me)[...].astype(F32)
+                    + self.near2_in[half, 0, m].astype(F32)
+                    + self.near2_in[half, 1, m].astype(F32)
+                )
+                return 0
+
+            lax.fori_loop(0, 6, add, 0)
+
+    def drain(self):
+        for copy in self.copies.values():
+            copy.wait_send()
+
+
 def back_kernel(
     dw, wall_hbm, small_in, vbuf, kvbuf, qbuf, oheads, lse, att, residual, normed_t, qpre, kpre, xall,
-    probs_in, picks_in, err, stats, dmid_in, dgates, tokens, cosine, sine,
+    probs_in, picks_in, nx, attx, err, stats, dmid_in, dgates, tokens, cosine, sine,
     gw, gtok, gq, gk, gv, gout, gsmall,
-    wall, own_a, own_b, in_a, in_b, sum_a, sum_b, in2_a, in2_b,
+    wall, own_a, own_b, near_a, near_b, wfar_in, near_in_a, near_in_b, wfar2_in, wnear2_in,
     dsend, dattbuf, qpad, dop, delta, dqacc, dkvsend, dqsend, dqbuf, dkvbuf, dqkv, dnorm, dlog,
-    pair_o, mine_o, sib_o, inbox_o, pair_n, mine_n, sib_n, inbox_n, smsend, sminbox, smsum, small,
+    dball, dqall, low, smsend, sminbox, smsum, small,
     pieces_o, pin_o, res_o, pieces_n, pin_n, res_n,
-    wall_sem, own_sem, sa1, ra1, sb1, rb1, sa2, ra2, sb2, rb2, sd, rd, sdq, rdq, sdkv, rdkv,
+    wall_sem, wload, sw, rw, sd, rd, sdq, rdq, sdkv, rdkv,
     so, ro, sn, rn, ssm, rsm, sp1, rp1, sp2, rp2, sp3, rp3, sp4, rp4, sp5, rp5,
 ):
     x, core, c, d = places()
@@ -713,23 +899,13 @@
     e = lax.axis_index("expert")
     wall_load = pltpu.make_async_copy(wall_hbm, wall, wall_sem)
     wall_load.start()
-    own = [
-        pltpu.make_async_copy(dw.at[pl.ds(0, 6), zh, :, zl], own_a, own_sem.at[0]),
-        pltpu.make_async_copy(dw.at[pl.ds(6, 6), :, y, :], own_b, own_sem.at[1]),
-    ]
-    for copy in own:
-        copy.start()
+    bulk = PlaneScatter(
+        dw, (own_a, own_b), (near_a, near_b), wfar_in, (near_in_a, near_in_b), wfar2_in, wnear2_in, wload, sw, rw
+    )
+    bulk.loads_start()
     greet_all()
-    a1, b1 = [], []
-    for o in (2, 1, 3):
-        to = lax.rem(z + o, 4)
-        a1.append(remote(
-            dw.at[pl.ds(0, 6), lax.div(to, 2), :, lax.rem(to, 2)], in_a.at[o - 1], sa1.at[o], ra1.at[o], plane_device(y, to)
-        ))
-        to = lax.rem(y + o, 4)
-        b1.append(remote(dw.at[pl.ds(6, 6), :, to, :], in_b.at[o - 1], sb1.at[o], rb1.at[o], plane_device(to, z)))
-    for copy in a1 + b1:
-        copy.start()
+    for j in range(2):
+        bulk.far(j)
 
     gains = small_in[...].astype(F32)
     lo = low_lanes()
@@ -759,6 +935,9 @@
     gtok[...] = dres
     wall_load.wait()
     dqkv[:, 0:1024] = dbranch
+    low[...] = dbranch
+    dball[me] = dbranch
+    branch_gather = line_gather_start(low, lambda i: dball.at[i], so, ro)
 
     def attended_back(t, _):
         dsend[t] = mm_nt(dqkv[:, 0:1024], wall[t, :, 2048:3072]).astype(BF16)
@@ -772,16 +951,21 @@
         copy = remote(dsend.at[to], dattbuf.at[c], sd.at[o], rd.at[o], (e, to, d))
         copy.start()
         d_copies.append(copy)
-    pair_copy_o = line_scatter_begin(lambda i: mm_tn(att[i], dqkv[:, 0:1024]).astype(BF16), pair_o, mine_o, sib_o, so, ro)
 
     def prepare(b, _):
         qpad[b] = (stack_heads(qbuf[b].astype(F32), False) * (HEAD**-0.5)).astype(BF16)
         return 0
 
     lax.fori_loop(0, 8, prepare, 0)
-    x_copies_o = line_scatter_send_x(mine_o, pair_copy_o, sib_o, inbox_o, so, ro)
     for copy in d_copies:
         copy.wait_recv()
+
+    for copy in bulk.loads:
+        copy.wait()
+    for j in range(2, 4):
+        bulk.far(j)
+    for j in range(2):
+        bulk.near_out(j)
 
     def prepare_back(b, _):
         tile = dattbuf[b].astype(F32)
@@ -829,12 +1013,7 @@
         return 0
 
     lax.fori_loop(0, 8, key_block, 0)
-
-    sum_o = line_scatter_sum(mine_o, sib_o, inbox_o, x_copies_o).astype(BF16)
-    for t in range(8):
-        for h in range(2):
-            pieces_o[2 * t + h] = sum_o[64 * h : 64 * h + 64, 128 * t : 128 * t + 128]
-    p_copies_o = plane_sum_send(pieces_o, 1, pin_o, sp1, rp1)
+    line_gather_finish(branch_gather, lambda i: dball.at[i], so, ro)
 
     def wait_dq(i, _):
         b = lax.rem(c + 1 + i, 8)
@@ -874,9 +1053,23 @@
     dgain_k = jnp.sum(dk * (k_pre * k_inv), axis=0, keepdims=True)
     dqkv[:, 1024:1536] = rms_back(k_pre, k_inv, dk * key_gain_row(gains)).astype(BF16)
     dqkv[:, 1536:2048] = jnp.concatenate(dv_tiles, axis=1).astype(BF16)
-    pair_copy_n = line_scatter_begin(lambda i: mm_tn(normed_t[i], dqkv[...]).astype(BF16), pair_n, mine_n, sib_n, sn, rn)
-
-    shares_o = plane_sum_share(p_copies_o, pieces_o, 1, pin_o, res_o, sp2, rp2)
+    dqall[me] = dqkv[...]
+    dqkv_gather = line_gather_start(dqkv, lambda i: dqall.at[i], sn, rn)
+    for j in range(2, 6):
+        if j >= 4:
+            bulk.far(j)
+    for j in range(2, 4):
+        bulk.near_out(j)
+
+    def out_grad(t, _):
+        at = pl.ds(pl.multiple_of(128 * t, 128), 128)
+        tile = mm_tn(attx[...].reshape(1024, 128), dball[:, :, at].reshape(1024, 128)).astype(BF16)
+        pieces_o[pl.ds(2 * t, 2)] = tile.reshape(2, 64, 128)
+        return 0
+
+    lax.fori_loop(0, 8, out_grad, 0)
+
+    p_copies_o = plane_sum_send(pieces_o, 1, pin_o, sp1, rp1)
 
     def normed_back(t, _):
         dnorm[t] = mm_nt(dqkv[...], wall[t, :, 0:2048])
@@ -884,7 +1077,6 @@
 
     lax.fori_loop(0, 8, normed_back, 0)
     dnormed = jnp.concatenate([dnorm[t] for t in range(8)], axis=1)
-    x_copies_n = line_scatter_send_x(mine_n, pair_copy_n, sib_n, inbox_n, sn, rn)
     values = tokens[...].astype(F32)
     inv = inverse_rms(values)
     dgain_in = jnp.sum(dnormed * (values * inv), axis=0, keepdims=True)
@@ -905,32 +1097,11 @@
         copy.start()
         sm_copies.append(copy)
 
-    for copy in own:
-        copy.wait()
-    for copy in a1 + b1:
-        copy.wait_recv()
-
-    def first_sums(m, _):
-        sum_a[m] = (
-            own_a[m].astype(F32) + in_a[0, m].astype(F32) + in_a[1, m].astype(F32) + in_a[2, m].astype(F32)
-        ).astype(BF16)
-        sum_b[m] = (
-            own_b[m].astype(F32) + in_b[0, m].astype(F32) + in_b[1, m].astype(F32) + in_b[2, m].astype(F32)
-        ).astype(BF16)
-        return 0
-
-    lax.fori_loop(0, 6, first_sums, 0)
-    a2, b2 = [], []
-    for o in (2, 1, 3):
-        to = lax.rem(y + o, 4)
-        a2.append(remote(sum_a.at[:, to], in2_a.at[o - 1], sa2.at[o], ra2.at[o], plane_device(to, z)))
-        to = lax.rem(z + o, 4)
-        b2.append(remote(
-            sum_b.at[:, lax.div(to, 2), lax.rem(to, 2)], in2_b.at[o - 1], sb2.at[o], rb2.at[o], plane_device(y, to)
-        ))
-    for copy in a2 + b2:
-        copy.start()
-
+    for j in range(4, 6):
+        bulk.near_out(j)
+    for j in range(4):
+        bulk.near_sum(j)
+    shares_o = plane_sum_share(p_copies_o, pieces_o, 1, pin_o, res_o, sp2, rp2)
     total = smsend[me]
     for at, copy in enumerate(sm_copies):
         copy.wait_recv()
@@ -942,31 +1113,30 @@
         copy = remote(smsum, small.at[o], sp5.at[o], rp5.at[o], device)
         copy.start()
         small_copies.append(copy)
-    sum_n = line_scatter_sum(mine_n, sib_n, inbox_n, x_copies_n).astype(BF16)
-    for t in range(16):
-        for h in range(2):
-            pieces_n[2 * t + h] = sum_n[64 * h : 64 * h + 64, 128 * t : 128 * t + 128]
+    line_gather_finish(dqkv_gather, lambda i: dqall.at[i], sn, rn)
+
+    def qkv_grad(t, _):
+        at = pl.ds(pl.multiple_of(128 * t, 128), 128)
+        tile = mm_tn(nx[...].reshape(1024, 128), dqall[:, :, at].reshape(1024, 128)).astype(BF16)
+        pieces_n[pl.ds(2 * t, 2)] = tile.reshape(2, 64, 128)
+        return 0
+
+    lax.fori_loop(0, 16, qkv_grad, 0)
     p_copies_n = plane_sum_send(pieces_n, 2, pin_n, sp3, rp3)
+    for j in range(4, 6):
+        bulk.near_sum(j)
+    bulk.far2()
     for copy in shares_o:
         copy.wait_recv()
     for t in range(8):
         gout[:, 128 * t : 128 * t + 128] = jnp.concatenate([res_o[2 * t], res_o[2 * t + 1]], axis=0).astype(F32)
+    bulk.near2()
     shares_n = plane_sum_share(p_copies_n, pieces_n, 2, pin_n, res_n, sp4, rp4)
     for at, copy in enumerate(small_copies):
         copy.wait_recv()
         total = total + small[at + 1]
     gsmall[...] = total
-    for copy in a2 + b2:
-        copy.wait_recv()
-
-    def second_sums(m, _):
-        gw[m] = sum_a[m, y].astype(F32) + in2_a[0, m].astype(F32) + in2_a[1, m].astype(F32) + in2_a[2, m].astype(F32)
-        gw[6 + m] = (
-            sum_b[m, zh, zl].astype(F32) + in2_b[0, m].astype(F32) + in2_b[1, m].astype(F32) + in2_b[2, m].astype(F32)
-        )
-        return 0
-
-    lax.fori_loop(0, 6, second_sums, 0)
+    bulk.finish(gw)
     for copy in shares_n:
         copy.wait_recv()
     for t in range(16):
@@ -977,10 +1147,8 @@
             gk[:, 128 * (t - 8) : 128 * (t - 8) + 128] = tile
         else:
             gv[:, 128 * (t - 12) : 128 * (t - 12) + 128] = tile
-    for copy in (
-        a1 + b1 + a2 + b2 + d_copies + [pair_copy_o, pair_copy_n] + x_copies_o + x_copies_n + sm_copies
-        + small_copies + p_copies_o + p_copies_n + shares_o + shares_n
-    ):
+    bulk.drain()
+    for copy in d_copies + sm_copies + small_copies + p_copies_o + p_copies_n + shares_o + shares_n:
         copy.wait_send()
 
 
@@ -1000,18 +1168,19 @@
             shape((128, 1024), F32),
             shape((48, 128), F32),
         ),
-        in_specs=[hbm, hbm] + [vm] * 21,
+        in_specs=[hbm, hbm] + [vm] * 23,
         out_specs=(vm,) * 7,
         scratch_shapes=[
             pltpu.VMEM((8, 128, 3072), BF16),
             pltpu.VMEM((6, 4, 64, 512), BF16),
             pltpu.VMEM((6, 2, 2, 64, 512), BF16),
-            pltpu.VMEM((3, 6, 4, 64, 512), BF16),
-            pltpu.VMEM((3, 6, 2, 2, 64, 512), BF16),
-            pltpu.VMEM((6, 4, 64, 512), BF16),
-            pltpu.VMEM((6, 2, 2, 64, 512), BF16),
-            pltpu.VMEM((3, 6, 64, 512), BF16),
-            pltpu.VMEM((3, 6, 64, 512), BF16),
+            pltpu.VMEM((2, 6, 4, 64, 512), BF16),
+            pltpu.VMEM((2, 6, 2, 2, 64, 512), BF16),
+            pltpu.VMEM((2, 2, 6, 2, 64, 512), BF16),
+            pltpu.VMEM((2, 6, 4, 64, 512), BF16),
+            pltpu.VMEM((2, 6, 2, 2, 64, 512), BF16),
+            pltpu.VMEM((2, 2, 6, 32, 512), BF16),
+            pltpu.VMEM((2, 2, 6, 64, 512), BF16),
             pltpu.VMEM((8, 128, 128), BF16),
             pltpu.VMEM((8, 128, 128), BF16),
             pltpu.VMEM((8, 256, 128), BF16),
@@ -1025,14 +1194,9 @@
             pltpu.VMEM((128, 2048), BF16),
             pltpu.VMEM((8, 128, 128), F32),
             pltpu.VMEM((64, 128), BF16),
-            pltpu.VMEM((4, 128, 1024), BF16),
-            pltpu.VMEM((4, 128, 1024), BF16),
-            pltpu.VMEM((4, 128, 1024), BF16),
-            pltpu.VMEM((3, 128, 1024), BF16),
-            pltpu.VMEM((4, 128, 2048), BF16),
-            pltpu.VMEM((4, 128, 2048), BF16),
-            pltpu.VMEM((4, 128, 2048), BF16),
-            pltpu.VMEM((3, 128, 2048), BF16),
+            pltpu.VMEM((8, 128, 1024), BF16),
+            pltpu.VMEM((8, 128, 2048), BF16),
+            pltpu.VMEM((128, 1024), BF16),
             pltpu.VMEM((8, 48, 128), F32),
             pltpu.VMEM((8, 48, 128), F32),
             pltpu.VMEM((48, 128), F32),
@@ -1043,10 +1207,9 @@
             pltpu.VMEM((32, 64, 128), BF16),
             pltpu.VMEM((16, 2, 64, 128), BF16),
             pltpu.VMEM((32, 64, 128), BF16),
-            sems(()), sems((2,)),
-            sems((4,)), sems((4,)), sems((4,)), sems((4,)), sems((4,)), sems((4,)), sems((4,)), sems((4,)),
+            sems(()), sems((6,)), sems((56,)), sems((56,)),
             sems((8,)), sems((8,)), sems((8,)), sems((8,)), sems((16,)), sems((16,)),
-            sems((4,)), sems((4,)), sems((4,)), sems((4,)), sems((8,)), sems((8,)),
+            sems((8,)), sems((8,)), sems((8,)), sems((8,)), sems((8,)), sems((8,)),
         ] + [sems((16,))] * 10,
         compiler_params=pltpu.CompilerParams(
             collective_id=2, has_side_effects=True, vmem_limit_bytes=60 << 20
@@ -1085,14 +1248,15 @@
     ew = jnp.concatenate([jnp.transpose(w, (1, 0, 2)) for w in (expert_gate, expert_up, expert_down)], axis=0)
     valid_rows = jnp.broadcast_to(valid.astype(F32)[None, :], (8, 128))
     (
-        wg, wall, small_all, vbuf, kvbuf, qbuf, oheads, lse, att, residual, normed_t, qpre, kpre, xall, meta, probs, picks
+        wg, wall, small_all, vbuf, kvbuf, qbuf, oheads, lse, att, residual, normed_t, qpre, kpre, xall, meta, probs, picks,
+        nx, attx,
     ) = front(tokens, w_query, w_key, w_value, w_out, small, ew, valid_rows, cosine, sine, routes.T)
     mixed, err, stats, dw, dmid, dgates = moe(
         wg.reshape(12, 1024, 512), xall, meta, residual, teacher, valid_rows
     )
     gw, gtok, gq, gk, gv, gout, gsmall = back(
         dw.reshape(12, 2, 4, 2, 64, 512), wall, small_all, vbuf, kvbuf, qbuf, oheads, lse, att, residual, normed_t,
-        qpre, kpre, xall, probs, picks, err, stats, dmid, dgates, tokens, cosine, sine,
+        qpre, kpre, xall, probs, picks, nx, attx, err, stats, dmid, dgates, tokens, cosine, sine,
     )
     loss = gsmall[4, 0] / (gsmall[5, 0] * 1024.0)
     grad_gate, grad_up, grad_down = [jnp.transpose(gw[4 * m : 4 * m + 4], (1, 0, 2)) for m in range(3)]

time: 434 us -> 352 us (0.81)
  Pallas kernels: 394 us -> 310 us
    pallas_call x1, Pallas kernels: 171 us -> 119 us  [back(): pl.pallas_call(back_kernel, out_shape=(shape((12, 64, 512), F32), shape((...]
    pallas_call x1, Pallas kernels: 146 us -> 113 us  [front(): pl.pallas_call(front_kernel, out_shape=(shape((12, 2, 4, 2, 64, 512), BF1...]
    unnamed x66 -> x70, local copies, waits for them, and re-layouts: 23.4 us -> 24.7 us
where the time goes in v2:
time: 352 us; the launch traced here: 349 us
  Pallas kernels  310 us (88%)
  local copies, waits for them, and re-layouts  34.2 us (10%)
    pallas_call x1, Pallas kernels, back(): pl.pallas_call(back_kernel, out_shape=(shape((12, 64, 512), F32), shape((...  119 us
    pallas_call x1, Pallas kernels, front(): pl.pallas_call(front_kernel, out_shape=(shape((12, 2, 4, 2, 64, 512), BF1...  113 us
    pallas_call x1, Pallas kernels, moe(): pl.pallas_call(moe_kernel, out_shape=(jax.ShapeDtypeStruct((128, 1024), B...  77.6 us
    unnamed x70, local copies, waits for them, and re-layouts  24.7 us

profile of v2, /device:TPU:1, one launch (start us, length us, event | category | flops | bytes accessed | tf_op | source)
XLA Modules:
  0.0 349.3 jit_solution(12577020286927037994)
XLA Ops:
  0.7 0.8 maximum_bitcast_fusion
  2.2 1.5 concatenate.16.small
  4.2 1.0 copy.47
  5.2 1.1 copy_bitcast_fusion
  6.5 0.9 copy-done.4
  7.4 0.9 copy-done.18
  8.4 0.9 copy-done.19
  9.3 0.9 copy-done.20
  10.2 0.9 copy-done.21
  11.8 113.1 %front.1 = (bf16[12,2,4,2,64,512]{5,4,3,2,1,0:T(8,128)(2,1)}, bf16[8,128,3072]{2,1,0:T(8,128)(2,1)}, bf16[8,48,128]{2,1,0:T(8,128)(2,1)S(1)}, f32[16,8,128]{2,1,...) custom-call(bf16[128,1024]{1,0:T(8,128)(2,1)S(1)} %copy-done.4, ...), custom_call_target="tpu_custom_call" | custom-call | flops 3000000000 | bytes 31457280 | tf_op jit(solution)/shard_map/front/pallas_call | solution.py:677
  125.0 0.8 copy-done
  125.8 0.8 copy-done.1
  126.6 0.8 copy-done.2
  127.3 0.8 copy-done.3
  128.1 0.7 copy-done.5
  128.8 0.7 copy-done.6
  135.4 77.6 %moe.1 = (bf16[128,1024]{1,0:T(8,128)(2,1)}, f32[128,1024]{1,0:T(8,128)}, f32[8,128]{1,0:T(8,128)}, bf16[12,1024,512]{2,1,0:T(8,128)(2,1)}, f32[128,1024]{1,0:T(8,128)}, /*index=5*/f32[8,8,128]{2,1,0:T(8,128)}) custom-call(bf16[12,1024,512]{2,1,0:T(8,128)(2,1)} %bitcast.40, bf16[8,128,1024]{2,1,0:T(8,128)(2,1)} %get-tuple-element.48.xall, ...), custom_call_target="tpu_custom_call" | custom-call | flops 22000001024 | bytes 31457280 | tf_op jit(solution)/shard_map/moe/pallas_call | solution.py:274
  213.0 119.1 %back.1 = (f32[12,64,512]{2,1,0:T(8,128)}, f32[128,1024]{1,0:T(8,128)}, f32[128,1024]{1,0:T(8,128)}, f32[128,512]{1,0:T(8,128)}, f32[128,512]{1,0:T(8,128)}, /*index=5*/f32[128,1024]{1,0:T(8,128)}, f32[48,128]{1,0:T(8,128)}) custom-call(bf16[12,2,4,2,64,512]{5,4,3,2,1,0:T(8,128)(2,1)} %bitcast.34, bf16[8,128,3072]{2,1,0:T(8,128)(2,1)} %get-tuple-element.53.wall_hbm, ...), custom_call_target="tpu_custom_call" | custom-call | flops 6000000000 | bytes 62914560 | tf_op jit(solution)/shard_map/back/pallas_call | solution.py:1160
  332.2 1.3 slice_bitcast_fusion.5
  333.5 1.3 fusion.1
  336.1 1.3 slice_bitcast_fusion.4
  337.4 1.3 slice_bitcast_fusion.3
  338.7 1.6 slice_bitcast_fusion
  340.3 1.1 copy.43
  341.4 1.1 copy.42
  342.5 1.1 copy.41
  343.7 0.7 copy.54
  344.4 0.8 copy.55
  345.2 0.8 copy.56
  346.0 0.7 copy.57
  346.7 0.7 copy.58
  347.4 0.8 copy.59
  (57 shorter events, 7.9 us)
Async XLA Ops:
  2.1 122.8 %copy-start.17 = (f32[8,128]{1,0:T(8,128)}, f32[8,128]{1,0:T(8,128)S(1)}, u32[]{:S(2)}) copy-start(f32[8,128]{1,0:T(8,128)S(1)} %broadcast_in_dim.5.valid.valid_row) | copy-start | bytes 12292
  4.2 120.8 %copy-start.11 = (f32[128,128]{1,0:T(8,128)}, f32[128,128]{1,0:T(8,128)S(1)}, u32[]{:S(2)}) copy-start(f32[128,128]{1,0:T(8,128)S(1)} %get-tuple-element.122.cosine) | copy-start | bytes 196612
  4.2 120.8 %copy-start.12 = (f32[128,128]{1,0:T(8,128)}, f32[128,128]{1,0:T(8,128)S(1)}, u32[]{:S(2)}) copy-start(f32[128,128]{1,0:T(8,128)S(1)} %get-tuple-element.123.sine) | copy-start | bytes 196612
  6.5 1.0 copy-start.4
  7.4 0.9 copy-start.18
  8.4 0.9 copy-start.19
  9.3 0.9 copy-start.20
  10.2 0.9 copy-start.21
  11.1 0.7 copy-start.22
  125.0 0.8 copy-start
  125.8 0.8 copy-start.1
  126.6 0.8 copy-start.2
  127.3 0.8 copy-start.3
  128.1 0.7 copy-start.5
  128.8 0.7 copy-start.6
  129.5 0.7 copy-start.7
  130.2 0.7 copy-start.8
  130.9 0.7 copy-start.9
  131.7 0.7 copy-start.10
  132.3 0.6 copy-start.13
  133.0 0.6 copy-start.14
  133.6 0.6 copy-start.15
  134.2 0.6 copy-start.16
  134.8 0.6 copy-start.23
  332.1 11.6 %copy-start.27 = (bf16[128,1024]{1,0:T(8,128)(2,1)S(1)}, bf16[128,1024]{1,0:T(8,128)(2,1)}, u32[]{:S(2)}) copy-start(bf16[128,1024]{1,0:T(8,128)(2,1)} %get-tuple-element.139) | copy-start | bytes 786436
  332.1 12.3 %copy-start.26 = (f32[128,1024]{1,0:T(8,128)S(1)}, f32[128,1024]{1,0:T(8,128)}, u32[]{:S(2)}) copy-start(f32[128,1024]{1,0:T(8,128)} %get-tuple-element.141) | copy-start | bytes 1572868
  332.1 13.0 %copy-start.25 = (f32[128,1024]{1,0:T(8,128)S(1)}, f32[128,1024]{1,0:T(8,128)}, u32[]{:S(2)}) copy-start(f32[128,1024]{1,0:T(8,128)} %get-tuple-element.143) | copy-start | bytes 1572868
  332.1 13.8 %copy-start.29 = (f32[128,512]{1,0:T(8,128)S(1)}, f32[128,512]{1,0:T(8,128)}, u32[]{:S(2)}) copy-start(f32[128,512]{1,0:T(8,128)} %get-tuple-element.144) | copy-start | bytes 786436
  332.1 14.5 %copy-start.28 = (f32[128,512]{1,0:T(8,128)S(1)}, f32[128,512]{1,0:T(8,128)}, u32[]{:S(2)}) copy-start(f32[128,512]{1,0:T(8,128)} %get-tuple-element.145) | copy-start | bytes 786436
  332.2 15.2 %copy-start.24 = (f32[128,1024]{1,0:T(8,128)S(1)}, f32[128,1024]{1,0:T(8,128)}, u32[]{:S(2)}) copy-start(f32[128,1024]{1,0:T(8,128)} %get-tuple-element.148) | copy-start | bytes 1572868

commit v3 on v0

v3 whole, which is shorter than its diff:
```python
import jax
import jax.numpy as jnp
from jax import lax
from jax.experimental import pallas as pl
from jax.experimental.pallas import tpu as pltpu
from jax.sharding import PartitionSpec as P

MESH = pl.DeviceIdType.MESH
F32 = jnp.float32
BF16 = jnp.bfloat16

HEAD = 64
TOP = 8
EPS = 1e-06
THETA = 10000.0
NEG = -1e30
SCALE = HEAD**-0.5


def mm(a, b):
    return lax.dot_general(a, b, (((1,), (0,)), ((), ())), preferred_element_type=F32)


def mm_nt(a, b):
    return lax.dot_general(a, b, (((1,), (1,)), ((), ())), preferred_element_type=F32)


def mm_tn(a, b):
    return lax.dot_general(a, b, (((0,), (0,)), ((), ())), preferred_element_type=F32)


def places():
    e, c, d = lax.axis_index("expert"), lax.axis_index("ctx"), lax.axis_index("dp")
    return e // 2, e % 2, c, d


def yz():
    c, d = lax.axis_index("ctx"), lax.axis_index("dp")
    return lax.rem(c, 4), lax.div(c, 4) * 2 + d


def remote(src, dst, send, recv, device):
    return pltpu.make_async_remote_copy(
        src_ref=src, dst_ref=dst, send_sem=send, recv_sem=recv, device_id=device, device_id_type=MESH
    )


def line_device(x, core):
    return (lax.rem(x + 4, 4) * 2 + core, lax.axis_index("ctx"), lax.axis_index("dp"))


def plane_device(y, z):
    return (lax.axis_index("expert"), lax.div(z, 2) * 4 + y, lax.rem(z, 2))


def plane_peer(o):
    e, c, d = lax.axis_index("expert"), lax.axis_index("ctx"), lax.axis_index("dp")
    q = lax.rem(c * 2 + d + o, 16)
    return q, (e, lax.div(q, 2), lax.rem(q, 2))


def greet_all():
    barrier = pltpu.get_barrier_semaphore()
    e, c, d = lax.axis_index("expert"), lax.axis_index("ctx"), lax.axis_index("dp")
    for o in range(1, 8):
        pl.semaphore_signal(barrier, inc=1, device_id=(lax.rem(e + o, 8), c, d), device_id_type=MESH)
    for o in range(1, 16):
        _, device = plane_peer(o)
        pl.semaphore_signal(barrier, inc=1, device_id=device, device_id_type=MESH)
    pl.semaphore_wait(barrier, 22)


def line_gather_start(own, buf, send, recv):
    x, core, _, _ = places()
    me = x * 2 + core
    copies = [remote(own, buf(me), send.at[o], recv.at[o], line_device(x + o, core)) for o in (2, 1, 3)]
    copies.append(remote(own, buf(me), send.at[0], recv.at[0], line_device(x, 1 - core)))
    for copy in copies:
        copy.start()
    return copies


def line_gather_finish(copies, buf, send, recv):
    x, core, _, _ = places()
    forwards = []
    for at, o in ((1, 1), (2, 3), (0, 2)):
        copies[at].wait_recv()
        block = buf(lax.rem(x - o + 4, 4) * 2 + core)
        copy = remote(block, block, send.at[4 + o], recv.at[4 + o], line_device(x, 1 - core))
        copy.start()
        forwards.append(copy)
    copies[3].wait_recv()
    for copy in forwards:
        copy.wait_recv()
    for copy in copies + forwards:
        copy.wait_send()


def line_scatter_send_pair(pair, sib, send, recv):
    x, core, _, _ = places()
    copy = remote(pair, sib, send.at[0], recv.at[0], line_device(x, 1 - core))
    copy.start()
    return copy


def line_scatter_send_x(mine, pair_copy, sib, inbox, send, recv):
    x, core, _, _ = places()
    pair_copy.wait_recv()
    copies = []
    for o in (2, 1, 3):
        to = lax.rem(x + o, 4)
        mine[to] = (mine[to].astype(F32) + sib[to].astype(F32)).astype(mine.dtype)
        copy = remote(mine.at[to], inbox.at[o - 1], send.at[o], recv.at[o], line_device(x + o, core))
        copy.start()
        copies.append(copy)
    return copies


def line_scatter_sum(mine, sib, inbox, copies):
    x, _, _, _ = places()
    total = mine[x].astype(F32) + sib[x].astype(F32)
    for at, o in ((1, 1), (2, 3), (0, 2)):
        copies[at].wait_recv()
        total = total + inbox[o - 1].astype(F32)
    return total


def plane_sum_send(pieces, n, inbox, send, recv):
    copies = []
    for o in range(1, 16):
        q, device = plane_peer(o)
        copy = remote(pieces.at[pl.ds(q * n, n)], inbox.at[o], send.at[o], recv.at[o], device)
        copy.start()
        copies.append(copy)
    return copies


def plane_sum_share(copies, pieces, n, inbox, result, send, recv):
    p = lax.axis_index("ctx") * 2 + lax.axis_index("dp")
    total = pieces[pl.ds(p * n, n)].astype(F32)
    for at, copy in enumerate(copies):
        copy.wait_recv()
        total = total + inbox[at + 1].astype(F32)
    result[pl.ds(p * n, n)] = total.astype(BF16)
    shares = []
    view = result.at[pl.ds(p * n, n)]
    for o in range(1, 16):
        _, device = plane_peer(o)
        copy = remote(view, view, send.at[o], recv.at[o], device)
        copy.start()
        shares.append(copy)
    return shares


class Copies:
    def __init__(self, send, recv):
        self.send, self.recv = send, recv
        self.y, self.z = yz()
        self.copies = {}

    def go(self, n, src, dst, device):
        copy = remote(src, dst, self.send.at[n], self.recv.at[n], device)
        copy.start()
        self.copies[n] = copy

    def drain(self):
        for copy in self.copies.values():
            copy.wait_send()


class PlaneGather(Copies):
    def __init__(self, wg, send, recv):
        super().__init__(send, recv)
        self.wg = wg

    def place(self, m, y, z):
        return self.wg.at[m, lax.div(z, 2), y, lax.rem(z, 2)]

    def shards(self):
        y, z = self.y, self.z
        a, b = pl.ds(0, 6), pl.ds(6, 6)
        for i, o in enumerate((1, 3)):
            view = self.place(a, y, z)
            self.go(i, view, view, plane_device(lax.rem(y + o, 4), z))
            view = self.place(b, y, z)
            self.go(2 + i, view, view, plane_device(y, lax.rem(z + o, 4)))

    def shards_on(self):
        y, z = self.y, self.z
        a, b = pl.ds(0, 6), pl.ds(6, 6)
        for i, o in enumerate((1, 3)):
            rows = pl.ds(32 * i, 32)
            self.copies[i].wait_recv()
            view = self.place(a, lax.rem(y - o + 4, 4), z).at[:, rows]
            self.go(4 + i, view, view, plane_device(lax.rem(y + o, 4), z))
            self.copies[2 + i].wait_recv()
            view = self.place(b, y, lax.rem(z - o + 4, 4)).at[:, rows]
            self.go(6 + i, view, view, plane_device(y, lax.rem(z + o, 4)))

    def shards_wait(self):
        for n in range(4, 8):
            self.copies[n].wait_recv()

    def lines(self, j):
        y, z = self.y, self.z
        for i, o in enumerate((1, 3)):
            view = self.wg.at[j, lax.div(z, 2), :, lax.rem(z, 2)]
            self.go(8 + 8 * j + i, view, view, plane_device(y, lax.rem(z + o, 4)))
            view = self.wg.at[6 + j, :, y]
            self.go(10 + 8 * j + i, view, view, plane_device(lax.rem(y + o, 4), z))

    def lines_on(self, j):
        y, z = self.y, self.z
        for i, o in enumerate((1, 3)):
            self.copies[8 + 8 * j + i].wait_recv()
            from_z = lax.rem(z - o + 4, 4)
            view = self.wg.at[j, lax.div(from_z, 2), pl.ds(2 * i, 2), lax.rem(from_z, 2)]
            self.go(12 + 8 * j + i, view, view, plane_device(y, lax.rem(z + o, 4)))
            self.copies[10 + 8 * j + i].wait_recv()
            view = self.wg.at[6 + j, i, lax.rem(y - o + 4, 4)]
            self.go(14 + 8 * j + i, view, view, plane_device(lax.rem(y + o, 4), z))

    def lines_wait(self, j):
        for n in range(12 + 8 * j, 16 + 8 * j):
            self.copies[n].wait_recv()


class PlaneScatter(Copies):
    def __init__(self, dw, far_in, near_in, far2_in, near2_in, stage, load, send, recv):
        super().__init__(send, recv)
        self.dw, self.far_in, self.near_in = dw, far_in, near_in
        self.far2_in, self.near2_in, self.stage, self.load = far2_in, near2_in, stage, load

    def block(self, half, m, at):
        if half == 0:
            return self.dw.at[m, lax.div(at, 2), :, lax.rem(at, 2)]
        return self.dw.at[6 + m, :, at]

    def due(self, half, m, at):
        if half == 0:
            return self.dw.at[m, lax.div(self.z, 2), at, lax.rem(self.z, 2)]
        return self.dw.at[m, lax.div(at, 2), self.y, lax.rem(at, 2)]

    def device(self, half, at):
        return plane_device(self.y, at) if half == 0 else plane_device(at, self.z)

    def place(self, half):
        return self.z if half == 0 else self.y

    def far(self, j):
        for half in range(2):
            me = self.place(half)
            for i, o in enumerate((1, 3)):
                view = self.block(half, j, lax.rem(me + 2, 4))
                view = view.at[pl.ds(2 * i, 2)] if half == 0 else view.at[i]
                self.go(8 * j + 2 * half + i, view, self.far_in.at[half, i, j], self.device(half, lax.rem(me + o, 4)))

    def near_out(self, j):
        loads = []
        for half in range(2):
            for i in range(2):
                self.copies[8 * j + 2 * half + i].wait_recv()
                spot = self.stage[0].at[i, pl.ds(0, 2)] if half == 0 else self.stage[1].at[i, 0]
                load = pltpu.make_async_copy(self.far_in.at[half, i, j], spot, self.load.at[2 * half + i])
                load.start()
                loads.append((load, spot))
        for half in range(2):
            me = self.place(half)
            for i, o in enumerate((1, 3)):
                load, spot = loads[2 * half + i]
                load.wait()
                to = lax.rem(me + o, 4)
                whole = self.block(half, j, to)
                part = whole.at[pl.ds(2 * i, 2)] if half == 0 else whole.at[i]
                part[...] = (part[...].astype(F32) + spot[...].astype(F32)).astype(BF16)
                self.go(8 * j + 4 + 2 * half + i, whole, self.near_in[half].at[i, j], self.device(half, to))

    def near_load(self, j):
        self.loads = []
        for half in range(2):
            for i in range(2):
                self.copies[8 * j + 4 + 2 * half + i].wait_recv()
                load = pltpu.make_async_copy(
                    self.near_in[half].at[i, j], self.stage[half].at[i], self.load.at[2 * half + i]
                )
                load.start()
                self.loads.append(load)

    def near_sum(self, j):
        self.near_load(j)
        for half in range(2):
            own, stage = self.block(half, j, self.place(half)), self.stage[half]
            self.loads[2 * half].wait()
            self.loads[2 * half + 1].wait()
            own[...] = (own[...].astype(F32) + stage[0].astype(F32) + stage[1].astype(F32)).astype(BF16)

    def place2(self, half):
        return self.y if half == 0 else self.z

    def device2(self, half, at):
        return plane_device(at, self.z) if half == 0 else plane_device(self.y, at)

    def far2(self):
        for half in range(2):
            me = self.place2(half)
            for i, o in enumerate((1, 3)):
                view = self.due(half, pl.ds(6 * half, 6), lax.rem(me + 2, 4)).at[:, pl.ds(32 * i, 32)]
                self.go(48 + 2 * half + i, view, self.far2_in.at[half, i], self.device2(half, lax.rem(me + o, 4)))

    def near2(self):
        for half in range(2):
            me = self.place2(half)
            for i, o in enumerate((1, 3)):
                self.copies[48 + 2 * half + i].wait_recv()
                to = lax.rem(me + o, 4)

                def add(m, _):
                    part = self.due(half, 6 * half + m, to).at[pl.ds(32 * i, 32)]
                    part[...] = (part[...].astype(F32) + self.far2_in[half, i, m].astype(F32)).astype(BF16)
                    return 0

                lax.fori_loop(0, 6, add, 0)
                view = self.due(half, pl.ds(6 * half, 6), to)
                self.go(52 + 2 * half + i, view, self.near2_in.at[half, i], self.device2(half, to))

    def finish(self, result):
        for half in range(2):
            me = self.place2(half)
            for i in range(2):
                self.copies[52 + 2 * half + i].wait_recv()

            def add(m, _):
                result[6 * half + m] = (
                    self.due(half, 6 * half + m, me)[...].astype(F32)
                    + self.near2_in[half, 0, m].astype(F32)
                    + self.near2_in[half, 1, m].astype(F32)
                )
                return 0

            lax.fori_loop(0, 6, add, 0)


def low_lanes():
    return lax.broadcasted_iota(jnp.int32, (128, 128), 1) < 64


def swap_halves(tile):
    lane = lax.rem(lax.broadcasted_iota(jnp.int32, (128, 128), 1), 64)
    return jnp.where(lane < 32, pltpu.roll(tile, 96, 1), pltpu.roll(tile, 32, 1))


def gain_row(small, row):
    return jnp.concatenate([small[i, row : row + 1, :] for i in range(8)], axis=1)


def key_gain_row(small):
    lane = lax.broadcasted_iota(jnp.int32, (1, 128), 1)
    return jnp.concatenate(
        [jnp.where(lane < 64, small[2 * t, 3:4, :], small[2 * t + 1, 3:4, :]) for t in range(4)], axis=1
    )


def router_rows(small):
    return jnp.concatenate([small[i, 16:48, :] for i in range(8)], axis=1)


def inverse_rms(values):
    return lax.rsqrt(jnp.mean(values * values, axis=1, keepdims=True) + EPS)


def rms_back(values, inverse, grad):
    hat = values * inverse
    return inverse * (grad - hat * jnp.mean(grad * hat, axis=1, keepdims=True))


def stack_heads(tile, upper):
    lo = low_lanes()
    turned = pltpu.roll(tile, 64, 1)
    first, second = (turned, tile) if upper else (tile, turned)
    keep = jnp.logical_not(lo) if upper else lo
    return jnp.concatenate([jnp.where(keep, first, 0.0), jnp.where(keep, second, 0.0)], axis=0)


def key_rows(kvbuf, k):
    return kvbuf[pl.ds(4 * k, 4)].reshape(512, 128)


def key_bias(vbuf, k):
    row = jnp.concatenate([vbuf[4 * k + i, 0:1, :] for i in range(4)], axis=1)
    return (row - 1.0) * 1e30


def mask_last(scores, bias, b, d):
    half = lax.rem(b, 2) * 256
    column = lax.broadcasted_iota(jnp.int32, (256, 512), 1)
    row = lax.rem(lax.broadcasted_iota(jnp.int32, (256, 512), 0), 128)
    masked = jnp.where(column < half + 256, scores + bias, NEG)
    return jnp.where(column == row + (half + 128 * d), scores, masked)


def down(e):
    return 4 + e + 4 * lax.div(e, 2)


class Refs:
    def __init__(self, names, refs):
        for name, ref in zip(names, refs, strict=True):
            setattr(self, name, ref)


INPUTS = (
    "tokens", "wq", "wk", "wv", "wo", "norm_in", "query_gain", "norm_mid", "key_gain", "w_router",
    "expert_gate", "expert_up", "expert_down", "valid", "cosine", "sine", "routes", "teacher",
)
OUTPUTS = (
    ("mixed", (128, 1024), BF16),
    ("gtok", (128, 1024), F32),
    ("res_o", (16, 64, 128), BF16),
    ("res_n", (32, 64, 128), BF16),
    ("gsmall", (48, 128), F32),
    ("gw", (12, 64, 512), F32),
)
SPILLS = (
    ("wall_keep", (8, 256, 1024), BF16),
    ("far_in", (2, 2, 6, 2, 64, 512), BF16),
    ("near_in_a", (2, 6, 4, 64, 512), BF16),
    ("near_in_b", (2, 6, 2, 2, 64, 512), BF16),
)
SCRATCH = (
    ("big1", (8, 256, 1024), BF16),
    ("big2", (8, 256, 1024), BF16),
    ("big3", (8, 256, 1024), BF16),
    ("rows", (8, 128, 1024), BF16),
    ("wo_all", (8, 128, 1024), BF16),
    ("wg", (12, 2, 4, 2, 64, 512), BF16),
    ("gbuf", (4, 512, 512), BF16),
    ("ubuf", (4, 512, 512), BF16),
    ("mine", (4, 128, 1024), BF16),
    ("pair", (4, 128, 1024), BF16),
    ("sib", (4, 128, 1024), BF16),
    ("inbox", (3, 128, 1024), BF16),
    ("stage_a", (2, 4, 64, 512), BF16),
    ("stage_b", (2, 2, 2, 64, 512), BF16),
    ("far2_in", (2, 2, 6, 32, 512), BF16),
    ("near2_in", (2, 2, 6, 64, 512), BF16),
    ("small_all", (8, 48, 128), BF16),
    ("vbuf", (16, 8, 128), F32),
    ("kvbuf", (16, 128, 128), BF16),
    ("qbuf", (8, 128, 128), BF16),
    ("oheads", (8, 128, 128), F32),
    ("lse", (8, 256, 128), F32),
    ("att", (8, 128, 128), BF16),
    ("attx", (8, 128, 128), BF16),
    ("normed_t", (8, 128, 128), BF16),
    ("nx", (8, 128, 128), BF16),
    ("sendq", (8, 128, 128), BF16),
    ("osend", (8, 128, 128), BF16),
    ("residual", (128, 1024), F32),
    ("qpre", (128, 1024), F32),
    ("kpre", (128, 512), F32),
    ("midl", (128, 1024), BF16),
    ("low", (128, 1024), BF16),
    ("meta", (8, 8, 128), F32),
    ("metasend", (8, 8, 128), F32),
    ("probs", (32, 128), F32),
    ("picks", (32, 128), F32),
    ("stats", (8, 128), F32),
    ("pcat", (8, 256, 128), BF16),
    ("gslot", (8, 256, 128), F32),
    ("dgates", (8, 8, 128), F32),
    ("dgsend", (8, 8, 128), F32),
    ("dattbuf", (8, 128, 128), BF16),
    ("qpad", (8, 256, 128), BF16),
    ("dop", (8, 256, 128), BF16),
    ("dkvsend", (16, 128, 128), BF16),
    ("dkvbuf", (16, 128, 128), BF16),
    ("dqkv", (256, 1024), BF16),
    ("dnorm", (8, 128, 128), F32),
    ("dlog", (64, 128), BF16),
    ("smsend", (8, 48, 128), F32),
    ("sminbox", (8, 48, 128), F32),
    ("smsum", (48, 128), F32),
    ("smplane", (16, 48, 128), F32),
    ("pieces_o", (16, 64, 128), BF16),
    ("pin_o", (16, 1, 64, 128), BF16),
    ("pieces_n", (32, 64, 128), BF16),
    ("pin_n", (16, 2, 64, 128), BF16),
)
SEMAPHORES = (
    ("own_sem", 6), ("keep_sem", 2), ("teacher_sem", 1), ("load_sem", 4),
    ("ssm", 8), ("rsm", 8), ("sqkv", 8), ("rqkv", 8), ("swo", 8), ("rwo", 8), ("sv", 16), ("rv", 16),
    ("sew", 56), ("rew", 56), ("snx", 8), ("rnx", 8), ("sax", 8), ("rax", 8),
    ("skv", 16), ("rkv", 16), ("sq", 8), ("rq", 8), ("so", 8), ("ro", 8), ("sx", 8), ("rx", 8), ("sm", 8), ("rm", 8),
    ("s1", 4), ("r1", 4), ("s2", 8), ("r2", 8), ("s3", 4), ("r3", 4), ("s4", 8), ("r4", 8),
    ("sw", 56), ("rw", 56), ("sd", 8), ("rd", 8), ("sdq", 8), ("rdq", 8), ("sdkv", 16), ("rdkv", 16),
    ("sb", 8), ("rb", 8), ("sn", 8), ("rn", 8), ("sms", 8), ("rms", 8),
    ("sp1", 16), ("rp1", 16), ("sp2", 16), ("rp2", 16), ("sp3", 16), ("rp3", 16), ("sp4", 16), ("rp4", 16),
    ("sp5", 16), ("rp5", 16),
)
NAMES = INPUTS + tuple(n for part in (OUTPUTS, SPILLS, SCRATCH, SEMAPHORES) for n, *_ in part)


def layer_kernel(*refs):
    r = Refs(NAMES, refs)
    x, core, c, d = places()
    me = x * 2 + core
    p = c * 2 + d
    y, z = yz()
    e_at = lax.axis_index("expert")
    lo = low_lanes()

    wall = r.big1
    own = [
        pltpu.make_async_copy(r.wq, wall.at[me, pl.ds(0, 128)], r.own_sem.at[0]),
        pltpu.make_async_copy(r.wk, wall.at[me, pl.ds(128, 128), pl.ds(0, 512)], r.own_sem.at[1]),
        pltpu.make_async_copy(r.wv, wall.at[me, pl.ds(128, 128), pl.ds(512, 512)], r.own_sem.at[2]),
        pltpu.make_async_copy(r.wo, r.wo_all.at[me], r.own_sem.at[3]),
    ]
    for copy in own:
        copy.start()
    teacher_load = pltpu.make_async_copy(r.teacher, r.gtok, r.teacher_sem.at[0])
    teacher_load.start()
    eye = lax.broadcasted_iota(jnp.int32, (128, 128), 0) == lax.broadcasted_iota(jnp.int32, (128, 128), 1)
    rows = [ref[...].astype(F32).reshape(1, 128) for ref in (r.norm_in, r.query_gain, r.norm_mid)]
    key_row = r.key_gain[...].astype(F32).reshape(1, 64)
    rows += [jnp.concatenate([key_row, key_row], axis=1), jnp.zeros((12, 128), F32), r.w_router[...].astype(F32)]
    r.small_all[me] = jnp.concatenate(rows, axis=0).astype(BF16)
    valid_row = r.valid[...].astype(F32).reshape(1, 128)
    r.vbuf[p] = jnp.broadcast_to(valid_row, (8, 128))
    greet_all()

    gather = PlaneGather(r.wg, r.sew, r.rew)
    small_gather = line_gather_start(r.small_all.at[me], lambda i: r.small_all.at[i], r.ssm, r.rsm)
    for copy in own[:3]:
        copy.wait()
    qkv_gather = line_gather_start(wall.at[me], lambda i: wall.at[i], r.sqkv, r.rqkv)
    for ref, first in ((r.expert_gate, (0, 1, 2, 3)), (r.expert_up, (6, 7, 8, 9)), (r.expert_down, (4, 5, 10, 11))):
        whole = ref[...].astype(F32)
        for e, m in enumerate(first):
            r.wg[m, lax.div(z, 2), y, lax.rem(z, 2)] = whole[:, e, :].astype(BF16)
    gather.shards()
    own[3].wait()
    out_gather = line_gather_start(r.wo_all.at[me], lambda i: r.wo_all.at[i], r.swo, r.rwo)
    valid_copies = []
    for o in range(1, 16):
        _, device = plane_peer(o)
        copy = remote(r.vbuf.at[p], r.vbuf.at[p], r.sv.at[o], r.rv.at[o], device)
        copy.start()
        valid_copies.append(copy)

    line_gather_finish(small_gather, lambda i: r.small_all.at[i], r.ssm, r.rsm)
    gains = r.small_all[...].astype(F32)
    values = r.tokens[...].astype(F32)
    normed = (values * inverse_rms(values) * gain_row(gains, 0)).astype(BF16)
    for t in range(8):
        r.normed_t[t] = normed[:, 128 * t : 128 * t + 128]
    r.nx[me] = r.normed_t[me]
    spread_copies = []
    for o in range(1, 8):
        to = lax.rem(me + o, 8)
        copy = remote(r.normed_t.at[to], r.nx.at[me], r.snx.at[o], r.rnx.at[o], (to, c, d))
        copy.start()
        spread_copies.append(copy)
    gather.shards_on()
    gather.shards_wait()
    for j in range(2):
        gather.lines(j)

    line_gather_finish(qkv_gather, lambda i: wall.at[i], r.sqkv, r.rqkv)
    for j in range(2):
        gather.lines_on(j)
    q_pre = mm(normed, wall[:, 0:128, :].reshape(1024, 1024))
    kv_pre = mm(normed, wall[:, 128:256, :].reshape(1024, 1024))
    k_pre = kv_pre[:, 0:512]
    v_low = kv_pre[:, 512:1024].astype(BF16).astype(F32)
    r.qpre[...] = q_pre
    r.kpre[...] = k_pre
    cos, sin = r.cosine[...], r.sine[...]
    kn = k_pre * inverse_rms(k_pre) * key_gain_row(gains)
    for t in range(4):
        tile = kn[:, 128 * t : 128 * t + 128]
        k_rot = tile * cos + swap_halves(tile) * sin
        v_tile = v_low[:, 128 * t : 128 * t + 128]
        r.dkvsend[2 * t] = jnp.where(lo, k_rot, pltpu.roll(v_tile, 64, 1)).astype(BF16)
        r.dkvsend[2 * t + 1] = jnp.where(lo, pltpu.roll(k_rot, 64, 1), v_tile).astype(BF16)
    r.kvbuf[p] = r.dkvsend[c]
    kv_copies = []
    for o in range(1, 16):
        q, device = plane_peer(o)
        copy = remote(r.dkvsend.at[lax.div(q, 2)], r.kvbuf.at[p], r.skv.at[o], r.rkv.at[o], device)
        copy.start()
        kv_copies.append(copy)
    qn = q_pre * inverse_rms(q_pre) * gain_row(gains, 1)
    for t in range(8):
        tile = qn[:, 128 * t : 128 * t + 128]
        r.sendq[t] = (tile * cos + swap_halves(tile) * sin).astype(BF16)
    r.qbuf[c] = r.sendq[c]
    q_copies = []
    for o in range(1, 8):
        to = lax.rem(c + o, 8)
        copy = remote(r.sendq.at[to], r.qbuf.at[c], r.sq.at[o], r.rq.at[o], (e_at, to, d))
        copy.start()
        q_copies.append(copy)
    keep = pltpu.make_async_copy(wall, r.wall_keep, r.keep_sem.at[0])
    keep.start()
    for copy in valid_copies + kv_copies + q_copies:
        copy.wait()
    gather.lines(2)

    def prepare(b, _):
        r.qpad[b] = (stack_heads(r.qbuf[b].astype(F32), False) * SCALE).astype(BF16)
        return 0

    lax.fori_loop(0, 8, prepare, 0)

    def chunk(i, _):
        b = lax.rem(c + 1 + i, 8)
        queries = r.qpad[b]
        last = lax.div(b, 2)

        def update(carry, block, scores):
            top, total, acc = carry
            new_top = jnp.maximum(top, jnp.max(scores, axis=1, keepdims=True))
            weights = jnp.exp(scores - new_top)
            shrink = jnp.exp(top - new_top)
            total = total * shrink + jnp.sum(weights, axis=1, keepdims=True)
            acc = acc * shrink + mm(weights.astype(BF16), block)
            return (new_top, total, acc)

        def keys(k, carry):
            block = key_rows(r.kvbuf, k)
            return update(carry, block, mm_nt(queries, block) + key_bias(r.vbuf, k))

        zero = jnp.zeros((256, 1), F32)
        carry = lax.fori_loop(0, last, keys, (zero + NEG, zero, jnp.zeros((256, 128), F32)))
        block = key_rows(r.kvbuf, last)
        scores = mask_last(mm_nt(queries, block), key_bias(r.vbuf, last), b, d)
        top, total, acc = update(carry, block, scores)
        acc = acc / total
        r.lse[b] = jnp.broadcast_to(top + jnp.log(total), (256, 128))
        merged = jnp.where(lo, pltpu.roll(acc[:128], 64, 1), acc[128:])
        r.oheads[b] = merged
        r.osend[b] = merged.astype(BF16)

        @pl.when(b != c)
        def _():
            remote(r.osend.at[b], r.att.at[c], r.so.at[b], r.ro.at[c], (e_at, b, d)).start()

        @pl.when(b == c)
        def _():
            r.att[c] = r.osend[c]

        return 0

    lax.fori_loop(0, 4, chunk, 0)
    gather.lines_on(2)
    lax.fori_loop(4, 8, chunk, 0)
    line_gather_finish(out_gather, lambda i: r.wo_all.at[i], r.swo, r.rwo)

    def wait_rest(i, _):
        b = lax.rem(c + 1 + i, 8)
        copy = remote(r.osend.at[b], r.att.at[b], r.so.at[b], r.ro.at[b], (e_at, b, d))
        copy.wait_send()
        copy.wait_recv()
        return 0

    lax.fori_loop(0, 7, wait_rest, 0)
    for j in range(3, 6):
        gather.lines(j)
    r.attx[me] = r.att[me]
    for o in range(1, 8):
        to = lax.rem(me + o, 8)
        copy = remote(r.att.at[to], r.attx.at[me], r.sax.at[o], r.rax.at[o], (to, c, d))
        copy.start()
        spread_copies.append(copy)
    attended = jnp.concatenate([r.att[t] for t in range(8)], axis=1)
    res = r.tokens[...].astype(F32) + mm(attended, r.wo_all[...].reshape(1024, 1024))
    r.residual[...] = res
    mid = (res * inverse_rms(res) * gain_row(gains, 2)).astype(BF16)
    r.midl[...] = mid
    r.rows[me] = mid
    mid_gather = line_gather_start(r.midl, lambda i: r.rows.at[i], r.sx, r.rx)

    logits = mm_nt(router_rows(r.small_all[...]), mid)
    terms = jnp.exp(logits - jnp.max(logits, axis=0, keepdims=True))
    probs = terms / jnp.sum(terms, axis=0, keepdims=True)
    ids = lax.broadcasted_iota(jnp.int32, (32, 128), 0).astype(F32)
    routes = r.routes[...].astype(F32)
    picks = jnp.zeros((32, 128), F32)
    for k in range(TOP):
        picks = picks + (ids == routes[k : k + 1, :]).astype(F32)
    before = lax.broadcasted_iota(jnp.int32, (128, 128), 0) < lax.broadcasted_iota(jnp.int32, (128, 128), 1)
    slots = mm(picks.astype(BF16), before.astype(F32).astype(BF16))
    slots = jnp.where(picks > 0.0, slots, -1.0)
    r.probs[...] = probs
    r.picks[...] = picks
    gates = probs * picks
    for i in range(8):
        r.metasend[i, 0:4, :] = gates[4 * i : 4 * i + 4, :]
        r.metasend[i, 4:8, :] = slots[4 * i : 4 * i + 4, :]
    r.meta[me] = r.metasend[me]
    meta_copies = []
    for o in range(1, 8):
        to = lax.rem(me + o, 8)
        copy = remote(r.metasend.at[to], r.meta.at[me], r.sm.at[o], r.rm.at[o], (to, c, d))
        copy.start()
        meta_copies.append(copy)
    gather.lines_on(3)
    line_gather_finish(mid_gather, lambda i: r.rows.at[i], r.sx, r.rx)
    for copy in meta_copies:
        copy.wait()
    keep.wait()

    slot_ids = lax.broadcasted_iota(jnp.int32, (64, 128), 0).astype(F32)

    def compact(s, _):
        for e in range(4):
            hit = slot_ids == r.meta[s, 4 + e : 5 + e, :]
            at = slice(e * 64, (e + 1) * 64)
            r.pcat[s, at, :] = hit.astype(F32).astype(BF16)
            gate = jnp.sum(jnp.where(hit, r.meta[s, e : e + 1, :], 0.0), axis=1, keepdims=True)
            r.gslot[s, at, :] = jnp.broadcast_to(gate, (64, 128))
        r.big1[s] = mm(r.pcat[s], r.rows[s]).astype(BF16)
        return 0

    lax.fori_loop(0, 8, compact, 0)
    gather.lines_on(4)
    gather.lines_on(5)

    def slots_of(e):
        return pl.ds(pl.multiple_of(e * 64, 64), 64)

    def expert_rows(ref, e):
        return ref[:, slots_of(e), :].reshape(512, ref.shape[2])

    def weight(m):
        return r.wg[m].reshape(1024, 512)

    def forward_in(e, _):
        rows = expert_rows(r.big1, e)
        g = mm(rows, weight(e))
        u = mm(rows, weight(6 + e))
        r.gbuf[e] = g.astype(BF16)
        r.ubuf[e] = u.astype(BF16)
        r.big3[:, slots_of(e), 0:512] = (g * jax.nn.sigmoid(g) * u).astype(BF16).reshape(8, 64, 512)
        return 0

    def forward_out(e, _):
        act = r.big3[:, slots_of(e), 0:512].reshape(512, 512)
        gate = expert_rows(r.gslot, e)[:, 0:1]
        r.big3[:, slots_of(e), :] = (mm_nt(act, weight(down(e))) * gate).astype(BF16).reshape(8, 64, 1024)
        return 0

    for j in range(4):
        gather.lines_wait(j)
    lax.fori_loop(0, 4, forward_in, 0)
    for j in range(4, 6):
        gather.lines_wait(j)
    lax.fori_loop(0, 4, forward_out, 0)

    def combine_pair(xs, _):
        s = xs * 2 + 1 - core
        r.pair[xs] = mm_tn(r.pcat[s], r.big3[s]).astype(BF16)
        return 0

    def combine_mine(xs, _):
        s = xs * 2 + core
        r.mine[xs] = mm_tn(r.pcat[s], r.big3[s]).astype(BF16)
        return 0

    lax.fori_loop(0, 4, combine_pair, 0)
    pair_copy = line_scatter_send_pair(r.pair, r.sib, r.s1, r.r1)
    lax.fori_loop(0, 4, combine_mine, 0)
    x_copies = line_scatter_send_x(r.mine, pair_copy, r.sib, r.inbox, r.s1, r.r1)
    teacher_load.wait()
    out = r.residual[...] + line_scatter_sum(r.mine, r.sib, r.inbox, x_copies)
    r.mixed[...] = out.astype(BF16)
    valid_row = r.vbuf[p, 0:1, :]
    valid_col = jnp.sum(jnp.where(eye, valid_row, 0.0), axis=1, keepdims=True)
    err = (out - r.gtok[...]) * valid_col
    r.gtok[...] = err
    r.low[...] = err.astype(BF16)
    r.rows[me] = r.low[...]
    err_gather = line_gather_start(r.low, lambda i: r.rows.at[i], r.s2, r.r2)
    square = jnp.sum(jnp.sum(err * err, axis=1, keepdims=True), axis=0, keepdims=True)
    count = jnp.sum(valid_row, axis=1, keepdims=True)
    r.stats[0:1, :] = jnp.broadcast_to(square, (1, 128))
    r.stats[1:2, :] = jnp.broadcast_to(count, (1, 128))
    for copy in [pair_copy] + x_copies:
        copy.wait_send()
    line_gather_finish(err_gather, lambda i: r.rows.at[i], r.s2, r.r2)

    def spread(s, _):
        r.big2[s] = mm(r.pcat[s], r.rows[s]).astype(BF16)
        return 0

    lax.fori_loop(0, 8, spread, 0)
    gather.drain()

    def store_grad(m, value):
        r.wg[m] = value.astype(BF16).reshape(2, 4, 2, 64, 512)

    def backward_act(e, _):
        g = r.gbuf[e].astype(F32)
        u = r.ubuf[e].astype(F32)
        sigma = jax.nn.sigmoid(g)
        silu = g * sigma
        gate = expert_rows(r.gslot, e)[:, 0:1]
        raw = mm(expert_rows(r.big2, e), weight(down(e)))
        act = silu * u
        dgate = jnp.sum(raw * act, axis=1, keepdims=True)
        r.gslot[:, slots_of(e), :] = jnp.broadcast_to(dgate, (512, 128)).reshape(8, 64, 128)
        r.big3[:, slots_of(e), 0:512] = (act * gate).astype(BF16).reshape(8, 64, 512)
        da = raw * gate
        r.gbuf[e] = (da * u * (sigma * (1.0 + g * (1.0 - sigma)))).astype(BF16)
        r.ubuf[e] = (da * silu).astype(BF16)
        return 0

    def backward_down(e, _):
        gated = r.big3[:, slots_of(e), 0:512].reshape(512, 512)
        store_grad(down(e), mm_tn(expert_rows(r.big2, e), gated))
        return 0

    def backward_in(e, _):
        dx = mm_nt(r.gbuf[e], weight(e)) + mm_nt(r.ubuf[e], weight(6 + e))
        r.big3[:, slots_of(e), :] = dx.astype(BF16).reshape(8, 64, 1024)
        return 0

    scatter = PlaneScatter(
        r.wg, r.far_in, (r.near_in_a, r.near_in_b), r.far2_in, r.near2_in, (r.stage_a, r.stage_b), r.load_sem, r.sw, r.rw
    )
    lax.fori_loop(0, 4, backward_act, 0)
    lax.fori_loop(0, 4, backward_down, 0)
    scatter.far(4)
    scatter.far(5)
    lax.fori_loop(0, 4, backward_in, 0)
    lax.fori_loop(0, 4, combine_pair, 0)
    pair_copy = line_scatter_send_pair(r.pair, r.sib, r.s3, r.r3)
    lax.fori_loop(0, 4, combine_mine, 0)

    def gate_rows(s, _):
        for e in range(4):
            hit = r.pcat[s, e * 64 : (e + 1) * 64, :].astype(F32)
            r.dgsend[s, e : e + 1, :] = jnp.sum(hit * r.gslot[s, e * 64 : (e + 1) * 64, :], axis=0, keepdims=True)
        return 0

    x_copies = line_scatter_send_x(r.mine, pair_copy, r.sib, r.inbox, r.s3, r.r3)
    lax.fori_loop(0, 8, gate_rows, 0)
    gate_copies = []
    for o in range(1, 8):
        to = lax.rem(me + o, 8)
        copy = remote(r.dgsend.at[to], r.dgates.at[me], r.s4.at[o], r.r4.at[o], (to, c, d))
        copy.start()
        gate_copies.append(copy)
    r.dgates[me] = r.dgsend[me]
    for e in range(4):
        rows = r.big1[:, 64 * e : 64 * e + 64, :].reshape(512, 1024)
        store_grad(e, mm_tn(rows, r.gbuf[e]))
        store_grad(6 + e, mm_tn(rows, r.ubuf[e]))
        scatter.far(e)
    wall_back = pltpu.make_async_copy(r.wall_keep, wall, r.keep_sem.at[1])
    wall_back.start()
    dmid = line_scatter_sum(r.mine, r.sib, r.inbox, x_copies)
    for copy in gate_copies:
        copy.wait()

    probs = r.probs[...]
    dprobs = jnp.concatenate([r.dgates[i, 0:4, :] for i in range(8)], axis=0) * r.picks[...]
    dlogits = probs * (dprobs - jnp.sum(probs * dprobs, axis=0, keepdims=True))
    high = dlogits.astype(BF16)
    r.dlog[0:32, :] = high
    r.dlog[32:64, :] = (dlogits - high.astype(F32)).astype(BF16)

    def router_back(i, _):
        at = pl.ds(pl.multiple_of(128 * i, 128), 128)
        part = mm(r.dlog[...], r.midl[:, at])
        r.smsend[i, 16:48, :] = part[:32] + part[32:]
        router = r.small_all[i, 16:48, :]
        r.dnorm[i] = mm_tn(r.dlog[...], jnp.concatenate([router, router], axis=0))
        return 0

    lax.fori_loop(0, 8, router_back, 0)
    gains = r.small_all[...].astype(F32)
    dmid = dmid + jnp.concatenate([r.dnorm[i] for i in range(8)], axis=1)
    res = r.residual[...]
    res_inv = inverse_rms(res)
    dgain_mid = jnp.sum(dmid * (res * res_inv), axis=0, keepdims=True)
    dres = r.gtok[...] + rms_back(res, res_inv, dmid * gain_row(gains, 2))
    r.gtok[...] = dres
    r.low[...] = dres.astype(BF16)

    def attended_back(t, _):
        both = mm_nt(r.low[...], r.wo_all[pl.ds(2 * t, 2)].reshape(256, 1024)).astype(BF16)
        for h in range(2):
            r.osend[2 * t + h] = both[:, 128 * h : 128 * h + 128]
        return 0

    lax.fori_loop(0, 4, attended_back, 0)
    r.dattbuf[c] = r.osend[c]
    d_copies = []
    for o in range(1, 8):
        to = lax.rem(c + o, 8)
        copy = remote(r.osend.at[to], r.dattbuf.at[c], r.sd.at[o], r.rd.at[o], (e_at, to, d))
        copy.start()
        d_copies.append(copy)
    r.rows[me] = r.low[...]
    branch_gather = line_gather_start(r.low, lambda i: r.rows.at[i], r.sb, r.rb)
    for copy in spread_copies:
        copy.wait()
    for copy in d_copies:
        copy.wait_recv()
    scatter.near_out(4)
    scatter.near_out(5)

    def prepare_back(b, _):
        tile = r.dattbuf[b].astype(F32)
        r.dop[b] = stack_heads(tile, True).astype(BF16)
        both = tile * r.oheads[b]
        first = jnp.sum(jnp.where(lo, both, 0.0), axis=1, keepdims=True)
        second = jnp.sum(jnp.where(lo, 0.0, both), axis=1, keepdims=True)
        delta = jnp.concatenate([first, second], axis=0)
        lane = lax.broadcasted_iota(jnp.int32, (256, 128), 1)
        r.lse[b] = jnp.where(lane < 64, r.lse[b], delta)
        r.gslot[b] = jnp.zeros((256, 128), F32)
        return 0

    lax.fori_loop(0, 8, prepare_back, 0)

    def key_block(k, _):
        block = key_rows(r.kvbuf, k)
        bias = key_bias(r.vbuf, k)

        def one(b, acc, scores):
            weights = jnp.exp(scores - r.lse[b][:, 0:1])
            dweights = mm_nt(r.dop[b], block)
            dscores = (weights * (dweights - r.lse[b][:, 64:65])).astype(BF16)
            r.gslot[b] = r.gslot[b] + mm(dscores, block)
            return acc + mm_tn(weights.astype(BF16), r.dop[b]) + mm_tn(dscores, r.qpad[b])

        def edge(b, acc):
            return one(b, acc, mask_last(mm_nt(r.qpad[b], block), bias, b, d))

        acc = lax.fori_loop(2 * k, 2 * k + 2, edge, jnp.zeros((512, 128), F32))
        acc = lax.fori_loop(2 * k + 2, 8, lambda b, acc: one(b, acc, mm_nt(r.qpad[b], block) + bias), acc)
        r.dkvsend[pl.ds(4 * k, 4)] = acc.astype(BF16).reshape(4, 128, 128)
        for h in range(2):
            b = 2 * k + h
            done = r.gslot[b] * SCALE
            r.sendq[b] = jnp.where(lo, done[:128], pltpu.roll(done[128:], 64, 1)).astype(BF16)

            @pl.when(b != c)
            def _():
                remote(r.sendq.at[b], r.qbuf.at[c], r.sdq.at[b], r.rdq.at[c], (e_at, b, d)).start()
                for g in range(2):
                    to = 2 * b + g
                    remote(r.dkvsend.at[to], r.dkvbuf.at[p], r.sdkv.at[to], r.rdkv.at[p], (e_at, b, g)).start()

            @pl.when(b == c)
            def _():
                r.qbuf[c] = r.sendq[c]
                r.dkvbuf[p] = r.dkvsend[p]
                to = c * 2 + 1 - d
                remote(r.dkvsend.at[to], r.dkvbuf.at[p], r.sdkv.at[to], r.rdkv.at[p], (e_at, c, 1 - d)).start()

        return 0

    lax.fori_loop(0, 1, key_block, 0)
    scatter.near_out(0)
    lax.fori_loop(1, 4, key_block, 0)
    line_gather_finish(branch_gather, lambda i: r.rows.at[i], r.sb, r.rb)

    def wait_dq(i, _):
        b = lax.rem(c + 1 + i, 8)
        copy = remote(r.sendq.at[b], r.qbuf.at[b], r.sdq.at[b], r.rdq.at[b], (e_at, b, d))
        copy.wait_send()
        copy.wait_recv()
        return 0

    def wait_dkv(i, _):
        q = lax.rem(p + 1 + i, 16)
        copy = remote(
            r.dkvsend.at[q], r.dkvbuf.at[q], r.sdkv.at[q], r.rdkv.at[q], (e_at, lax.div(q, 2), lax.rem(q, 2))
        )
        copy.wait_send()
        copy.wait_recv()
        return 0

    lax.fori_loop(0, 7, wait_dq, 0)
    lax.fori_loop(0, 15, wait_dkv, 0)
    cos, sin = r.cosine[...], -r.sine[...]
    dq_tiles = []
    for t in range(8):
        tile = r.qbuf[t].astype(F32)
        dq_tiles.append(tile * cos + swap_halves(tile) * sin)
    dq = jnp.concatenate(dq_tiles, axis=1)
    q_pre = r.qpre[...]
    q_inv = inverse_rms(q_pre)
    dgain_q = jnp.sum(dq * (q_pre * q_inv), axis=0, keepdims=True)
    r.dqkv[0:128, :] = rms_back(q_pre, q_inv, dq * gain_row(gains, 1)).astype(BF16)
    dk_tiles, dv_tiles = [], []
    for t in range(4):
        even = r.dkvbuf[4 * t].astype(F32) + r.dkvbuf[4 * t + 1].astype(F32)
        odd = r.dkvbuf[4 * t + 2].astype(F32) + r.dkvbuf[4 * t + 3].astype(F32)
        tile = jnp.where(lo, even, pltpu.roll(odd, 64, 1))
        dk_tiles.append(tile * cos + swap_halves(tile) * sin)
        dv_tiles.append(jnp.where(lo, pltpu.roll(even, 64, 1), odd))
    dk = jnp.concatenate(dk_tiles, axis=1)
    k_pre = r.kpre[...]
    k_inv = inverse_rms(k_pre)
    dgain_k = jnp.sum(dk * (k_pre * k_inv), axis=0, keepdims=True)
    r.dqkv[128:256, 0:512] = rms_back(k_pre, k_inv, dk * key_gain_row(gains)).astype(BF16)
    r.dqkv[128:256, 512:1024] = jnp.concatenate(dv_tiles, axis=1).astype(BF16)
    r.big3[me] = r.dqkv[...]
    dqkv_gather = line_gather_start(r.dqkv, lambda i: r.big3.at[i], r.sn, r.rn)
    for j in range(1, 4):
        scatter.near_out(j)

    def out_grad(t, _):
        at = pl.ds(pl.multiple_of(512 * t, 512), 512)
        tiles = mm_tn(r.attx[...].reshape(1024, 128), r.rows[:, :, at].reshape(1024, 512)).astype(BF16)
        for i in range(4):
            r.pieces_o[pl.ds(8 * t + 2 * i, 2)] = tiles[:, 128 * i : 128 * i + 128].reshape(2, 64, 128)
        return 0

    lax.fori_loop(0, 2, out_grad, 0)
    p_copies_o = plane_sum_send(r.pieces_o, 1, r.pin_o, r.sp1, r.rp1)
    wall_back.wait()

    def normed_back(t, _):
        for i in range(2):
            part = slice(128 * i, 128 * i + 128)
            both = mm_nt(r.dqkv[part, :], wall[pl.ds(2 * t, 2), part, :].reshape(256, 1024))
            for h in range(2):
                tile = both[:, 128 * h : 128 * h + 128]
                r.dnorm[2 * t + h] = tile if i == 0 else r.dnorm[2 * t + h] + tile
        return 0

    lax.fori_loop(0, 4, normed_back, 0)
    dnormed = jnp.concatenate([r.dnorm[t] for t in range(8)], axis=1)
    values = r.tokens[...].astype(F32)
    inv = inverse_rms(values)
    dgain_in = jnp.sum(dnormed * (values * inv), axis=0, keepdims=True)
    r.gtok[...] = r.gtok[...] + rms_back(values, inv, dnormed * gain_row(gains, 0))
    for i in range(8):
        at = slice(128 * i, 128 * i + 128)
        r.smsend[i, 0:1, :] = dgain_in[:, at]
        r.smsend[i, 1:2, :] = dgain_q[:, at]
        r.smsend[i, 2:3, :] = dgain_mid[:, at]
        half = dgain_k[:, 128 * (i // 2) : 128 * (i // 2) + 128]
        r.smsend[i, 3:4, :] = half if i % 2 == 0 else pltpu.roll(jnp.broadcast_to(half, (8, 128)), 64, 1)[0:1]
        r.smsend[i, 4:6, :] = r.stats[0:2, :]
        r.smsend[i, 6:16, :] = jnp.zeros((10, 128), F32)
    sm_copies = []
    for o in range(1, 8):
        to = lax.rem(me + o, 8)
        copy = remote(r.smsend.at[to], r.sminbox.at[o], r.sms.at[o], r.rms.at[o], (to, c, d))
        copy.start()
        sm_copies.append(copy)
    for j in (4, 5, 0):
        scatter.near_sum(j)
    shares_o = plane_sum_share(p_copies_o, r.pieces_o, 1, r.pin_o, r.res_o, r.sp2, r.rp2)

    total = r.smsend[me]
    for at, copy in enumerate(sm_copies):
        copy.wait_recv()
        total = total + r.sminbox[at + 1]
    r.smsum[...] = total
    small_copies = []
    for o in range(1, 16):
        _, device = plane_peer(o)
        copy = remote(r.smsum, r.smplane.at[o], r.sp5.at[o], r.rp5.at[o], device)
        copy.start()
        small_copies.append(copy)
    line_gather_finish(dqkv_gather, lambda i: r.big3.at[i], r.sn, r.rn)

    def qkv_grad(t, _):
        at = pl.ds(pl.multiple_of(512 * lax.rem(t, 2), 512), 512)
        part = pl.ds(pl.multiple_of(128 * lax.div(t, 2), 128), 128)
        tiles = mm_tn(r.nx[...].reshape(1024, 128), r.big3[:, part, at].reshape(1024, 512)).astype(BF16)
        for i in range(4):
            r.pieces_n[pl.ds(8 * t + 2 * i, 2)] = tiles[:, 128 * i : 128 * i + 128].reshape(2, 64, 128)
        return 0

    lax.fori_loop(0, 4, qkv_grad, 0)
    p_copies_n = plane_sum_send(r.pieces_n, 2, r.pin_n, r.sp3, r.rp3)
    for j in range(1, 4):
        scatter.near_sum(j)
    scatter.far2()
    for copy in shares_o:
        copy.wait_recv()
    scatter.near2()
    shares_n = plane_sum_share(p_copies_n, r.pieces_n, 2, r.pin_n, r.res_n, r.sp4, r.rp4)
    for at, copy in enumerate(small_copies):
        copy.wait_recv()
        total = total + r.smplane[at + 1]
    r.gsmall[...] = total
    scatter.finish(r.gw)
    for copy in shares_n:
        copy.wait_recv()
    scatter.drain()
    for copy in (
        [pair_copy] + x_copies + d_copies + sm_copies
        + small_copies + p_copies_o + p_copies_n + shares_o + shares_n
    ):
        copy.wait_send()


def layer(*args):
    vm = pl.BlockSpec(memory_space=pltpu.VMEM)
    hbm = pl.BlockSpec(memory_space=pl.ANY)
    in_hbm = ("wq", "wk", "wv", "wo", "teacher")
    return pl.pallas_call(
        layer_kernel,
        out_shape=tuple(jax.ShapeDtypeStruct(shape, dtype) for _, shape, dtype in OUTPUTS + SPILLS),
        in_specs=[hbm if name in in_hbm else vm for name in INPUTS],
        out_specs=(vm,) * len(OUTPUTS) + (hbm,) * len(SPILLS),
        scratch_shapes=[pltpu.VMEM(shape, dtype) for _, shape, dtype in SCRATCH]
        + [pltpu.SemaphoreType.DMA((count,)) for _, count in SEMAPHORES],
        compiler_params=pltpu.CompilerParams(
            collective_id=0, has_side_effects=True, vmem_limit_bytes=64 << 20
        ),
        cost_estimate=pl.CostEstimate(flops=32 * 10**9, bytes_accessed=60 << 20, transcendentals=8 << 20),
        name="layer",
    )(*args)[: len(OUTPUTS)]


def finish_kernel(
    mixed, gtok, res_o_in, res_n_in, small_in, gw_in,
    mixed_out, loss, gtok_out, gnorm_in, gq, gk, gv, gq_gain, gk_gain, gout, gnorm_mid, grouter, ggate, gup, gdown,
    res_o, res_n, small, gw, sems,
):
    pairs = ((small_in, small), (res_o_in, res_o), (res_n_in, res_n), (gw_in, gw), (mixed, mixed_out), (gtok, gtok_out))
    copies = [pltpu.make_async_copy(src, dst, sems.at[i]) for i, (src, dst) in enumerate(pairs)]
    for copy in copies:
        copy.start()
    copies[0].wait()
    loss[...] = small[4:5, 0:1] / (small[5:6, 0:1] * 1024.0)
    gnorm_in[...] = small[0:1, :]
    gq_gain[...] = small[1:2, :]
    gnorm_mid[...] = small[2:3, :]
    gk_gain[...] = small[3:4, 0:64]
    grouter[...] = small[16:48, :]

    def tiles(ref, out, first, count):
        for t in range(count):
            n = 2 * (first + t)
            out[:, 128 * t : 128 * t + 128] = jnp.concatenate([ref[n], ref[n + 1]], axis=0).astype(F32)

    copies[1].wait()
    tiles(res_o, gout, 0, 8)
    copies[2].wait()
    tiles(res_n, gq, 0, 8)
    tiles(res_n, gk, 8, 4)
    tiles(res_n, gv, 12, 4)
    copies[3].wait()
    for e in range(4):
        ggate[:, e, :] = gw[e]
        gup[:, e, :] = gw[6 + e]
        gdown[:, e, :] = gw[4 + e + 4 * (e // 2)]
    for copy in copies[4:]:
        copy.wait()


def finish(*args):
    vm = pl.BlockSpec(memory_space=pltpu.VMEM)
    hbm = pl.BlockSpec(memory_space=pl.ANY)
    shapes = (
        (128, 1024), (1, 1), (128, 1024), (1, 128), (128, 1024), (128, 512), (128, 512), (1, 128), (1, 64), (128, 1024),
        (1, 128), (32, 128), (64, 4, 512), (64, 4, 512), (64, 4, 512),
    )
    return pl.pallas_call(
        finish_kernel,
        out_shape=tuple(jax.ShapeDtypeStruct(v, BF16 if i == 0 else F32) for i, v in enumerate(shapes)),
        in_specs=[hbm] * 6,
        out_specs=(vm,) * len(shapes),
        scratch_shapes=[
            pltpu.VMEM((16, 64, 128), BF16),
            pltpu.VMEM((32, 64, 128), BF16),
            pltpu.VMEM((48, 128), F32),
            pltpu.VMEM((12, 64, 512), F32),
            pltpu.SemaphoreType.DMA((6,)),
        ],
        compiler_params=pltpu.CompilerParams(vmem_limit_bytes=62 << 20),
        name="finish",
    )(*args)


def per_device(
    tokens,
    norm_in,
    w_query,
    w_key,
    w_value,
    query_gain,
    key_gain,
    w_out,
    norm_mid,
    w_router,
    expert_gate,
    expert_up,
    expert_down,
    routes,
    valid,
    teacher,
):
    positions = (lax.axis_index("ctx") * 2 + lax.axis_index("dp")) * 128 + jnp.arange(128, dtype=jnp.int32)
    lane = jnp.arange(128, dtype=jnp.int32)
    frequency = THETA ** (-((lane % 32).astype(F32) * (2.0 / HEAD)))
    angles = positions.astype(F32)[:, None] * frequency[None, :]
    sign = jnp.where(lane % 64 < 32, -1.0, 1.0)
    parts = layer(
        tokens, w_query, w_key, w_value, w_out, norm_in, query_gain, norm_mid, key_gain, w_router.T,
        expert_gate, expert_up, expert_down, valid, jnp.cos(angles), jnp.sin(angles) * sign, routes.T, teacher,
    )
    (
        mixed, loss, gtok, gnorm_in, gq, gk, gv, gq_gain, gk_gain, gout, gnorm_mid, grouter, ggate, gup, gdown
    ) = finish(*parts)
    return (
        mixed, loss.reshape(()), gtok, gnorm_in.reshape(128), gq, gk, gv, gq_gain.reshape(128), gk_gain.reshape(64), gout,
        gnorm_mid.reshape(128), grouter.T, ggate, gup, gdown,
    )


def solution(mesh):
    placed = (
        P(("expert", "ctx", "dp"), None),
        P("expert"),
        P("expert", None),
        P("expert", None),
        P("expert", None),
        P("expert"),
        P("expert"),
        P("expert", None),
        P("expert"),
        P("expert", None),
        P(("ctx", "dp"), "expert", None),
        P(("ctx", "dp"), "expert", None),
        P(("ctx", "dp"), "expert", None),
        P(("expert", "ctx", "dp"), None),
        P(("expert", "ctx", "dp")),
        P(("expert", "ctx", "dp"), None),
    )
    return jax.shard_map(
        per_device,
        mesh=mesh,
        in_specs=placed,
        out_specs=(
            P(("expert", "ctx", "dp"), None),
            P(),
            P(("expert", "ctx", "dp"), None),
            P("expert"),
            P("expert", None),
            P("expert", None),
            P("expert", None),
            P("expert"),
            P("expert"),
            P("expert", None),
            P("expert"),
            P("expert", None),
            P(("ctx", "dp"), "expert", None),
            P(("ctx", "dp"), "expert", None),
            P(("ctx", "dp"), "expert", None),
        ),
        check_vma=False,
    )
```

time: 1440 us -> 293 us (0.20)
  waiting for transfers between devices: 642 us -> 0 us
  blocking collectives: 388 us -> 0 us
  Pallas kernels: 0 us -> 290 us
  local copies, waits for them, and re-layouts: 152 us -> 0 us
  matrix products: 128 us -> 0 us
  other arithmetic: 72.2 us -> 0.98 us
  between operations: 21 us -> 0.87 us
  starting transfers between devices: 14.6 us -> 0 us
    all_gather x9 -> x0, waiting for transfers between devices: 292 us -> none  [the longest x1 91.5 us: per_device(): lax.all_gather(expert_up, ('ctx', 'dp'), axis=0, tiled=True)]
    pallas_call x0 -> x2, Pallas kernels: none -> 290 us  [the longest x1 286 us: layer(): pl.pallas_call(layer_kernel, out_shape=tuple((jax.ShapeDtypeStruct(shape,...]
    reduce_scatter x6 -> x0, waiting for transfers between devices: 228 us -> none  [the longest x1 77 us: per_device(): lax.psum_scatter(d_values_all.reshape(seq_len, kv_width).astype(jnp.bfloa...]
    psum x2 -> x0, blocking collectives: 129 us -> none  [the longest x1 69.5 us: per_device(): lax.psum((jnp.sum(err * err), jnp.sum(valid.astype(jnp.float32))), ('expe...]
    dot_general x52 -> x0, matrix products: 128 us -> none  [the longest x8 14.3 us: block_scores(): jnp.einsum('tkgd,skd->kgts', query_grouped, keys_part, preferred_element_...]
    all_gather x5 -> x0, blocking collectives: 123 us -> none  [the longest x1 54.6 us: per_device(): lax.all_gather(w_router, 'expert', axis=0, tiled=True)]
    all_to_all x2 -> x0, blocking collectives: 111 us -> none  [the longest x1 58.2 us: per_device(): lax.all_to_all(send_rows, 'expert', split_axis=0, concat_axis=2, tiled=True)]
    psum x1 -> x0, waiting for transfers between devices: 73.9 us -> none  [per_device(): lax.psum(grads[1].astype(jnp.bfloat16), ('ctx', 'dp')).astype(jnp.float32)]
  transfers between devices with their start and end apart: 19 -> 0, of which waited for: 14 -> 0; matrix products, arithmetic and copies ran while one was open for 14% -> 0% of each run, Pallas kernels for 0% -> 0%
where the time goes in v3:
time: 293 us; the launch traced here: 292 us
  Pallas kernels  290 us (99%)
    pallas_call x1, Pallas kernels, layer(): pl.pallas_call(layer_kernel, out_shape=tuple((jax.ShapeDtypeStruct(shape,...  286 us

profile of v3, /device:TPU:1, one launch (start us, length us, event | category | flops | bytes accessed | tf_op | source)
XLA Modules:
  0.0 292.2 jit_solution(14762947375467448677)
XLA Ops:
  0.7 1.0 fusion
  1.6 286.4 %layer.1 = (bf16[128,1024]{1,0:T(8,128)(2,1)}, f32[128,1024]{1,0:T(8,128)}, bf16[16,64,128]{2,1,0:T(8,128)(2,1)}, bf16[32,64,128]{2,1,0:T(8,128)(2,1)}, f32[48,1...) custom-call(bf16[128,1024]{1,0:T(8,128)(2,1)} %refs_0_.1, ...), custom_call_target="tpu_custom_call" | custom-call | flops 32000000000 | bytes 62914560 | tf_op jit(solution)/shard_map/layer/pallas_call | solution.py:1112
  288.1 4.0 %finish.1 = (bf16[128,1024]{1,0:T(8,128)(2,1)}, f32[1,1]{1,0:T(1,128)}, f32[128,1024]{1,0:T(8,128)}, f32[1,128]{1,0:T(1,128)}, f32[128,1024]{1,0:T(8,128)}, /*in...) custom-call(bf16[128,1024]{1,0:T(8,128)(2,1)} %get-tuple-element.36., ...), custom_call_target="tpu_custom_call" | custom-call | tf_op jit(solution)/shard_map/finish/pallas_call | solution.py:1171
  (2 shorter events, 0.0 us)

commit v4 on v3

--- a/solution.py
+++ b/solution.py
@@ -80,45 +80,56 @@
     return copies
 
 
-def line_gather_finish(copies, buf, send, recv):
+def line_gather_finish(copies, buf, send, recv, use=None):
     x, core, _, _ = places()
+
+    def used(o, c):
+        if use is not None:
+            use(lax.rem(x - o + 4, 4) * 2 + c)
+
+    used(0, core)
+    copies[3].wait_recv()
+    used(0, 1 - core)
     forwards = []
     for at, o in ((1, 1), (2, 3), (0, 2)):
         copies[at].wait_recv()
         block = buf(lax.rem(x - o + 4, 4) * 2 + core)
         copy = remote(block, block, send.at[4 + o], recv.at[4 + o], line_device(x, 1 - core))
         copy.start()
-        forwards.append(copy)
-    copies[3].wait_recv()
-    for copy in forwards:
+        forwards.append((copy, o))
+        used(o, core)
+    for copy, o in forwards:
         copy.wait_recv()
-    for copy in copies + forwards:
+        used(o, 1 - core)
+    for copy in copies + [copy for copy, _ in forwards]:
         copy.wait_send()
 
 
-def line_scatter_send_pair(pair, sib, send, recv):
+def line_scatter(part, mine, pair, sib, inbox, send, recv):
     x, core, _, _ = places()
-    copy = remote(pair, sib, send.at[0], recv.at[0], line_device(x, 1 - core))
-    copy.start()
-    return copy
-
-
-def line_scatter_send_x(mine, pair_copy, sib, inbox, send, recv):
-    x, core, _, _ = places()
-    pair_copy.wait_recv()
-    copies = []
-    for o in (2, 1, 3):
-        to = lax.rem(x + o, 4)
-        mine[to] = (mine[to].astype(F32) + sib[to].astype(F32)).astype(mine.dtype)
-        copy = remote(mine.at[to], inbox.at[o - 1], send.at[o], recv.at[o], line_device(x + o, core))
+    copies, order = [], (2, 1, 3, 0)
+    for o in order:
+        at = lax.rem(x + o, 4)
+        pair[at] = part(at * 2 + 1 - core).astype(BF16)
+        copy = remote(pair.at[at], sib.at[at], send.at[o], recv.at[o], line_device(x, 1 - core))
         copy.start()
         copies.append(copy)
-    return copies
-
-
-def line_scatter_sum(mine, sib, inbox, copies):
+    out = []
+    for n, o in enumerate(order):
+        at = lax.rem(x + o, 4)
+        own = part(at * 2 + core)
+        copies[n].wait_recv()
+        mine[at] = (own + sib[at].astype(F32)).astype(BF16)
+        if o > 0:
+            copy = remote(mine.at[at], inbox.at[o - 1], send.at[4 + o], recv.at[4 + o], line_device(x + o, core))
+            copy.start()
+            out.append(copy)
+    return copies, out
+
+
+def line_scatter_sum(mine, inbox, copies):
     x, _, _, _ = places()
-    total = mine[x].astype(F32) + sib[x].astype(F32)
+    total = mine[x].astype(F32)
     for at, o in ((1, 1), (2, 3), (0, 2)):
         copies[at].wait_recv()
         total = total + inbox[o - 1].astype(F32)
@@ -416,7 +427,8 @@
     ("mixed", (128, 1024), BF16),
     ("gtok", (128, 1024), F32),
     ("res_o", (16, 64, 128), BF16),
-    ("res_n", (32, 64, 128), BF16),
+    ("res_q", (16, 64, 128), BF16),
+    ("res_n", (16, 64, 128), BF16),
     ("gsmall", (48, 128), F32),
     ("gw", (12, 64, 512), F32),
 )
@@ -483,19 +495,21 @@
     ("smplane", (16, 48, 128), F32),
     ("pieces_o", (16, 64, 128), BF16),
     ("pin_o", (16, 1, 64, 128), BF16),
-    ("pieces_n", (32, 64, 128), BF16),
-    ("pin_n", (16, 2, 64, 128), BF16),
+    ("pieces_q", (16, 64, 128), BF16),
+    ("pin_q", (16, 1, 64, 128), BF16),
+    ("pieces_n", (16, 64, 128), BF16),
+    ("pin_n", (16, 1, 64, 128), BF16),
 )
 SEMAPHORES = (
     ("own_sem", 6), ("keep_sem", 2), ("teacher_sem", 1), ("load_sem", 4),
-    ("ssm", 8), ("rsm", 8), ("sqkv", 8), ("rqkv", 8), ("swo", 8), ("rwo", 8), ("sv", 16), ("rv", 16),
+    ("ssm", 8), ("rsm", 8), ("skvw", 8), ("rkvw", 8), ("sqw", 8), ("rqw", 8), ("swo", 8), ("rwo", 8), ("sv", 16), ("rv", 16),
     ("sew", 56), ("rew", 56), ("snx", 8), ("rnx", 8), ("sax", 8), ("rax", 8),
     ("skv", 16), ("rkv", 16), ("sq", 8), ("rq", 8), ("so", 8), ("ro", 8), ("sx", 8), ("rx", 8), ("sm", 8), ("rm", 8),
-    ("s1", 4), ("r1", 4), ("s2", 8), ("r2", 8), ("s3", 4), ("r3", 4), ("s4", 8), ("r4", 8),
+    ("s1", 8), ("r1", 8), ("s2", 8), ("r2", 8), ("s3", 8), ("r3", 8), ("s4", 8), ("r4", 8),
     ("sw", 56), ("rw", 56), ("sd", 8), ("rd", 8), ("sdq", 8), ("rdq", 8), ("sdkv", 16), ("rdkv", 16),
-    ("sb", 8), ("rb", 8), ("sn", 8), ("rn", 8), ("sms", 8), ("rms", 8),
+    ("sb", 8), ("rb", 8), ("sn", 8), ("rn", 8), ("sn2", 8), ("rn2", 8), ("sms", 8), ("rms", 8),
     ("sp1", 16), ("rp1", 16), ("sp2", 16), ("rp2", 16), ("sp3", 16), ("rp3", 16), ("sp4", 16), ("rp4", 16),
-    ("sp5", 16), ("rp5", 16),
+    ("sp5", 16), ("rp5", 16), ("sp6", 16), ("rp6", 16), ("sp7", 16), ("rp7", 16),
 )
 NAMES = INPUTS + tuple(n for part in (OUTPUTS, SPILLS, SCRATCH, SEMAPHORES) for n, *_ in part)
 
@@ -533,7 +547,9 @@
     small_gather = line_gather_start(r.small_all.at[me], lambda i: r.small_all.at[i], r.ssm, r.rsm)
     for copy in own[:3]:
         copy.wait()
-    qkv_gather = line_gather_start(wall.at[me], lambda i: wall.at[i], r.sqkv, r.rqkv)
+    kv_part, q_part = pl.ds(128, 128), pl.ds(0, 128)
+    kv_gather = line_gather_start(wall.at[me, kv_part], lambda i: wall.at[i, kv_part], r.skvw, r.rkvw)
+    q_gather = line_gather_start(wall.at[me, q_part], lambda i: wall.at[i, q_part], r.sqw, r.rqw)
     for ref, first in ((r.expert_gate, (0, 1, 2, 3)), (r.expert_up, (6, 7, 8, 9)), (r.expert_down, (4, 5, 10, 11))):
         whole = ref[...].astype(F32)
         for e, m in enumerate(first):
@@ -563,17 +579,11 @@
         spread_copies.append(copy)
     gather.shards_on()
     gather.shards_wait()
-    for j in range(2):
-        gather.lines(j)
-
-    line_gather_finish(qkv_gather, lambda i: wall.at[i], r.sqkv, r.rqkv)
-    for j in range(2):
-        gather.lines_on(j)
-    q_pre = mm(normed, wall[:, 0:128, :].reshape(1024, 1024))
+
+    line_gather_finish(kv_gather, lambda i: wall.at[i, kv_part], r.skvw, r.rkvw)
     kv_pre = mm(normed, wall[:, 128:256, :].reshape(1024, 1024))
     k_pre = kv_pre[:, 0:512]
     v_low = kv_pre[:, 512:1024].astype(BF16).astype(F32)
-    r.qpre[...] = q_pre
     r.kpre[...] = k_pre
     cos, sin = r.cosine[...], r.sine[...]
     kn = k_pre * inverse_rms(k_pre) * key_gain_row(gains)
@@ -590,6 +600,11 @@
         copy = remote(r.dkvsend.at[lax.div(q, 2)], r.kvbuf.at[p], r.skv.at[o], r.rkv.at[o], device)
         copy.start()
         kv_copies.append(copy)
+    for j in range(2):
+        gather.lines(j)
+    line_gather_finish(q_gather, lambda i: wall.at[i, q_part], r.sqw, r.rqw)
+    q_pre = mm(normed, wall[:, 0:128, :].reshape(1024, 1024))
+    r.qpre[...] = q_pre
     qn = q_pre * inverse_rms(q_pre) * gain_row(gains, 1)
     for t in range(8):
         tile = qn[:, 128 * t : 128 * t + 128]
@@ -603,9 +618,11 @@
         q_copies.append(copy)
     keep = pltpu.make_async_copy(wall, r.wall_keep, r.keep_sem.at[0])
     keep.start()
+    for j in range(2):
+        gather.lines_on(j)
+    gather.lines(2)
     for copy in valid_copies + kv_copies + q_copies:
         copy.wait()
-    gather.lines(2)
 
     def prepare(b, _):
         r.qpad[b] = (stack_heads(r.qbuf[b].astype(F32), False) * SCALE).astype(BF16)
@@ -665,8 +682,8 @@
         return 0
 
     lax.fori_loop(0, 7, wait_rest, 0)
-    for j in range(3, 6):
-        gather.lines(j)
+    gather.lines(3)
+    gather.lines(4)
     r.attx[me] = r.att[me]
     for o in range(1, 8):
         to = lax.rem(me + o, 8)
@@ -706,14 +723,14 @@
         copy.start()
         meta_copies.append(copy)
     gather.lines_on(3)
-    line_gather_finish(mid_gather, lambda i: r.rows.at[i], r.sx, r.rx)
+    gather.lines(5)
     for copy in meta_copies:
         copy.wait()
     keep.wait()
 
     slot_ids = lax.broadcasted_iota(jnp.int32, (64, 128), 0).astype(F32)
 
-    def compact(s, _):
+    def compact(s):
         for e in range(4):
             hit = slot_ids == r.meta[s, 4 + e : 5 + e, :]
             at = slice(e * 64, (e + 1) * 64)
@@ -721,11 +738,9 @@
             gate = jnp.sum(jnp.where(hit, r.meta[s, e : e + 1, :], 0.0), axis=1, keepdims=True)
             r.gslot[s, at, :] = jnp.broadcast_to(gate, (64, 128))
         r.big1[s] = mm(r.pcat[s], r.rows[s]).astype(BF16)
-        return 0
-
-    lax.fori_loop(0, 8, compact, 0)
+
+    line_gather_finish(mid_gather, lambda i: r.rows.at[i], r.sx, r.rx, compact)
     gather.lines_on(4)
-    gather.lines_on(5)
 
     def slots_of(e):
         return pl.ds(pl.multiple_of(e * 64, 64), 64)
@@ -751,29 +766,22 @@
         r.big3[:, slots_of(e), :] = (mm_nt(act, weight(down(e))) * gate).astype(BF16).reshape(8, 64, 1024)
         return 0
 
-    for j in range(4):
-        gather.lines_wait(j)
-    lax.fori_loop(0, 4, forward_in, 0)
-    for j in range(4, 6):
-        gather.lines_wait(j)
-    lax.fori_loop(0, 4, forward_out, 0)
-
-    def combine_pair(xs, _):
-        s = xs * 2 + 1 - core
-        r.pair[xs] = mm_tn(r.pcat[s], r.big3[s]).astype(BF16)
-        return 0
-
-    def combine_mine(xs, _):
-        s = xs * 2 + core
-        r.mine[xs] = mm_tn(r.pcat[s], r.big3[s]).astype(BF16)
-        return 0
-
-    lax.fori_loop(0, 4, combine_pair, 0)
-    pair_copy = line_scatter_send_pair(r.pair, r.sib, r.s1, r.r1)
-    lax.fori_loop(0, 4, combine_mine, 0)
-    x_copies = line_scatter_send_x(r.mine, pair_copy, r.sib, r.inbox, r.s1, r.r1)
+    for e in range(4):
+        if e == 1:
+            gather.lines_on(5)
+        gather.lines_wait(e)
+        forward_in(e, 0)
+    for e in range(4):
+        if e % 2 == 0:
+            gather.lines_wait(4 + e // 2)
+        forward_out(2 * (e % 2) + e // 2, 0)
+
+    def combine(s):
+        return mm_tn(r.pcat[s], r.big3[s])
+
+    pair_copies, x_copies = line_scatter(combine, r.mine, r.pair, r.sib, r.inbox, r.s1, r.r1)
     teacher_load.wait()
-    out = r.residual[...] + line_scatter_sum(r.mine, r.sib, r.inbox, x_copies)
+    out = r.residual[...] + line_scatter_sum(r.mine, r.inbox, x_copies)
     r.mixed[...] = out.astype(BF16)
     valid_row = r.vbuf[p, 0:1, :]
     valid_col = jnp.sum(jnp.where(eye, valid_row, 0.0), axis=1, keepdims=True)
@@ -786,15 +794,13 @@
     count = jnp.sum(valid_row, axis=1, keepdims=True)
     r.stats[0:1, :] = jnp.broadcast_to(square, (1, 128))
     r.stats[1:2, :] = jnp.broadcast_to(count, (1, 128))
-    for copy in [pair_copy] + x_copies:
+    for copy in pair_copies + x_copies:
         copy.wait_send()
-    line_gather_finish(err_gather, lambda i: r.rows.at[i], r.s2, r.r2)
-
-    def spread(s, _):
+
+    def spread(s):
         r.big2[s] = mm(r.pcat[s], r.rows[s]).astype(BF16)
-        return 0
-
-    lax.fori_loop(0, 8, spread, 0)
+
+    line_gather_finish(err_gather, lambda i: r.rows.at[i], r.s2, r.r2, spread)
     gather.drain()
 
     def store_grad(m, value):
@@ -834,9 +840,7 @@
     scatter.far(4)
     scatter.far(5)
     lax.fori_loop(0, 4, backward_in, 0)
-    lax.fori_loop(0, 4, combine_pair, 0)
-    pair_copy = line_scatter_send_pair(r.pair, r.sib, r.s3, r.r3)
-    lax.fori_loop(0, 4, combine_mine, 0)
+    pair_copies, x_copies = line_scatter(combine, r.mine, r.pair, r.sib, r.inbox, r.s3, r.r3)
 
     def gate_rows(s, _):
         for e in range(4):
@@ -844,7 +848,6 @@
             r.dgsend[s, e : e + 1, :] = jnp.sum(hit * r.gslot[s, e * 64 : (e + 1) * 64, :], axis=0, keepdims=True)
         return 0
 
-    x_copies = line_scatter_send_x(r.mine, pair_copy, r.sib, r.inbox, r.s3, r.r3)
     lax.fori_loop(0, 8, gate_rows, 0)
     gate_copies = []
     for o in range(1, 8):
@@ -860,7 +863,7 @@
         scatter.far(e)
     wall_back = pltpu.make_async_copy(r.wall_keep, wall, r.keep_sem.at[1])
     wall_back.start()
-    dmid = line_scatter_sum(r.mine, r.sib, r.inbox, x_copies)
+    dmid = line_scatter_sum(r.mine, r.inbox, x_copies)
     for copy in gate_copies:
         copy.wait()
 
@@ -905,12 +908,12 @@
         d_copies.append(copy)
     r.rows[me] = r.low[...]
     branch_gather = line_gather_start(r.low, lambda i: r.rows.at[i], r.sb, r.rb)
+    scatter.near_out(4)
+    scatter.near_out(5)
     for copy in spread_copies:
         copy.wait()
     for copy in d_copies:
         copy.wait_recv()
-    scatter.near_out(4)
-    scatter.near_out(5)
 
     def prepare_back(b, _):
         tile = r.dattbuf[b].astype(F32)
@@ -997,6 +1000,8 @@
     q_inv = inverse_rms(q_pre)
     dgain_q = jnp.sum(dq * (q_pre * q_inv), axis=0, keepdims=True)
     r.dqkv[0:128, :] = rms_back(q_pre, q_inv, dq * gain_row(gains, 1)).astype(BF16)
+    r.big3[me, 0:128, :] = r.dqkv[0:128, :]
+    dq_gather = line_gather_start(r.dqkv.at[q_part], lambda i: r.big3.at[i, q_part], r.sn, r.rn)
     dk_tiles, dv_tiles = [], []
     for t in range(4):
         even = r.dkvbuf[4 * t].astype(F32) + r.dkvbuf[4 * t + 1].astype(F32)
@@ -1010,8 +1015,8 @@
     dgain_k = jnp.sum(dk * (k_pre * k_inv), axis=0, keepdims=True)
     r.dqkv[128:256, 0:512] = rms_back(k_pre, k_inv, dk * key_gain_row(gains)).astype(BF16)
     r.dqkv[128:256, 512:1024] = jnp.concatenate(dv_tiles, axis=1).astype(BF16)
-    r.big3[me] = r.dqkv[...]
-    dqkv_gather = line_gather_start(r.dqkv, lambda i: r.big3.at[i], r.sn, r.rn)
+    r.big3[me, 128:256, :] = r.dqkv[128:256, :]
+    dkv_gather = line_gather_start(r.dqkv.at[kv_part], lambda i: r.big3.at[i, kv_part], r.sn2, r.rn2)
     for j in range(1, 4):
         scatter.near_out(j)
 
@@ -1071,36 +1076,40 @@
         copy = remote(r.smsum, r.smplane.at[o], r.sp5.at[o], r.rp5.at[o], device)
         copy.start()
         small_copies.append(copy)
-    line_gather_finish(dqkv_gather, lambda i: r.big3.at[i], r.sn, r.rn)
-
-    def qkv_grad(t, _):
-        at = pl.ds(pl.multiple_of(512 * lax.rem(t, 2), 512), 512)
-        part = pl.ds(pl.multiple_of(128 * lax.div(t, 2), 128), 128)
-        tiles = mm_tn(r.nx[...].reshape(1024, 128), r.big3[:, part, at].reshape(1024, 512)).astype(BF16)
-        for i in range(4):
-            r.pieces_n[pl.ds(8 * t + 2 * i, 2)] = tiles[:, 128 * i : 128 * i + 128].reshape(2, 64, 128)
-        return 0
-
-    lax.fori_loop(0, 4, qkv_grad, 0)
-    p_copies_n = plane_sum_send(r.pieces_n, 2, r.pin_n, r.sp3, r.rp3)
+
+    def qkv_grad(part, pieces):
+        def one(t, _):
+            at = pl.ds(pl.multiple_of(512 * t, 512), 512)
+            tiles = mm_tn(r.nx[...].reshape(1024, 128), r.big3[:, part, at].reshape(1024, 512)).astype(BF16)
+            for i in range(4):
+                pieces[pl.ds(8 * t + 2 * i, 2)] = tiles[:, 128 * i : 128 * i + 128].reshape(2, 64, 128)
+            return 0
+
+        lax.fori_loop(0, 2, one, 0)
+
+    line_gather_finish(dq_gather, lambda i: r.big3.at[i, q_part], r.sn, r.rn)
+    qkv_grad(slice(0, 128), r.pieces_q)
+    p_copies_q = plane_sum_send(r.pieces_q, 1, r.pin_q, r.sp3, r.rp3)
     for j in range(1, 4):
         scatter.near_sum(j)
     scatter.far2()
-    for copy in shares_o:
-        copy.wait_recv()
+    line_gather_finish(dkv_gather, lambda i: r.big3.at[i, kv_part], r.sn2, r.rn2)
+    qkv_grad(slice(128, 256), r.pieces_n)
+    p_copies_n = plane_sum_send(r.pieces_n, 1, r.pin_n, r.sp6, r.rp6)
     scatter.near2()
-    shares_n = plane_sum_share(p_copies_n, r.pieces_n, 2, r.pin_n, r.res_n, r.sp4, r.rp4)
+    shares_q = plane_sum_share(p_copies_q, r.pieces_q, 1, r.pin_q, r.res_q, r.sp4, r.rp4)
+    shares_n = plane_sum_share(p_copies_n, r.pieces_n, 1, r.pin_n, r.res_n, r.sp7, r.rp7)
     for at, copy in enumerate(small_copies):
         copy.wait_recv()
         total = total + r.smplane[at + 1]
     r.gsmall[...] = total
     scatter.finish(r.gw)
-    for copy in shares_n:
+    for copy in shares_o + shares_q + shares_n:
         copy.wait_recv()
     scatter.drain()
     for copy in (
-        [pair_copy] + x_copies + d_copies + sm_copies
-        + small_copies + p_copies_o + p_copies_n + shares_o + shares_n
+        pair_copies + x_copies + d_copies + sm_copies
+        + small_copies + p_copies_o + p_copies_q + p_copies_n + shares_o + shares_q + shares_n
     ):
         copy.wait_send()
 
@@ -1125,11 +1134,14 @@
 
 
 def finish_kernel(
-    mixed, gtok, res_o_in, res_n_in, small_in, gw_in,
+    mixed, gtok, res_o_in, res_q_in, res_n_in, small_in, gw_in,
     mixed_out, loss, gtok_out, gnorm_in, gq, gk, gv, gq_gain, gk_gain, gout, gnorm_mid, grouter, ggate, gup, gdown,
-    res_o, res_n, small, gw, sems,
+    res_o, res_q, res_n, small, gw, sems,
 ):
-    pairs = ((small_in, small), (res_o_in, res_o), (res_n_in, res_n), (gw_in, gw), (mixed, mixed_out), (gtok, gtok_out))
+    pairs = (
+        (small_in, small), (res_o_in, res_o), (res_q_in, res_q), (res_n_in, res_n), (gw_in, gw),
+        (mixed, mixed_out), (gtok, gtok_out),
+    )
     copies = [pltpu.make_async_copy(src, dst, sems.at[i]) for i, (src, dst) in enumerate(pairs)]
     for copy in copies:
         copy.start()
@@ -1149,15 +1161,16 @@
     copies[1].wait()
     tiles(res_o, gout, 0, 8)
     copies[2].wait()
-    tiles(res_n, gq, 0, 8)
-    tiles(res_n, gk, 8, 4)
-    tiles(res_n, gv, 12, 4)
+    tiles(res_q, gq, 0, 8)
     copies[3].wait()
+    tiles(res_n, gk, 0, 4)
+    tiles(res_n, gv, 4, 4)
+    copies[4].wait()
     for e in range(4):
         ggate[:, e, :] = gw[e]
         gup[:, e, :] = gw[6 + e]
         gdown[:, e, :] = gw[4 + e + 4 * (e // 2)]
-    for copy in copies[4:]:
+    for copy in copies[5:]:
         copy.wait()
 
 
@@ -1171,14 +1184,15 @@
     return pl.pallas_call(
         finish_kernel,
         out_shape=tuple(jax.ShapeDtypeStruct(v, BF16 if i == 0 else F32) for i, v in enumerate(shapes)),
-        in_specs=[hbm] * 6,
+        in_specs=[hbm] * 7,
         out_specs=(vm,) * len(shapes),
         scratch_shapes=[
             pltpu.VMEM((16, 64, 128), BF16),
-            pltpu.VMEM((32, 64, 128), BF16),
+            pltpu.VMEM((16, 64, 128), BF16),
+            pltpu.VMEM((16, 64, 128), BF16),
             pltpu.VMEM((48, 128), F32),
             pltpu.VMEM((12, 64, 512), F32),
-            pltpu.SemaphoreType.DMA((6,)),
+            pltpu.SemaphoreType.DMA((7,)),
         ],
         compiler_params=pltpu.CompilerParams(vmem_limit_bytes=62 << 20),
         name="finish",

time: 293 us -> 284 us (0.969); the launches traced: 292 us -> 279 us
  Pallas kernels: 290 us -> 277 us
    pallas_call x1, Pallas kernels: 286 us -> 273 us  [layer(): pl.pallas_call(layer_kernel, out_shape=tuple((jax.ShapeDtypeStruct(shape,...]
where the time goes in v4:
time: 284 us; the launch traced here: 279 us
  Pallas kernels  277 us (98%)
    pallas_call x1, Pallas kernels, layer(): pl.pallas_call(layer_kernel, out_shape=tuple((jax.ShapeDtypeStruct(shape,...  273 us

profile of v4, /device:TPU:1, one launch (start us, length us, event | category | flops | bytes accessed | tf_op | source)
XLA Modules:
  0.0 278.9 jit_solution(12078782807170746557)
XLA Ops:
  0.7 1.0 fusion
  1.6 272.8 %layer.1 = (bf16[128,1024]{1,0:T(8,128)(2,1)}, f32[128,1024]{1,0:T(8,128)}, bf16[16,64,128]{2,1,0:T(8,128)(2,1)}, bf16[16,64,128]{2,1,0:T(8,128)(2,1)}, bf16[16,...) custom-call(bf16[128,1024]{1,0:T(8,128)(2,1)} %refs_0_.1, ...), custom_call_target="tpu_custom_call" | custom-call | flops 32000000000 | bytes 62914560 | tf_op jit(solution)/shard_map/layer/pallas_call | solution.py:1121
  274.4 4.0 %finish.1 = (bf16[128,1024]{1,0:T(8,128)(2,1)}, f32[1,1]{1,0:T(1,128)}, f32[128,1024]{1,0:T(8,128)}, f32[1,128]{1,0:T(1,128)}, f32[128,1024]{1,0:T(8,128)}, /*in...) custom-call(bf16[128,1024]{1,0:T(8,128)(2,1)} %get-tuple-element.37., ...), custom_call_target="tpu_custom_call" | custom-call | tf_op jit(solution)/shard_map/finish/pallas_call | solution.py:1184
  (2 shorter events, 0.0 us)

commit v5 on v4

--- a/solution.py
+++ b/solution.py
@@ -266,44 +266,55 @@
                 view = view.at[pl.ds(2 * i, 2)] if half == 0 else view.at[i]
                 self.go(8 * j + 2 * half + i, view, self.far_in.at[half, i, j], self.device(half, lax.rem(me + o, 4)))
 
-    def near_out(self, j):
+    def far_load(self, j, slot):
         loads = []
         for half in range(2):
             for i in range(2):
                 self.copies[8 * j + 2 * half + i].wait_recv()
-                spot = self.stage[0].at[i, pl.ds(0, 2)] if half == 0 else self.stage[1].at[i, 0]
-                load = pltpu.make_async_copy(self.far_in.at[half, i, j], spot, self.load.at[2 * half + i])
+                spot = self.stage[0].at[i, pl.ds(2 * slot, 2)] if half == 0 else self.stage[1].at[i, slot]
+                load = pltpu.make_async_copy(self.far_in.at[half, i, j], spot, self.load.at[4 * slot + 2 * half + i])
                 load.start()
                 loads.append((load, spot))
-        for half in range(2):
-            me = self.place(half)
-            for i, o in enumerate((1, 3)):
-                load, spot = loads[2 * half + i]
-                load.wait()
-                to = lax.rem(me + o, 4)
-                whole = self.block(half, j, to)
-                part = whole.at[pl.ds(2 * i, 2)] if half == 0 else whole.at[i]
-                part[...] = (part[...].astype(F32) + spot[...].astype(F32)).astype(BF16)
-                self.go(8 * j + 4 + 2 * half + i, whole, self.near_in[half].at[i, j], self.device(half, to))
-
-    def near_load(self, j):
-        self.loads = []
-        for half in range(2):
-            for i in range(2):
-                self.copies[8 * j + 4 + 2 * half + i].wait_recv()
-                load = pltpu.make_async_copy(
-                    self.near_in[half].at[i, j], self.stage[half].at[i], self.load.at[2 * half + i]
-                )
-                load.start()
-                self.loads.append(load)
-
-    def near_sum(self, j):
-        self.near_load(j)
-        for half in range(2):
-            own, stage = self.block(half, j, self.place(half)), self.stage[half]
-            self.loads[2 * half].wait()
-            self.loads[2 * half + 1].wait()
-            own[...] = (own[...].astype(F32) + stage[0].astype(F32) + stage[1].astype(F32)).astype(BF16)
+        return loads
+
+    def near_out(self, *steps):
+        loads = self.far_load(steps[0], 0)
+        for n, j in enumerate(steps):
+            now = loads
+            if n + 1 < len(steps):
+                loads = self.far_load(steps[n + 1], (n + 1) % 2)
+            for half in range(2):
+                me = self.place(half)
+                for i, o in enumerate((1, 3)):
+                    load, spot = now[2 * half + i]
+                    load.wait()
+                    to = lax.rem(me + o, 4)
+                    whole = self.block(half, j, to)
+                    part = whole.at[pl.ds(2 * i, 2)] if half == 0 else whole.at[i]
+                    part[...] = part[...] + spot[...]
+                    self.go(8 * j + 4 + 2 * half + i, whole, self.near_in[half].at[i, j], self.device(half, to))
+
+    def near_load(self, j, half):
+        loads = []
+        for i in range(2):
+            self.copies[8 * j + 4 + 2 * half + i].wait_recv()
+            load = pltpu.make_async_copy(
+                self.near_in[half].at[i, j], self.stage[half].at[i], self.load.at[2 * half + i]
+            )
+            load.start()
+            loads.append(load)
+        return loads
+
+    def near_sum(self, *steps):
+        loads = [self.near_load(steps[0], half) for half in range(2)]
+        for n, j in enumerate(steps):
+            for half in range(2):
+                own, stage = self.block(half, j, self.place(half)), self.stage[half]
+                for load in loads[half]:
+                    load.wait()
+                own[...] = own[...] + (stage[0] + stage[1])
+                if n + 1 < len(steps):
+                    loads[half] = self.near_load(steps[n + 1], half)
 
     def place2(self, half):
         return self.y if half == 0 else self.z
@@ -327,7 +338,7 @@
 
                 def add(m, _):
                     part = self.due(half, 6 * half + m, to).at[pl.ds(32 * i, 32)]
-                    part[...] = (part[...].astype(F32) + self.far2_in[half, i, m].astype(F32)).astype(BF16)
+                    part[...] = part[...] + self.far2_in[half, i, m]
                     return 0
 
                 lax.fori_loop(0, 6, add, 0)
@@ -501,7 +512,7 @@
     ("pin_n", (16, 1, 64, 128), BF16),
 )
 SEMAPHORES = (
-    ("own_sem", 6), ("keep_sem", 2), ("teacher_sem", 1), ("load_sem", 4),
+    ("own_sem", 6), ("keep_sem", 2), ("teacher_sem", 1), ("load_sem", 8),
     ("ssm", 8), ("rsm", 8), ("skvw", 8), ("rkvw", 8), ("sqw", 8), ("rqw", 8), ("swo", 8), ("rwo", 8), ("sv", 16), ("rv", 16),
     ("sew", 56), ("rew", 56), ("snx", 8), ("rnx", 8), ("sax", 8), ("rax", 8),
     ("skv", 16), ("rkv", 16), ("sq", 8), ("rq", 8), ("so", 8), ("ro", 8), ("sx", 8), ("rx", 8), ("sm", 8), ("rm", 8),
@@ -908,8 +919,7 @@
         d_copies.append(copy)
     r.rows[me] = r.low[...]
     branch_gather = line_gather_start(r.low, lambda i: r.rows.at[i], r.sb, r.rb)
-    scatter.near_out(4)
-    scatter.near_out(5)
+    scatter.near_out(4, 5)
     for copy in spread_copies:
         copy.wait()
     for copy in d_copies:
@@ -1017,8 +1027,7 @@
     r.dqkv[128:256, 512:1024] = jnp.concatenate(dv_tiles, axis=1).astype(BF16)
     r.big3[me, 128:256, :] = r.dqkv[128:256, :]
     dkv_gather = line_gather_start(r.dqkv.at[kv_part], lambda i: r.big3.at[i, kv_part], r.sn2, r.rn2)
-    for j in range(1, 4):
-        scatter.near_out(j)
+    scatter.near_out(1, 2, 3)
 
     def out_grad(t, _):
         at = pl.ds(pl.multiple_of(512 * t, 512), 512)
@@ -1061,8 +1070,7 @@
         copy = remote(r.smsend.at[to], r.sminbox.at[o], r.sms.at[o], r.rms.at[o], (to, c, d))
         copy.start()
         sm_copies.append(copy)
-    for j in (4, 5, 0):
-        scatter.near_sum(j)
+    scatter.near_sum(4, 5, 0)
     shares_o = plane_sum_share(p_copies_o, r.pieces_o, 1, r.pin_o, r.res_o, r.sp2, r.rp2)
 
     total = r.smsend[me]
@@ -1090,8 +1098,7 @@
     line_gather_finish(dq_gather, lambda i: r.big3.at[i, q_part], r.sn, r.rn)
     qkv_grad(slice(0, 128), r.pieces_q)
     p_copies_q = plane_sum_send(r.pieces_q, 1, r.pin_q, r.sp3, r.rp3)
-    for j in range(1, 4):
-        scatter.near_sum(j)
+    scatter.near_sum(1, 2, 3)
     scatter.far2()
     line_gather_finish(dkv_gather, lambda i: r.big3.at[i, kv_part], r.sn2, r.rn2)
     qkv_grad(slice(128, 256), r.pieces_n)

time: 284 us -> 279 us (0.982); the launches traced: 279 us -> 279 us
  no operation moved by 1% of the time
where the time goes in v5:
time: 279 us
  Pallas kernels  277 us (99%)
    pallas_call x1, Pallas kernels, layer(): pl.pallas_call(layer_kernel, out_shape=tuple((jax.ShapeDtypeStruct(shape,...  273 us

profile of v5, /device:TPU:1, one launch (start us, length us, event | category | flops | bytes accessed | tf_op | source)
XLA Modules:
  0.0 278.8 jit_solution(10802170068294697155)
XLA Ops:
  0.7 1.0 fusion
  1.6 272.9 %layer.1 = (bf16[128,1024]{1,0:T(8,128)(2,1)}, f32[128,1024]{1,0:T(8,128)}, bf16[16,64,128]{2,1,0:T(8,128)(2,1)}, bf16[16,64,128]{2,1,0:T(8,128)(2,1)}, bf16[16,...) custom-call(bf16[128,1024]{1,0:T(8,128)(2,1)} %refs_0_.1, ...), custom_call_target="tpu_custom_call" | custom-call | flops 32000000000 | bytes 62914560 | tf_op jit(solution)/shard_map/layer/pallas_call | solution.py:1128
  274.6 4.0 %finish.1 = (bf16[128,1024]{1,0:T(8,128)(2,1)}, f32[1,1]{1,0:T(1,128)}, f32[128,1024]{1,0:T(8,128)}, f32[1,128]{1,0:T(1,128)}, f32[128,1024]{1,0:T(8,128)}, /*in...) custom-call(bf16[128,1024]{1,0:T(8,128)(2,1)} %get-tuple-element.37., ...), custom_call_target="tpu_custom_call" | custom-call | tf_op jit(solution)/shard_map/finish/pallas_call | solution.py:1191
  (2 shorter events, 0.0 us)

commit v6 on v5

--- a/solution.py
+++ b/solution.py
@@ -456,6 +456,9 @@
     ("rows", (8, 128, 1024), BF16),
     ("wo_all", (8, 128, 1024), BF16),
     ("wg", (12, 2, 4, 2, 64, 512), BF16),
+    ("shard_gate", (64, 4, 512), BF16),
+    ("shard_up", (64, 4, 512), BF16),
+    ("shard_down", (64, 4, 512), BF16),
     ("gbuf", (4, 512, 512), BF16),
     ("ubuf", (4, 512, 512), BF16),
     ("mine", (4, 128, 1024), BF16),
@@ -512,7 +515,7 @@
     ("pin_n", (16, 1, 64, 128), BF16),
 )
 SEMAPHORES = (
-    ("own_sem", 6), ("keep_sem", 2), ("teacher_sem", 1), ("load_sem", 8),
+    ("own_sem", 8), ("keep_sem", 2), ("teacher_sem", 1), ("load_sem", 8),
     ("ssm", 8), ("rsm", 8), ("skvw", 8), ("rkvw", 8), ("sqw", 8), ("rqw", 8), ("swo", 8), ("rwo", 8), ("sv", 16), ("rv", 16),
     ("sew", 56), ("rew", 56), ("snx", 8), ("rnx", 8), ("sax", 8), ("rax", 8),
     ("skv", 16), ("rkv", 16), ("sq", 8), ("rq", 8), ("so", 8), ("ro", 8), ("sx", 8), ("rx", 8), ("sm", 8), ("rm", 8),
@@ -540,6 +543,9 @@
         pltpu.make_async_copy(r.wk, wall.at[me, pl.ds(128, 128), pl.ds(0, 512)], r.own_sem.at[1]),
         pltpu.make_async_copy(r.wv, wall.at[me, pl.ds(128, 128), pl.ds(512, 512)], r.own_sem.at[2]),
         pltpu.make_async_copy(r.wo, r.wo_all.at[me], r.own_sem.at[3]),
+        pltpu.make_async_copy(r.expert_gate, r.shard_gate, r.own_sem.at[4]),
+        pltpu.make_async_copy(r.expert_up, r.shard_up, r.own_sem.at[5]),
+        pltpu.make_async_copy(r.expert_down, r.shard_down, r.own_sem.at[6]),
     ]
     for copy in own:
         copy.start()
@@ -561,7 +567,9 @@
     kv_part, q_part = pl.ds(128, 128), pl.ds(0, 128)
     kv_gather = line_gather_start(wall.at[me, kv_part], lambda i: wall.at[i, kv_part], r.skvw, r.rkvw)
     q_gather = line_gather_start(wall.at[me, q_part], lambda i: wall.at[i, q_part], r.sqw, r.rqw)
-    for ref, first in ((r.expert_gate, (0, 1, 2, 3)), (r.expert_up, (6, 7, 8, 9)), (r.expert_down, (4, 5, 10, 11))):
+    for copy in own[4:]:
+        copy.wait()
+    for ref, first in ((r.shard_gate, (0, 1, 2, 3)), (r.shard_up, (6, 7, 8, 9)), (r.shard_down, (4, 5, 10, 11))):
         whole = ref[...].astype(F32)
         for e, m in enumerate(first):
             r.wg[m, lax.div(z, 2), y, lax.rem(z, 2)] = whole[:, e, :].astype(BF16)
@@ -1124,7 +1132,7 @@
 def layer(*args):
     vm = pl.BlockSpec(memory_space=pltpu.VMEM)
     hbm = pl.BlockSpec(memory_space=pl.ANY)
-    in_hbm = ("wq", "wk", "wv", "wo", "teacher")
+    in_hbm = ("wq", "wk", "wv", "wo", "expert_gate", "expert_up", "expert_down", "teacher")
     return pl.pallas_call(
         layer_kernel,
         out_shape=tuple(jax.ShapeDtypeStruct(shape, dtype) for _, shape, dtype in OUTPUTS + SPILLS),

time: 279 us -> 279 us (level)
  no operation moved by 1% of the time
where the time goes in v6:
time: 279 us; the launch traced here: 278 us
  Pallas kernels  277 us (99%)
    pallas_call x1, Pallas kernels, layer(): pl.pallas_call(layer_kernel, out_shape=tuple((jax.ShapeDtypeStruct(shape,...  273 us

profile of v6, /device:TPU:1, one launch (start us, length us, event | category | flops | bytes accessed | tf_op | source)
XLA Modules:
  0.0 278.4 jit_solution(12207711807204455958)
XLA Ops:
  0.7 1.0 fusion
  1.6 272.5 %layer.1 = (bf16[128,1024]{1,0:T(8,128)(2,1)}, f32[128,1024]{1,0:T(8,128)}, bf16[16,64,128]{2,1,0:T(8,128)(2,1)}, bf16[16,64,128]{2,1,0:T(8,128)(2,1)}, bf16[16,...) custom-call(bf16[128,1024]{1,0:T(8,128)(2,1)} %refs_0_.1, ...), custom_call_target="tpu_custom_call" | custom-call | flops 32000000000 | bytes 62914560 | tf_op jit(solution)/shard_map/layer/pallas_call | solution.py:1136
  274.2 4.0 %finish.1 = (bf16[128,1024]{1,0:T(8,128)(2,1)}, f32[1,1]{1,0:T(1,128)}, f32[128,1024]{1,0:T(8,128)}, f32[1,128]{1,0:T(1,128)}, f32[128,1024]{1,0:T(8,128)}, /*in...) custom-call(bf16[128,1024]{1,0:T(8,128)(2,1)} %get-tuple-element.37., ...), custom_call_target="tpu_custom_call" | custom-call | tf_op jit(solution)/shard_map/finish/pallas_call | solution.py:1199
  (2 shorter events, 0.0 us)
